TPU v7x, 128 devices: a whole 4x4x4 slice. The times are simulated.
128 devices in a mesh: inst: 32 (over z, y, x_hi), span: 2 (over core), rad: 2 (over x_lo).
Axes of the slice: x: 4 (x_hi: 2, x_lo: 2; x = x_hi * 2 + x_lo), y: 4, z: 4, core: 2. Of those that a mesh axis runs over, the one named last changes fastest.
Arguments:
- adjoint_start: float32 [64, 5, 32, 1024], P('inst', None, 'rad', 'span'), may hold values from -6 to 6
- jac_rad: bfloat16 [64, 5, 5, 32, 1024], P('inst', None, None, 'rad', 'span'), may hold values from -2.5 to 2.5
- jac_circ: bfloat16 [64, 5, 5, 32, 1024], P('inst', None, None, 'rad', 'span'), may hold values from -2.5 to 2.5
- dissip: float32 [32, 1024], P('rad', 'span'), may hold values from 0.5 to 4
- pseudo_step: float32 [32, 1024], P('rad', 'span'), may hold values from 0.1 to 0.4
- source: float32 [64, 5, 32, 1024], P('inst', None, 'rad', 'span'), may hold values from -6 to 6
- node_cell: int32 [4096], P(('span', 'rad')), may hold values from 0 to 8191
- node_owner: int32 [4096, 1], P(('span', 'rad')), may hold values from 0 to 1; in each aligned block of 1024 rows (0 to 1023, 1024 to 2047, ...) at most 1024 rows name the same one
- node_local: int32 [4096], P(('span', 'rad')), may hold values from 0 to 31
- shape_deriv: bfloat16 [64, 5, 3, 4096], P('inst', None, None, ('span', 'rad')), may hold values from -0.119628906 to 0.119628906
Outputs:
- adjoint: float32 [64, 5, 32, 1024], P('inst', None, 'rad', 'span')
- sensitivity: float32 [3, 64], P(None, 'span')
Inputs may be any that keep to these rules, and one draw needn't show every extreme that they name: `node_owner`: among the node entries of one span and rad index, no owner is named more than 1024 times.
All inputs are finite; a program needn't handle non-finite values.
Results may differ from a plain program's by a relative error of at most 0.0003.
Values sent between devices are 32-bit elements; how exact they have to be, the bound alone decides.
No kernel may reach another device: no remote copies, remote signals or barrier semaphores. Data moves between devices by JAX's collectives and lax.ppermute only.
A program may use at most 64 MiB of HBM per device.

v0:
```python
import jax
import jax.numpy as jnp
from jax import lax
from jax.sharding import PartitionSpec as P

ITERS = 2
KD = 3
VAR_DEV = 32


eps_fourth = 0.0625


def with_halo(block, sides, width, periodic):
    for axis, dim in sides:
        count = lax.axis_size(axis)
        forward = [(i, i + 1) for i in range(count - 1)]
        if periodic:
            forward.append((count - 1, 0))
        backward = [(target, source) for source, target in forward]
        low = lax.ppermute(
            lax.slice_in_dim(block, block.shape[dim] - width, None, axis=dim), axis, forward
        )
        high = lax.ppermute(lax.slice_in_dim(block, 0, width, axis=dim), axis, backward)
        block = jnp.concatenate([low, block, high], axis=dim)
    return block


def spectral_table(count):
    index = jnp.arange(count, dtype=jnp.int32)
    diff = index[:, None] - index[None, :]
    safe = jnp.where(diff == 0, 1, diff).astype(jnp.float32)
    tangent = jnp.tan(jnp.pi * safe / count)
    parity = jnp.where(diff % 2 == 0, 1.0, -1.0).astype(jnp.float32)
    return jnp.where(diff == 0, 0.0, 0.5 * parity / tangent)


def apply_transposed(jac, vec):
    total = jac[:, 0].astype(jnp.float32) * vec[:, 0:1]
    for field in range(1, 5):
        total = total + jac[:, field].astype(jnp.float32) * vec[:, field : field + 1]
    return total


def body(
    adjoint_start,
    jac_rad,
    jac_circ,
    dissip,
    pseudo_step,
    source,
    node_cell,
    node_owner,
    node_local,
    shape_deriv,
):
    inst_dev = adjoint_start.shape[0]
    count = adjoint_start.shape[2]
    width = adjoint_start.shape[3]
    table = spectral_table(inst_dev * lax.axis_size("inst"))
    first = lax.axis_index("inst") * inst_dev
    my_cols = lax.dynamic_slice_in_dim(table, first, inst_dev, 1)
    psi = adjoint_start
    for step in range(ITERS):
        circle = with_halo(psi, (("span", 3),), 2, True)
        radial = with_halo(psi, (("rad", 2),), 2, False)
        time = jnp.einsum(
            "st,sfrc->tfrc",
            my_cols,
            lax.all_gather(psi, "inst", axis=0, tiled=True),
            precision=lax.Precision.HIGHEST,
        )
        conv = apply_transposed(
            jac_rad, 0.5 * (radial[:, :, 1 : count + 1] - radial[:, :, 3 : count + 3])
        )
        conv = conv + apply_transposed(
            jac_circ, 0.5 * (circle[..., 1 : width + 1] - circle[..., 3 : width + 3])
        )
        fourth = (
            radial[:, :, 4:]
            - 4.0 * radial[:, :, 3 : count + 3]
            + 6.0 * psi
            - 4.0 * radial[:, :, 1 : count + 1]
            + radial[:, :, :count]
        )
        fourth = (
            fourth
            + circle[..., 4:]
            - 4.0 * circle[..., 3 : width + 3]
            + 6.0 * psi
            - 4.0 * circle[..., 1 : width + 1]
            + circle[..., :width]
        )
        psi = psi - pseudo_step * (conv + eps_fourth * dissip * fourth + time - source)
    flat = psi.reshape(inst_dev, psi.shape[1], count * width)
    values = flat[:, :, node_cell]
    rows = jnp.einsum(
        "tfn,tfkn->kn", values, shape_deriv.astype(jnp.float32), precision=lax.Precision.HIGHEST
    )
    owner = node_owner[:, 0]
    n_span = lax.axis_size("span")
    nodes = node_cell.shape[0]
    capacity = min(nodes, 2 * nodes // n_span)
    onehot = (owner[:, None] == jnp.arange(n_span, dtype=jnp.int32)[None, :]).astype(jnp.int32)
    before = jnp.cumsum(onehot, axis=0) - onehot
    position = jnp.sum(before * onehot, axis=1)
    slot = owner * capacity + position
    packed = (
        jnp.zeros((KD, n_span * capacity), jnp.float32)
        .at[:, slot]
        .set(rows)
        .reshape(KD, n_span, capacity)
    )
    labels = (
        jnp.full((n_span * capacity,), VAR_DEV, jnp.int32)
        .at[slot]
        .set(node_local)
        .reshape(1, n_span, capacity)
    )
    got_rows, got_labels = (
        lax.all_to_all(packed, "span", split_axis=1, concat_axis=1, tiled=True),
        lax.all_to_all(labels, "span", split_axis=1, concat_axis=1, tiled=True),
    )
    match = (
        got_labels.reshape(-1)[:, None] == jnp.arange(VAR_DEV, dtype=jnp.int32)[None, :]
    ).astype(jnp.float32)
    partial_sens = jnp.dot(got_rows.reshape(KD, -1), match, precision=lax.Precision.HIGHEST)
    sensitivity = lax.psum(partial_sens, ("inst", "rad"))
    return (psi, sensitivity)


def solution(mesh):
    in_specs = (
        P("inst", None, "rad", "span"),
        P("inst", None, None, "rad", "span"),
        P("inst", None, None, "rad", "span"),
        P("rad", "span"),
        P("rad", "span"),
        P("inst", None, "rad", "span"),
        P(("span", "rad")),
        P(("span", "rad"), None),
        P(("span", "rad")),
        P("inst", None, None, ("span", "rad")),
    )
    out_specs = (P("inst", None, "rad", "span"), P(None, "span"))
    return jax.shard_map(body, mesh=mesh, in_specs=in_specs, out_specs=out_specs, check_vma=False)
```

profile of v0, /device:TPU:0, one launch (start us, length us, event | category | flops | bytes accessed | tf_op | source)
XLA Modules:
  0.0 498.9 jit_solution(18147436960971187667)
XLA Ops:
  7.2 0.0 all-gather.3.cloned.1.call-start
  7.2 0.7 all-gather.3.cloned.1.call-update
  7.9 0.0 all-gather.5.cloned.1.call-start
  7.9 1.2 copy.82
  9.2 3.5 collective-permute-start
  12.7 0.2 fusion.83
  12.8 0.1 collective-permute-start.3
  12.9 0.5 collective-permute-start.2
  13.4 1.3 collective-permute-start.1
  14.7 0.6 broadcast_add_fusion
  15.3 0.6 negate_select_fusion
  16.0 1.4 broadcast_multiply_fusion
  17.3 1.7 fusion.78
  19.0 0.0 copy-start
  19.1 0.0 copy-start.9
  19.1 0.0 copy-start.10
  19.1 0.0 collective-permute-done
  19.1 1.6 constant_dynamic-update-slice_fusion.3
  20.8 0.0 collective-permute-done.3
  20.9 0.0 collective-permute-done.1
  20.9 0.8 constant_dynamic-update-slice_fusion.2
  21.7 0.0 collective-permute-done.2
  21.7 0.8 subtract_multiply_fusion.2
  22.5 0.7 slice_bitcast_fusion.14
  23.2 0.3 subtract_multiply_fusion.3
  23.5 0.7 slice_bitcast_fusion.19
  24.2 106.5 %all-gather.3.cloned.1.call-done = f32[64,5,16,512]{3,2,1,0:T(8,128)} async-done(((f32[2,5,16,512]{3,2,1,0:T(8,128)}), f32[64,5,16,512]{3,2,1,0:T(8,128)}) %all-gather.3.cloned.1.call-update) | async-done | bytes 10485776 | tf_op jit(solution)/shard_map/all_gather | solution.py:70
  130.7 18.8 %multiply_subtract_fusion.1 = f32[2,5,16,512]{3,0,2,1:T(2,128)S(1)} fusion(f32[2,5,16,512]{3,0,2,1:T(2,128)S(1)} %copy.82, f32[2,5,16,2]{3,0,2,1:T(2,128)S(1)} %collective-permute-done.2, f32[2,5,16,514]{3,0,2,1:T(2,128)S(1)} %constant_dynamic-update-slice_fusion.4, f32[2,5,18,512]{3,0,2,1:T(2,128)S(1)} %get-tuple-element.47, ...), kind=kOutput, calls=%fused_computation.95 | convolution fusion | flops 67093632 | bytes 15880196 | tf_op jit(solution)/shard_map/st,sfrc->tfrc/dot_general | solution.py:67
  149.6 0.8 copy.83
  150.4 0.0 all-gather.5.cloned.1.call-update
  150.5 0.6 reduce-window.6
  151.1 0.2 slice_reduce_fusion
  151.3 0.2 reduce-window.9
  151.4 0.1 add_bitcast_fusion
  151.6 5.0 %scatter_custom_fusion.1 = s32[2048]{0:T(1024)} fusion(s32[1024]{0:T(1024)S(1)} %bitcast.166, s32[1024]{0:T(1024)} %param.18, s32[]{:T(128)} %constant.59.clone.1), kind=kCustom, calls=%fused_computation.153 | custom fusion | bytes 8704 | tf_op jit(solution)/shard_map/scatter | solution.py:117
  156.6 3.8 all-to-all-start.1
  160.4 0.2 fusion.81
  160.6 0.7 collective-permute-start.6
  161.3 0.1 collective-permute-start.7
  161.5 2.5 collective-permute-start.4
  163.9 1.3 collective-permute-start.5
  165.2 0.6 fusion.56
  165.8 2.5 copy.91
  168.4 0.0 collective-permute-done.6
  168.4 0.0 collective-permute-done.7
  168.4 0.0 collective-permute-done.4
  168.4 0.6 copy-done.6
  169.1 0.9 collective-permute-done.5
  169.9 1.9 subtract_multiply_fusion.1
  171.9 0.0 copy-done.7
  171.9 0.7 slice_bitcast_fusion.9
  172.6 0.7 slice_bitcast_fusion.4
  173.3 92.3 %all-gather.5.cloned.1.call-done = f32[64,5,16,512]{3,2,1,0:T(8,128)} async-done(((f32[2,5,16,512]{3,2,1,0:T(8,128)}), f32[64,5,16,512]{3,2,1,0:T(8,128)}) %all-gather.5.cloned.1.call-update) | async-done | bytes 10485776 | tf_op jit(solution)/shard_map/all_gather | solution.py:70
  265.6 19.4 %multiply_subtract_fusion = f32[2,5,16,512]{3,0,2,1:T(2,128)S(1)} fusion(f32[2,5,16,512]{3,0,2,1:T(2,128)S(1)} %multiply_subtract_fusion.1, f32[2,5,16,2]{3,0,2,1:T(2,128)S(1)} %collective-permute-done.6, f32[2,5,16,2]{3,0,2,1:T(2,128)} %copy-done.6, f32[2,5,2,512]{3,0,2,1:T(2,128)} %copy-done.7, f32[2,5,2,512]{3,0,2,1:T(2,128)} %collective-permute-done.5, ...), kind=kOutput, calls=%fused_computation.92 | convolution fusion | flops 67585152 | bytes 13997316 | tf_op jit(solution)/shard_map/st,sfrc->tfrc/dot_general | solution.py:67
  285.1 0.8 copy.88
  285.8 7.8 %copy.86 = f32[2,5,8192]{1,0,2:T(2,128)} copy(f32[2,5,8192]{2,0,1:T(2,128)S(1)} %bitcast.161) | data formatting | bytes 655360 | tf_op jit(solution)/shard_map/reshape | solution.py:95
  293.7 7.4 %gather_fusion = f32[1024,2,5]{2,1,0:T(2,128)S(1)} fusion(f32[2,5,8192]{1,0,2:T(2,128)} %copy.86, s32[1024]{0:T(1024)} %fusion.56), kind=kCustom, calls=%fused_computation | custom fusion | bytes 86016 | tf_op jit(solution)/shard_map/gather | solution.py:96
  301.1 5.8 %fusion.86 = f32[1024,1,3,1]{2,1,3,0:T(1,128)} fusion(f32[2,5,1024,1]{1,3,0,2:T(1,128)S(1)} %bitcast.169, bf16[2,5,3,1024]{1,2,0,3:T(4,128)(2,1)S(1)} %copy.91), kind=kOutput, calls=%fused_computation.178 | convolution fusion | flops 368640 | bytes 114688 | tf_op jit(solution)/shard_map/tfn,tfkn->kn/dot_general | solution.py:97
  306.9 3.7 scatter_custom_fusion
  310.6 0.3 copy.87
  311.0 0.0 all-to-all-done.1
  311.0 3.7 all_to_all.10
  314.7 1.3 fusion.4
  316.0 176.1 %psum.7 = f32[3,32]{1,0:T(4,128)} all-reduce(f32[3,32]{1,0:T(4,128)S(1)} %fusion.4), channel_id=1, replica_groups=mesh['inst'=32,'span'=2,'rad'=2] {'inst','rad'}, use_global_device_ids=true, to_apply=%region_5.6 | all-reduce | flops 96 | bytes 768 | tf_op jit(solution)/shard_map/psum | solution.py:128
  (29 shorter events, 0.2 us)
Async XLA Ops:
  7.2 123.6 %all-gather.3.cloned.1.call-start = ((), (), s32[]{:S(2)}) async-start(), calls=%async_computation.2 | async-start | bytes 10813440 | tf_op jit(solution)/shard_map/all_gather | solution.py:70
  7.9 257.8 %all-gather.5.cloned.1.call-start = ((), (), s32[]{:S(2)}) async-start(), calls=%async_computation.3 | async-start | bytes 10813440 | tf_op jit(solution)/shard_map/all_gather | solution.py:70
  9.2 9.9 %collective-permute-start = (f32[2,5,2,512]{3,0,2,1:T(2,128)S(1)}, f32[2,5,2,512]{3,0,2,1:T(2,128)S(1)}, u32[]{:S(2)}, u32[]{:S(2)}) collective-permute-start(f32[2,5,2,512]{3,0,2,1:T(2,128)S(1)} %get-tuple-element.45), channel_id=1, source_target_pairs={{0,1},{2,3},{4,5},{6,7},{8,9},{10,11},{12,13},{14,15},{16,17},{18,... | collective-permute-start | bytes 122888 | tf_op jit(solution)/shard_map/ppermute | solution.py:21
  12.8 8.0 %collective-permute-start.3 = (f32[2,5,16,2]{3,0,2,1:T(2,128)S(1)}, f32[2,5,16,2]{3,0,2,1:T(2,128)S(1)}, u32[]{:S(2)}, u32[]{:S(2)}) collective-permute-start(f32[2,5,16,2]{3,0,2,1:T(2,128)S(1)} %get-tuple-element.49), channel_id=1, source_target_pairs={{2,0},{0,2},{3,1},{1,3},{6,4},{4,6},{7,5},{5,7},{10,8},{8,10},{11,... | collective-permute-start | bytes 3848 | tf_op jit(solution)/shard_map/ppermute | solution.py:24
  12.9 8.7 %collective-permute-start.2 = (f32[2,5,16,2]{3,0,2,1:T(2,128)S(1)}, f32[2,5,16,2]{3,0,2,1:T(2,128)S(1)}, u32[]{:S(2)}, u32[]{:S(2)}) collective-permute-start(f32[2,5,16,2]{3,0,2,1:T(2,128)S(1)} %get-tuple-element.50), channel_id=1, source_target_pairs={{0,2},{2,0},{1,3},{3,1},{4,6},{6,4},{5,7},{7,5},{8,10},{10,8},{9,1... | collective-permute-start | bytes 3848 | tf_op jit(solution)/shard_map/ppermute | solution.py:21
  13.4 7.4 %collective-permute-start.1 = (f32[2,5,2,512]{3,0,2,1:T(2,128)S(1)}, f32[2,5,2,512]{3,0,2,1:T(2,128)}, u32[]{:S(2)}, u32[]{:S(2)}) collective-permute-start(f32[2,5,2,512]{3,0,2,1:T(2,128)S(1)} %get-tuple-element.44), channel_id=1, source_target_pairs={{1,0},{3,2},{5,4},{7,6},{9,8},{11,10},{13,12},{15,14},{17,16},{19,... | collective-permute-start | bytes 122888 | tf_op jit(solution)/shard_map/ppermute | solution.py:24
  19.0 130.5 %copy-start = (bf16[2,1,5,16,512]{4,3,2,1,0:T(8,128)(2,1)}, bf16[2,1,5,16,512]{4,3,2,1,0:T(8,128)(2,1)S(1)}, u32[]{:S(2)}) copy-start(bf16[2,1,5,16,512]{4,3,2,1,0:T(8,128)(2,1)S(1)} %get-tuple-element.12) | copy-start | bytes 491524
  19.0 130.5 %copy-start.1 = (bf16[2,1,5,16,512]{4,3,2,1,0:T(8,128)(2,1)}, bf16[2,1,5,16,512]{4,3,2,1,0:T(8,128)(2,1)S(1)}, u32[]{:S(2)}) copy-start(bf16[2,1,5,16,512]{4,3,2,1,0:T(8,128)(2,1)S(1)} %get-tuple-element.55) | copy-start | bytes 491524
  19.0 130.5 %copy-start.2 = (bf16[2,1,5,16,512]{4,3,2,1,0:T(8,128)(2,1)}, bf16[2,1,5,16,512]{4,3,2,1,0:T(8,128)(2,1)S(1)}, u32[]{:S(2)}) copy-start(bf16[2,1,5,16,512]{4,3,2,1,0:T(8,128)(2,1)S(1)} %get-tuple-element.56) | copy-start | bytes 491524
  19.0 130.5 %copy-start.3 = (bf16[2,1,5,16,512]{4,3,2,1,0:T(8,128)(2,1)}, bf16[2,1,5,16,512]{4,3,2,1,0:T(8,128)(2,1)S(1)}, u32[]{:S(2)}) copy-start(bf16[2,1,5,16,512]{4,3,2,1,0:T(8,128)(2,1)S(1)} %get-tuple-element.57) | copy-start | bytes 491524
  19.0 130.5 %copy-start.4 = (bf16[2,1,5,16,512]{4,3,2,1,0:T(8,128)(2,1)}, bf16[2,1,5,16,512]{4,3,2,1,0:T(8,128)(2,1)S(1)}, u32[]{:S(2)}) copy-start(bf16[2,1,5,16,512]{4,3,2,1,0:T(8,128)(2,1)S(1)} %get-tuple-element.58) | copy-start | bytes 491524
  19.1 130.5 %copy-start.5 = (bf16[2,1,5,16,512]{4,3,2,1,0:T(8,128)(2,1)}, bf16[2,1,5,16,512]{4,3,2,1,0:T(8,128)(2,1)S(1)}, u32[]{:S(2)}) copy-start(bf16[2,1,5,16,512]{4,3,2,1,0:T(8,128)(2,1)S(1)} %get-tuple-element.59) | copy-start | bytes 491524
  19.1 130.5 %copy-start.9 = (pred[64,64]{0,1:T(8,128)(4,1)}, pred[64,64]{0,1:T(8,128)(4,1)S(1)}, u32[]{:S(2)}) copy-start(pred[64,64]{0,1:T(8,128)(4,1)S(1)} %get-tuple-element.53) | copy-start | bytes 12292
  19.1 130.5 %copy-start.10 = (pred[64,64]{0,1:T(8,128)(4,1)}, pred[64,64]{0,1:T(8,128)(4,1)S(1)}, u32[]{:S(2)}) copy-start(pred[64,64]{0,1:T(8,128)(4,1)S(1)} %get-tuple-element.54) | copy-start | bytes 12292
  130.7 19.7 %copy-start.8 = (s32[1024,1]{0,1:T(1,128)S(1)}, s32[1024,1]{0,1:T(1,128)}, u32[]{:S(2)}) copy-start(s32[1024,1]{0,1:T(1,128)} %param.17) | copy-start | bytes 12292
  130.7 34.5 %copy-start.12 = (s32[1024]{0:T(1024)S(1)}, s32[1024]{0:T(1024)}, u32[]{:S(2)}) copy-start(s32[1024]{0:T(1024)} %param.16) | copy-start | bytes 12292
  151.6 9.8 %copy-start.11 = (s32[1024,1]{0,1:T(1,128)}, s32[1024,1]{0,1:T(1,128)S(1)}, u32[]{:S(2)}) copy-start(s32[1024,1]{0,1:T(1,128)S(1)} %compare_select_fusion) | copy-start | bytes 12292
  156.6 154.3 %all-to-all-start.1 = ((s32[1,2,1024]{2,0,1:T(1,128)}), s32[1,2,1024]{2,0,1:T(1,128)}, u32[]{:S(2)}, u32[]{:S(2)}) async-start(s32[1,2,1024]{2,0,1:T(1,128)} %bitcast.56), calls=%async_computation.1 | async-start | bytes 16384 | tf_op jit(solution)/shard_map/all_to_all | solution.py:122
  160.6 7.8 %collective-permute-start.6 = (f32[2,5,16,2]{3,0,2,1:T(2,128)S(1)}, f32[2,5,16,2]{3,0,2,1:T(2,128)S(1)}, u32[]{:S(2)}, u32[]{:S(2)}) collective-permute-start(f32[2,5,16,2]{3,0,2,1:T(2,128)S(1)} %get-tuple-element.33), channel_id=1, source_target_pairs={{0,2},{2,0},{1,3},{3,1},{4,6},{6,4},{5,7},{7,5},{8,10},{10,8},{9,1... | collective-permute-start | bytes 3848 | tf_op jit(solution)/shard_map/ppermute | solution.py:21
  161.3 7.1 %collective-permute-start.7 = (f32[2,5,16,2]{3,0,2,1:T(2,128)S(1)}, f32[2,5,16,2]{3,0,2,1:T(2,128)S(1)}, u32[]{:S(2)}, u32[]{:S(2)}) collective-permute-start(f32[2,5,16,2]{3,0,2,1:T(2,128)S(1)} %get-tuple-element.32), channel_id=1, source_target_pairs={{2,0},{0,2},{3,1},{1,3},{6,4},{4,6},{7,5},{5,7},{10,8},{8,10},{11,... | collective-permute-start | bytes 3848 | tf_op jit(solution)/shard_map/ppermute | solution.py:24
  161.5 7.0 %collective-permute-start.4 = (f32[2,5,2,512]{3,0,2,1:T(2,128)S(1)}, f32[2,5,2,512]{3,0,2,1:T(2,128)S(1)}, u32[]{:S(2)}, u32[]{:S(2)}) collective-permute-start(f32[2,5,2,512]{3,0,2,1:T(2,128)S(1)} %get-tuple-element.31), channel_id=1, source_target_pairs={{0,1},{2,3},{4,5},{6,7},{8,9},{10,11},{12,13},{14,15},{16,17},{18,... | collective-permute-start | bytes 122888 | tf_op jit(solution)/shard_map/ppermute | solution.py:21
  163.9 6.0 %collective-permute-start.5 = (f32[2,5,2,512]{3,0,2,1:T(2,128)S(1)}, f32[2,5,2,512]{3,0,2,1:T(2,128)}, u32[]{:S(2)}, u32[]{:S(2)}) collective-permute-start(f32[2,5,2,512]{3,0,2,1:T(2,128)S(1)} %get-tuple-element.30), channel_id=1, source_target_pairs={{1,0},{3,2},{5,4},{7,6},{9,8},{11,10},{13,12},{15,14},{17,16},{19,... | collective-permute-start | bytes 122888 | tf_op jit(solution)/shard_map/ppermute | solution.py:24
  168.4 0.6 copy-start.6
  169.1 2.8 copy-start.7
Sparse Core Ops, SparseCore 0:
  11.1 119.5 all-gather.2
  150.6 115.0 all-gather.4
where the time goes:
time: 500 us; the launch traced here: 499 us
  waiting for transfers between devices  200 us (40%)
  blocking collectives  180 us (36%)
  matrix products  45.3 us (9%)
  local copies, waits for them, and re-layouts  37.9 us (8%)
  between operations  14.4 us (3%)
  starting transfers between devices  13.8 us (3%)
  other arithmetic  7.21 us (1%)
    all_gather x2, waiting for transfers between devices, body(): lax.all_gather(psi, 'inst', axis=0, tiled=True)  199 us
    psum x1, blocking collectives, body(): sensitivity = lax.psum(partial_sens, ('inst', 'rad'))  176 us
    dot_general x2, matrix products, body(): jnp.einsum('st,sfrc->tfrc', my_cols, lax.all_gather(psi, 'inst', axis=0,...  38.2 us
  transfers between devices with their start and end apart: 11, of which 3 were waited for; matrix products, arithmetic and copies ran while one was open for 14% of the time, Pallas kernels for 0%

commit v1 on v0

v1 whole, which is shorter than its diff:
```python
import jax
import jax.numpy as jnp
import numpy as np
from jax import lax
from jax.experimental import pallas as pl
from jax.experimental.pallas import tpu as pltpu
from jax.sharding import PartitionSpec as P

NT = 64
TD = 2
NF = 5
CR = 16
CT = 512
LT = 4
HB = 2
ROWS = 40
GRP = 8 * ROWS
NODES = 1024
VAR_DEV = 32
EPS4 = 0.0625
F32 = jnp.float32
BF = jnp.bfloat16
SWAP = [(0, 1), (1, 0)]
ALL = ("inst", "span", "rad")


def spectral_blocks():
    index = np.arange(NT)
    diff = index[:, None] - index[None, :]
    safe = np.where(diff == 0, 1, diff)
    table = np.where(diff == 0, 0.0, 0.5 * np.where(diff % 2 == 0, 1.0, -1.0) / np.tan(np.pi * safe / NT))
    order = np.concatenate([index[0::2], index[1::2]])
    apply = table.T[order][:, order].astype(np.float32)
    high = apply.astype(BF)
    low = (apply - high.astype(np.float32)).astype(BF)
    return np.concatenate([high, high, low], axis=1)


def row_of(t, what, f, h):
    return ((t * 2 + what) * NF + f) * HB + h


def lanes(q):
    return slice(128 * q, 128 * q + 128)


def local_operator(cell, edge_ref, halo_ref, pad_ref, jr_ref, jc_ref, dis, has_low, has_high, t, q):
    lane = lax.broadcasted_iota(jnp.int32, (CR, 128), 1)
    d_rad, d_circ, fourth = [], [], []
    for f in range(NF):
        tf = t * NF + f
        mid = cell(f, q)
        edge = edge_ref[tf]
        left = edge if q == 0 else cell(f, q - 1)
        right = edge if q == LT - 1 else cell(f, q + 1)
        m1 = jnp.where(lane < 1, pltpu.roll(left, 1, 1), pltpu.roll(mid, 1, 1))
        m2 = jnp.where(lane < 2, pltpu.roll(left, 2, 1), pltpu.roll(mid, 2, 1))
        p1 = jnp.where(lane >= 127, pltpu.roll(right, 127, 1), pltpu.roll(mid, 127, 1))
        p2 = jnp.where(lane >= 126, pltpu.roll(right, 126, 1), pltpu.roll(mid, 126, 1))
        halo = halo_ref[2 * tf:2 * tf + 2, lanes(q)]
        base = f * 32
        pad_ref[base + 6:base + 8, :] = halo * has_low
        pad_ref[base + 8:base + 24, :] = mid
        pad_ref[base + 24:base + 26, :] = halo * has_high
        rm2 = pad_ref[base + 6:base + 22, :]
        rm1 = pad_ref[base + 7:base + 23, :]
        rp1 = pad_ref[base + 9:base + 25, :]
        rp2 = pad_ref[base + 10:base + 26, :]
        d_circ.append(0.5 * (m1 - p1))
        d_rad.append(0.5 * (rm1 - rp1))
        fourth.append((m2 + p2) + (rm2 + rp2) - 4.0 * ((m1 + p1) + (rm1 + rp1)) + 12.0 * mid)
    out = []
    for j in range(NF):
        acc = (EPS4 * dis) * fourth[j]
        for i in range(NF):
            acc = acc + jr_ref[t, i, j, :, lanes(q)].astype(F32) * d_rad[i]
            acc = acc + jc_ref[t, i, j, :, lanes(q)].astype(F32) * d_circ[i]
        out.append(acc)
    return out


def first_kernel(rad_ref, psi_ref, edge_ref, halo_ref, jr_ref, jc_ref, dis_ref, step_ref, src_ref, x_ref, pad_ref):
    rad = rad_ref[0]
    has_low = (rad == 1).astype(F32)
    has_high = (rad == 0).astype(F32)
    for t in range(TD):
        for q in range(LT):
            cell = lambda f, qq: psi_ref[t * NF + f, :, lanes(qq)]
            res = local_operator(cell, edge_ref, halo_ref, pad_ref, jr_ref, jc_ref, dis_ref[:, lanes(q)], has_low, has_high, t, q)
            sigma = step_ref[:, lanes(q)]
            for f in range(NF):
                mid = cell(f, q)
                w = mid - sigma * (res[f] - src_ref[t * NF + f, :, lanes(q)])
                for h in range(HB):
                    x_ref[pl.ds(q * GRP + row_of(t, 0, f, h), 8, stride=ROWS), :] = mid[8 * h:8 * h + 8]
                    x_ref[pl.ds(q * GRP + row_of(t, 1, f, h), 8, stride=ROWS), :] = w[8 * h:8 * h + 8]


def time_kernel(table_ref, sig_ref, y_ref, v_ref):
    table = table_ref[...]

    def apply(x):
        high = x.astype(BF)
        low = (x - high.astype(F32)).astype(BF)
        return jnp.dot(table, jnp.concatenate([high, low, high], axis=0), preferred_element_type=F32)

    def gather(what):
        cols = []
        for f in range(NF):
            for h in range(HB):
                cols.append(jnp.concatenate(
                    [y_ref[pl.ds(row_of(t, what, f, h), 32, stride=ROWS), :] for t in range(TD)], axis=0))
        return jnp.concatenate(cols, axis=1)

    def scatter(what, value):
        for f in range(NF):
            for h in range(HB):
                for t in range(TD):
                    v_ref[pl.ds(row_of(t, what, f, h), 32, stride=ROWS), :] = value[32 * t:32 * t + 32, lanes(f * HB + h)]

    sigma = jnp.concatenate([sig_ref[0:1, :], sig_ref[1:2, :]] * NF, axis=1)
    time0 = apply(gather(0))
    scatter(0, time0)
    psi1 = gather(1) - sigma * time0
    scatter(1, apply(psi1))


def middle_kernel(rad_ref, x_ref, u_ref, step_ref, src_ref, psi_ref, base_ref, edge_ref, halo_ref):
    rad = rad_ref[0]
    lane = lax.broadcasted_iota(jnp.int32, (CR, 128), 1)
    for t in range(TD):
        for f in range(NF):
            tf = t * NF + f
            tiles = []
            for q in range(LT):
                sigma = step_ref[:, lanes(q)]

                def plane(ref, what):
                    return jnp.concatenate(
                        [ref[pl.ds(q * GRP + row_of(t, what, f, h), 8, stride=ROWS), :] for h in range(HB)], axis=0)

                psi1 = plane(x_ref, 1) - sigma * plane(u_ref, 0)
                base_ref[tf, :, lanes(q)] = psi1 - sigma * (plane(u_ref, 1) - src_ref[tf, :, lanes(q)])
                psi_ref[tf, :, lanes(q)] = psi1
                tiles.append(psi1)
                halo_ref[2 * tf:2 * tf + 2, lanes(q)] = jnp.where(rad == 0, psi1[14:16], psi1[0:2])
            edge_ref[tf] = jnp.where(lane < 64, tiles[0], tiles[3])


def last_kernel(rad_ref, psi_ref, base_ref, edge_ref, halo_ref, jr_ref, jc_ref, dis_ref, step_ref, cell_ref, owner_ref,
                local_ref, sd_ref, out_ref, sens_ref, pad_ref):
    rad = rad_ref[0]
    has_low = (rad == 1).astype(F32)
    has_high = (rad == 0).astype(F32)
    for t in range(TD):
        for q in range(LT):
            cell = lambda f, qq: psi_ref[t * NF + f, :, lanes(qq)]
            res = local_operator(cell, edge_ref, halo_ref, pad_ref, jr_ref, jc_ref, dis_ref[:, lanes(q)], has_low, has_high, t, q)
            sigma = step_ref[:, lanes(q)]
            for f in range(NF):
                out_ref[t * NF + f, :, lanes(q)] = base_ref[t * NF + f, :, lanes(q)] - sigma * res[f]
    cells = cell_ref[...]
    row, col = cells // CT, cells % CT
    pick = (lax.broadcasted_iota(jnp.int32, (CT, NODES), 0) == col).astype(F32).astype(BF)
    mask = (lax.broadcasted_iota(jnp.int32, (CR, NODES), 0) == row).astype(F32)
    acc = [jnp.zeros((CR, NODES), F32) for _ in range(3)]
    for t in range(TD):
        plane = out_ref[t * NF:(t + 1) * NF].reshape(NF * CR, CT)
        high = plane.astype(BF)
        low = (plane - high.astype(F32)).astype(BF)
        both = jnp.dot(jnp.concatenate([high, low], axis=0), pick, preferred_element_type=F32)
        value = both[:NF * CR] + both[NF * CR:]
        for f in range(NF):
            here = value[f * CR:(f + 1) * CR]
            for k in range(3):
                weight = sd_ref[t * NF + f, k:k + 1, :].astype(F32)
                acc[k] = acc[k] + here * weight
    owner = owner_ref[...]
    parts = []
    for k in range(3):
        kept = acc[k] * mask
        for s in range(2):
            parts.append(kept * (owner == s).astype(F32))
    stack = jnp.concatenate(parts, axis=0)
    high = stack.astype(BF)
    low = (stack - high.astype(F32)).astype(BF)
    label = (lax.broadcasted_iota(jnp.int32, (128, NODES), 0) % VAR_DEV == local_ref[...]).astype(F32).astype(BF)
    dims = (((1,), (1,)), ((), ()))
    total = lax.dot_general(high, label, dims, preferred_element_type=F32) + lax.dot_general(
        low, label, dims, preferred_element_type=F32)
    lane = lax.broadcasted_iota(jnp.int32, (1, 128), 1)
    line = []
    for s in range(2):
        full = jnp.zeros((1, 128), F32)
        for k in range(3):
            at = (k * 2 + s) * CR
            part = jnp.sum(total[at:at + CR], axis=0, keepdims=True)
            full = jnp.where(lane // VAR_DEV == k, part, full)
        line.append(full)
    peer = lax.broadcasted_iota(jnp.int32, (128, 128), 0)
    sens_ref[...] = jnp.where((peer // 2) % 2 == 0, line[0], line[1])


def call(kernel, outs, n_in, smem_first, scratch=()):
    specs = [pl.BlockSpec(memory_space=pltpu.VMEM)] * n_in
    if smem_first:
        specs = [pl.BlockSpec(memory_space=pltpu.SMEM)] + specs
    single = not isinstance(outs, (list, tuple))
    shapes = [outs] if single else list(outs)
    out_specs = [pl.BlockSpec(memory_space=pltpu.VMEM)] * len(shapes)
    return pl.pallas_call(
        kernel,
        out_shape=outs if single else shapes,
        in_specs=specs,
        out_specs=out_specs[0] if single else out_specs,
        scratch_shapes=list(scratch),
        compiler_params=pltpu.CompilerParams(vmem_limit_bytes=40 * 1024 * 1024),
    )


def f32(*shape):
    return jax.ShapeDtypeStruct(shape, F32)


def body(adjoint_start, jac_rad, jac_circ, dissip, pseudo_step, source, node_cell, node_owner, node_local, shape_deriv):
    me = lax.axis_index("inst")
    rad = lax.axis_index("rad")
    rad_s = rad.astype(jnp.int32).reshape(1)
    n = TD * NF
    psi0 = adjoint_start.reshape(n, CR, CT)
    src = source.reshape(n, CR, CT)
    lane = lax.broadcasted_iota(jnp.int32, (1, 1, 128), 2)
    edge = jnp.where(lane < 64, psi0[:, :, :128], psi0[:, :, 384:])
    halo = jnp.where(rad == 0, psi0[:, 14:16], psi0[:, 0:2]).reshape(2 * n, CT)
    edge = lax.ppermute(edge, "span", SWAP)
    halo = lax.ppermute(halo, "rad", SWAP)
    pad = pltpu.VMEM((NF * 32, 128), F32)
    x = call(first_kernel, f32(32 * ROWS, 128), 8, True, (pad,))(
        rad_s, psi0, edge, halo, jac_rad, jac_circ, dissip, pseudo_step, src)
    y = lax.all_to_all(x, "inst", 0, 0, tiled=True)
    sig = lax.dynamic_slice(pseudo_step.reshape(2, 8, LT, 128), (0, me % 8, me // 8, 0), (2, 1, 1, 128)).reshape(2, 128)
    v = call(time_kernel, f32(32 * ROWS, 128), 3, False)(jnp.asarray(spectral_blocks()), sig, y)
    u = lax.all_to_all(v, "inst", 0, 0, tiled=True)
    psi1, base, edge, halo = call(
        middle_kernel, (f32(n, CR, CT), f32(n, CR, CT), f32(n, CR, 128), f32(2 * n, CT)), 4, True)(
        rad_s, x, u, pseudo_step, src)
    edge = lax.ppermute(edge, "span", SWAP)
    halo = lax.ppermute(halo, "rad", SWAP)
    psi2, parts = call(last_kernel, (f32(n, CR, CT), f32(128, 128)), 12, True, (pad,))(
        rad_s, psi1, base, edge, halo, jac_rad, jac_circ, dissip, pseudo_step, node_cell.reshape(1, NODES),
        node_owner.reshape(1, NODES), node_local.reshape(1, NODES), shape_deriv.reshape(n, 3, NODES))
    got = lax.all_to_all(parts, ALL, 0, 0, tiled=True)
    sens = jnp.sum(got, axis=0)[:3 * VAR_DEV].reshape(3, VAR_DEV)
    return psi2.reshape(TD, NF, CR, CT), sens


def solution(mesh):
    in_specs = (
        P("inst", None, "rad", "span"),
        P("inst", None, None, "rad", "span"),
        P("inst", None, None, "rad", "span"),
        P("rad", "span"),
        P("rad", "span"),
        P("inst", None, "rad", "span"),
        P(("span", "rad")),
        P(("span", "rad"), None),
        P(("span", "rad")),
        P("inst", None, None, ("span", "rad")),
    )
    out_specs = (P("inst", None, "rad", "span"), P(None, "span"))
    return jax.shard_map(body, mesh=mesh, in_specs=in_specs, out_specs=out_specs, check_vma=False)
```

time: 500 us -> 80.2 us (0.16)
  waiting for transfers between devices: 200 us -> 20.9 us
  blocking collectives: 180 us -> 30.9 us
  matrix products: 45.3 us -> 0 us
  local copies, waits for them, and re-layouts: 37.9 us -> 4.71 us
  between operations: 14.4 us -> 0.82 us
  Pallas kernels: 0 us -> 6.02 us
  other arithmetic: 7.21 us -> 2.17 us
    all_gather x2 -> x0, waiting for transfers between devices: 199 us -> none  [body(): lax.all_gather(psi, 'inst', axis=0, tiled=True)]
    psum x1 -> x0, blocking collectives: 176 us -> none  [body(): sensitivity = lax.psum(partial_sens, ('inst', 'rad'))]
    dot_general x4 -> x0, matrix products: 45.3 us -> none  [the longest x2 38.2 us: body(): jnp.einsum('st,sfrc->tfrc', my_cols, lax.all_gather(psi, 'inst', axis=0,...]
    all_to_all x1 -> x2, blocking collectives: 3.75 us -> 30.9 us  [the longest x1 17.7 us: body(): u = lax.all_to_all(v, 'inst', 0, 0, tiled=True)]
    all_to_all x1, waiting for transfers between devices: 0.01 us -> 14.9 us  [body(): y = lax.all_to_all(x, 'inst', 0, 0, tiled=True)]
    scatter x2 -> x0, local copies, waits for them, and re-layouts: 8.77 us -> none  [the longest x1 5.04 us: body(): labels = jnp.full((n_span * capacity,), VAR_DEV, jnp.int32).at[slot].set(...]
    reshape x2, local copies, waits for them, and re-layouts: 8.15 us -> 0.69 us  [the longest x1 0.66 us: body(): sens = jnp.sum(got, axis=0)[:3 * VAR_DEV].reshape(3, VAR_DEV)]
    gather x1 -> x0, local copies, waits for them, and re-layouts: 7.41 us -> none  [body(): values = flat[:, :, node_cell]]
  transfers between devices with their start and end apart: 11 -> 5, of which waited for: 3 -> 3; matrix products, arithmetic and copies ran while one was open for 14% -> 1% of each run, Pallas kernels for 0% -> 0%
where the time goes in v1:
time: 80.2 us; the launch traced here: 79 us
  blocking collectives  30.9 us (39%)
  waiting for transfers between devices  20.9 us (26%)
  starting transfers between devices  13.4 us (17%)
  Pallas kernels  6.02 us (8%)
  local copies, waits for them, and re-layouts  4.71 us (6%)
  other arithmetic  2.17 us (3%)
  between operations  0.82 us (1%)
    all_to_all x1, blocking collectives, body(): u = lax.all_to_all(v, 'inst', 0, 0, tiled=True)  17.7 us
    all_to_all x1, waiting for transfers between devices, body(): y = lax.all_to_all(x, 'inst', 0, 0, tiled=True)  14.9 us
    all_to_all x1, blocking collectives, body(): got = lax.all_to_all(parts, ALL, 0, 0, tiled=True)  13.2 us
    all_to_all x1, starting transfers between devices, body(): y = lax.all_to_all(x, 'inst', 0, 0, tiled=True)  10.9 us
    ppermute x2, waiting for transfers between devices, body(): halo = lax.ppermute(halo, 'rad', SWAP)  5.97 us
    unnamed x27, local copies, waits for them, and re-layouts  4.01 us
    ppermute x2, starting transfers between devices, body(): halo = lax.ppermute(halo, 'rad', SWAP)  2.37 us
    pallas_call x1, Pallas kernels, body(): call(last_kernel, (f32(n, CR, CT), f32(128, 128)), 12, True, (pad,))  2.34 us
  transfers between devices with their start and end apart: 5, of which 3 were waited for; matrix products, arithmetic and copies ran while one was open for 1% of the time, Pallas kernels for 0%

profile of v1, /device:TPU:0, one launch (start us, length us, event | category | flops | bytes accessed | tf_op | source)
XLA Modules:
  0.0 79.0 jit_solution(10585826725431834133)
XLA Ops:
  0.6 0.0 copy-start.4
  0.7 1.0 %slice_select_fusion = f32[10,16,128]{2,1,0:T(8,128)S(1)} fusion(f32[10,16,512]{2,1,0:T(8,128)} %bitcast.25, pred[128]{0:T(512)(128)(4,1)S(1)} %iota_compare_fusion), kind=kLoop, calls=%fused_computation | loop fusion | flops 20480 | bytes 245888 | tf_op jit(solution)/shard_map/jit(_where)/select_n | solution.py:233
  1.6 0.1 collective-permute-start
  1.7 1.0 %slice_select_fusion.1 = f32[10,2,512]{2,1,0:T(2,128)S(1)} fusion(f32[10,16,512]{2,1,0:T(8,128)} %bitcast.26, pred[]{:T(512)S(6)} %eq.5), kind=kLoop, calls=%fused_computation.1 | loop fusion | flops 10240 | bytes 122881 | tf_op jit(solution)/shard_map/jit(_where)/select_n | solution.py:234
  2.8 0.0 copy-start.6
  2.8 0.0 copy-start.7
  2.8 1.7 %collective-permute-start.1 = (f32[20,512]{1,0:T(8,128)S(1)}, f32[20,512]{1,0:T(8,128)S(1)}, u32[]{:S(2)}, u32[]{:S(2)}) collective-permute-start(f32[20,512]{1,0:T(8,128)S(1)} %reshape.61), channel_id=1, source_target_pairs={{0,1},{1,0},{2,3},{3,2},{4,5},{5,4},{6,7},{7,6},{8,9},{9,8},{10,11... | collective-permute-start | bytes 122888 | tf_op jit(solution)/shard_map/ppermute | solution.py:236
  4.5 2.6 %collective-permute-done.1.halo_ref = f32[20,512]{1,0:T(8,128)S(1)} collective-permute-done((f32[20,512]{1,0:T(8,128)S(1)}, f32[20,512]{1,0:T(8,128)S(1)}, u32[]{:S(2)}, u32[]{:S(2)}) %collective-permute-start.1) | collective-permute-done | bytes 40992 | tf_op jit(solution)/shard_map/ppermute | solution.py:236
  7.0 0.0 collective-permute-done.edge_ref
  7.0 0.0 copy-done.4
  7.0 0.0 copy-done.6
  7.1 0.0 copy-done.7
  7.1 0.0 copy-start
  7.1 1.1 %copy-done = bf16[2,5,5,16,512]{4,3,2,1,0:T(8,128)(2,1)S(1)} copy-done((bf16[2,5,5,16,512]{4,3,2,1,0:T(8,128)(2,1)S(1)}, bf16[2,5,5,16,512]{4,3,2,1,0:T(8,128)(2,1)}, u32[]{:S(2)}) %copy-start) | copy-done | bytes 819224
  8.2 0.0 copy-start.2
  8.2 1.1 %copy-done.2 = bf16[2,5,5,16,512]{4,3,2,1,0:T(8,128)(2,1)S(1)} copy-done((bf16[2,5,5,16,512]{4,3,2,1,0:T(8,128)(2,1)S(1)}, bf16[2,5,5,16,512]{4,3,2,1,0:T(8,128)(2,1)}, u32[]{:S(2)}) %copy-start.2) | copy-done | bytes 819224
  9.4 0.0 copy-start.5
  9.4 1.0 %copy-done.5 = f32[2,5,16,512]{3,2,1,0:T(8,128)S(1)} copy-done((f32[2,5,16,512]{3,2,1,0:T(8,128)S(1)}, f32[2,5,16,512]{3,2,1,0:T(8,128)}, u32[]{:S(2)}) %copy-start.5) | copy-done | bytes 327704
  10.3 1.9 %shard_map.122.x_ref = f32[1280,128]{1,0:T(8,128)} custom-call(s32[1]{0:T(128)} %bitcast.rad_ref, f32[10,16,512]{2,1,0:T(8,128)S(1)} %bitcast.27, f32[10,16,128]{2,1,0:T(8,128)S(1)} %collective-permute-done.edge_ref, f32[20,512]{1,0:T(8,128)S(1)} %collective-permute-done.1.halo_ref, bf16[2,5,5,16,512]{4,3,2,1,0:T(8,128)(2,1)S(1)} %copy-done, ...), custom_call_target="tpu_custom_call" | custom-call | tf_op jit(solution)/shard_map/pallas_call | solution.py:238
  12.2 10.9 %all-to-all-start = ((f32[32,40,128]{2,1,0:T(8,128)}), f32[32,40,128]{2,1,0:T(8,128)S(1)}, u32[]{:S(2)}, u32[]{:S(2)}) async-start(f32[32,40,128]{2,1,0:T(8,128)} %bitcast.5), calls=%async_computation | async-start | bytes 1310720 | tf_op jit(solution)/shard_map/all_to_all | solution.py:240
  23.1 0.0 copy-start.8
  23.1 14.9 %all-to-all-done = f32[32,40,128]{2,1,0:T(8,128)S(1)} async-done(((f32[32,40,128]{2,1,0:T(8,128)}), f32[32,40,128]{2,1,0:T(8,128)S(1)}, u32[]{:S(2)}, u32[]{:S(2)}) %all-to-all-start) | async-done | bytes 655392 | tf_op jit(solution)/shard_map/all_to_all | solution.py:240
  38.1 0.0 copy-done.8
  38.1 0.4 shard_map.123
  38.5 0.0 copy-start.12
  38.5 17.7 %all_to_all.31 = f32[32,40,128]{2,1,0:T(8,128)S(1)} all-to-all(f32[32,40,128]{2,1,0:T(8,128)S(1)} %bitcast.22), channel_id=1, replica_groups=mesh['inst'=32,'span'=2,'rad'=2] {'inst'}, dimensions={0} | all-to-all | bytes 1310720 | tf_op jit(solution)/shard_map/all_to_all | solution.py:243
  56.2 0.0 copy-start.1
  56.2 0.0 copy-start.3
  56.2 1.4 %shard_map.124 = (f32[10,16,512]{2,1,0:T(8,128)S(1)}, f32[10,16,512]{2,1,0:T(8,128)S(1)}, f32[10,16,128]{2,1,0:T(8,128)S(1)}, f32[20,512]{1,0:T(8,128)S(1)}) custom-call(s32[1]{0:T(128)} %bitcast.rad_ref, f32[1280,128]{1,0:T(8,128)} %shard_map.122.x_ref, f32[1280,128]{1,0:T(8,128)S(1)} %bitcast.21, f32[16,512]{1,0:T(8,128)S(1)} %copy-done.6, ...), custom_call_target="tpu_custom_call" | custom-call | tf_op jit(solution)/shard_map/pallas_call | solution.py:244
  57.6 0.1 collective-permute-start.2
  57.7 0.7 collective-permute-start.3
  58.4 0.0 copy-done.12
  58.4 0.0 copy-start.11
  58.4 3.4 %collective-permute-done.3.halo_ref = f32[20,512]{1,0:T(8,128)S(1)} collective-permute-done((f32[20,512]{1,0:T(8,128)S(1)}, f32[20,512]{1,0:T(8,128)S(1)}, u32[]{:S(2)}, u32[]{:S(2)}) %collective-permute-start.3) | collective-permute-done | bytes 40992 | tf_op jit(solution)/shard_map/ppermute | solution.py:248
  61.9 0.0 collective-permute-done.2.edge_ref
  61.9 0.0 copy-start.10
  61.9 0.0 copy-start.9
  61.9 0.0 copy-done.1
  61.9 0.0 copy-done.3
  61.9 0.0 copy-done.11
  61.9 0.7 copy-done.10
  62.6 0.0 copy-done.9
  62.6 2.3 %shard_map.125 = (f32[10,16,512]{2,1,0:T(8,128)}, f32[128,128]{1,0:T(8,128)S(1)}) custom-call(s32[1]{0:T(128)} %bitcast.rad_ref, f32[10,16,512]{2,1,0:T(8,128)S(1)} %get-tuple-element.8.psi_ref, f32[10,16,512]{2,1,0:T(8,128)S(1)} %get-tuple-element.9.base_ref, f32[10,16,128]{2,1,0:T(8,128)S(1)} %collective-permute-done.2.edge_ref, ...), custom_call_target="tpu_custom_call" | custom-call | tf_op jit(solution)/shard_map/pallas_call | solution.py:249
  64.9 13.2 %all_to_all.32 = f32[128,1,128]{2,1,0:T(1,128)S(1)} all-to-all(f32[128,1,128]{2,1,0:T(1,128)S(1)} %bitcast.30), channel_id=1, replica_groups=mesh['inst'=32,'span'=2,'rad'=2] {'inst','span','rad'}, dimensions={0} | all-to-all | bytes 131072 | tf_op jit(solution)/shard_map/all_to_all | solution.py:252
  78.2 0.2 reduce_sum.9
  78.3 0.7 reshape.70
  (4 shorter events, 0.1 us)
Async XLA Ops:
  0.6 6.4 %copy-start.4 = (f32[2,5,16,512]{3,2,1,0:T(8,128)S(1)}, f32[2,5,16,512]{3,2,1,0:T(8,128)}, u32[]{:S(2)}) copy-start(f32[2,5,16,512]{3,2,1,0:T(8,128)} %param.16) | copy-start | bytes 983044
  1.6 5.4 %collective-permute-start = (f32[10,16,128]{2,1,0:T(8,128)S(1)}, f32[10,16,128]{2,1,0:T(8,128)S(1)}, u32[]{:S(2)}, u32[]{:S(2)}) collective-permute-start(f32[10,16,128]{2,1,0:T(8,128)S(1)} %slice_select_fusion), channel_id=1, source_target_pairs={{0,2},{2,0},{1,3},{3,1},{4,6},{6,4},{5,7},{7,5},{8,10},{10,8},{9,1... | collective-permute-start | bytes 245768 | tf_op jit(solution)/shard_map/ppermute | solution.py:235
  2.8 4.3 %copy-start.6 = (f32[16,512]{1,0:T(8,128)S(1)}, f32[16,512]{1,0:T(8,128)}, u32[]{:S(2)}) copy-start(f32[16,512]{1,0:T(8,128)} %step_ref.5) | copy-start | bytes 98308
  2.8 4.3 %copy-start.7 = (f32[16,512]{1,0:T(8,128)S(1)}, f32[16,512]{1,0:T(8,128)}, u32[]{:S(2)}) copy-start(f32[16,512]{1,0:T(8,128)} %dis_ref.3) | copy-start | bytes 98308
  2.8 4.2 %collective-permute-start.1 = (f32[20,512]{1,0:T(8,128)S(1)}, f32[20,512]{1,0:T(8,128)S(1)}, u32[]{:S(2)}, u32[]{:S(2)}) collective-permute-start(f32[20,512]{1,0:T(8,128)S(1)} %reshape.61), channel_id=1, source_target_pairs={{0,1},{1,0},{2,3},{3,2},{4,5},{5,4},{6,7},{7,6},{8,9},{9,8},{10,11... | collective-permute-start | bytes 122888 | tf_op jit(solution)/shard_map/ppermute | solution.py:236
  7.1 1.1 %copy-start = (bf16[2,5,5,16,512]{4,3,2,1,0:T(8,128)(2,1)S(1)}, bf16[2,5,5,16,512]{4,3,2,1,0:T(8,128)(2,1)}, u32[]{:S(2)}) copy-start(bf16[2,5,5,16,512]{4,3,2,1,0:T(8,128)(2,1)} %jr_ref.3) | copy-start | bytes 2457604
  8.2 1.1 %copy-start.2 = (bf16[2,5,5,16,512]{4,3,2,1,0:T(8,128)(2,1)S(1)}, bf16[2,5,5,16,512]{4,3,2,1,0:T(8,128)(2,1)}, u32[]{:S(2)}) copy-start(bf16[2,5,5,16,512]{4,3,2,1,0:T(8,128)(2,1)} %jc_ref.3) | copy-start | bytes 2457604
  9.4 1.0 %copy-start.5 = (f32[2,5,16,512]{3,2,1,0:T(8,128)S(1)}, f32[2,5,16,512]{3,2,1,0:T(8,128)}, u32[]{:S(2)}) copy-start(f32[2,5,16,512]{3,2,1,0:T(8,128)} %param.11) | copy-start | bytes 983044
  12.2 25.9 %all-to-all-start = ((f32[32,40,128]{2,1,0:T(8,128)}), f32[32,40,128]{2,1,0:T(8,128)S(1)}, u32[]{:S(2)}, u32[]{:S(2)}) async-start(f32[32,40,128]{2,1,0:T(8,128)} %bitcast.5), calls=%async_computation | async-start | bytes 1310720 | tf_op jit(solution)/shard_map/all_to_all | solution.py:240
  23.1 15.0 %copy-start.8 = (bf16[64,192]{1,0:T(8,128)(2,1)S(1)}, bf16[64,192]{1,0:T(8,128)(2,1)}, u32[]{:S(2)}) copy-start(bf16[64,192]{1,0:T(8,128)(2,1)} %constant.45.clone.table_ref) | copy-start | bytes 73732
  38.5 19.9 %copy-start.12 = (bf16[2,5,3,1024]{3,0,2,1:T(2,128)(2,1)S(1)}, bf16[2,5,3,1024]{3,0,2,1:T(2,128)(2,1)}, u32[]{:S(2)}) copy-start(bf16[2,5,3,1024]{3,0,2,1:T(2,128)(2,1)} %param.20) | copy-start | bytes 184324
  56.2 5.7 %copy-start.1 = (bf16[2,5,5,16,512]{4,3,2,1,0:T(8,128)(2,1)S(1)}, bf16[2,5,5,16,512]{4,3,2,1,0:T(8,128)(2,1)}, u32[]{:S(2)}) copy-start(bf16[2,5,5,16,512]{4,3,2,1,0:T(8,128)(2,1)} %jr_ref.3) | copy-start | bytes 2457604
  56.2 5.7 %copy-start.3 = (bf16[2,5,5,16,512]{4,3,2,1,0:T(8,128)(2,1)S(1)}, bf16[2,5,5,16,512]{4,3,2,1,0:T(8,128)(2,1)}, u32[]{:S(2)}) copy-start(bf16[2,5,5,16,512]{4,3,2,1,0:T(8,128)(2,1)} %jc_ref.3) | copy-start | bytes 2457604
  57.6 4.3 %collective-permute-start.2 = (f32[10,16,128]{2,1,0:T(8,128)S(1)}, f32[10,16,128]{2,1,0:T(8,128)S(1)}, u32[]{:S(2)}, u32[]{:S(2)}) collective-permute-start(f32[10,16,128]{2,1,0:T(8,128)S(1)} %get-tuple-element.10), channel_id=1, source_target_pairs={{0,2},{2,0},{1,3},{3,1},{4,6},{6,4},{5,7},{7,5},{8,10},{10,8},{9,1... | collective-permute-start | bytes 245768 | tf_op jit(solution)/shard_map/ppermute | solution.py:247
  57.7 4.2 %collective-permute-start.3 = (f32[20,512]{1,0:T(8,128)S(1)}, f32[20,512]{1,0:T(8,128)S(1)}, u32[]{:S(2)}, u32[]{:S(2)}) collective-permute-start(f32[20,512]{1,0:T(8,128)S(1)} %get-tuple-element.11), channel_id=1, source_target_pairs={{0,1},{1,0},{2,3},{3,2},{4,5},{5,4},{6,7},{7,6},{8,9},{9,8},{10,11... | collective-permute-start | bytes 122888 | tf_op jit(solution)/shard_map/ppermute | solution.py:248
  58.4 3.5 %copy-start.11 = (s32[1024]{0:T(1024)S(1)}, s32[1024]{0:T(1024)}, u32[]{:S(2)}) copy-start(s32[1024]{0:T(1024)} %param.19) | copy-start | bytes 12292
  61.9 0.7 copy-start.10
  61.9 0.7 copy-start.9

commit v2 on v1

v2 whole, which is shorter than its diff:
```python
import jax
import jax.numpy as jnp
import numpy as np
from jax import lax
from jax.experimental import pallas as pl
from jax.experimental.pallas import tpu as pltpu
from jax.sharding import PartitionSpec as P

NT = 64
TD = 2
NF = 5
CR = 16
CT = 512
LT = 4
HB = 2
ROWS = 40
GRP = 8 * ROWS
NODES = 1024
VAR_DEV = 32
EPS4 = 0.0625
F32 = jnp.float32
BF = jnp.bfloat16
SWAP = [(0, 1), (1, 0)]
ALL = ("inst", "span", "rad")


def spectral_blocks():
    index = np.arange(NT)
    diff = index[:, None] - index[None, :]
    safe = np.where(diff == 0, 1, diff)
    table = np.where(diff == 0, 0.0, 0.5 * np.where(diff % 2 == 0, 1.0, -1.0) / np.tan(np.pi * safe / NT))
    order = np.concatenate([index[0::2], index[1::2]])
    apply = table.T[order][:, order].astype(np.float32)
    high = apply.astype(BF)
    low = (apply - high.astype(np.float32)).astype(BF)
    return np.concatenate([high, high, low], axis=1)


def row_of(t, what, f, h):
    return ((t * 2 + what) * NF + f) * HB + h


def lanes(q):
    return slice(128 * q, 128 * q + 128)


def interior(cell, pad_ref, jr, jc, dis, q):
    lane = lax.broadcasted_iota(jnp.int32, (CR, 128), 1)
    none = jnp.zeros((CR, 128), F32)
    d_rad, d_circ, fourth = [], [], []
    for f in range(NF):
        mid = cell(f, q)
        left = none if q == 0 else cell(f, q - 1)
        right = none if q == LT - 1 else cell(f, q + 1)
        m1 = jnp.where(lane < 1, pltpu.roll(left, 1, 1), pltpu.roll(mid, 1, 1))
        m2 = jnp.where(lane < 2, pltpu.roll(left, 2, 1), pltpu.roll(mid, 2, 1))
        p1 = jnp.where(lane >= 127, pltpu.roll(right, 127, 1), pltpu.roll(mid, 127, 1))
        p2 = jnp.where(lane >= 126, pltpu.roll(right, 126, 1), pltpu.roll(mid, 126, 1))
        base = f * 32
        pad_ref[base + 8:base + 24, :] = mid
        rm2 = pad_ref[base + 6:base + 22, :]
        rm1 = pad_ref[base + 7:base + 23, :]
        rp1 = pad_ref[base + 9:base + 25, :]
        rp2 = pad_ref[base + 10:base + 26, :]
        d_circ.append(0.5 * (m1 - p1))
        d_rad.append(0.5 * (rm1 - rp1))
        fourth.append((m2 + p2) + (rm2 + rp2) - 4.0 * ((m1 + p1) + (rm1 + rp1)) + 12.0 * mid)
    out = []
    for j in range(NF):
        acc = (EPS4 * dis) * fourth[j]
        for i in range(NF):
            acc = acc + jr(i, j).astype(F32) * d_rad[i]
            acc = acc + jc(i, j).astype(F32) * d_circ[i]
        out.append(acc)
    return out


def clear_pad(pad_ref):
    pad_ref[...] = jnp.zeros(pad_ref.shape, F32)


def corrections(rad, edge_ref, halo_ref, jrb_ref, jce_ref, dis_ref, t):
    lane = lax.broadcasted_iota(jnp.int32, (CR, 128), 1)
    diff, fourth = [], []
    edge = edge_ref[t]
    for f in range(NF):
        turn = lambda by: pltpu.roll(edge, (by - 4 * f) % 128, 1)
        m1 = jnp.where(lane < 1, turn(1), 0.0)
        m2 = jnp.where(lane < 2, turn(2), 0.0)
        p1 = jnp.where(lane >= 127, turn(-1), 0.0)
        p2 = jnp.where(lane >= 126, turn(-2), 0.0)
        diff.append(0.5 * (m1 - p1))
        fourth.append(m2 + p2 - 4.0 * (m1 + p1))
    dis_edge = EPS4 * jnp.where(lane < 64, dis_ref[:, lanes(0)], dis_ref[:, lanes(LT - 1)])
    circ = []
    for j in range(NF):
        acc = dis_edge * fourth[j]
        for i in range(NF):
            acc = acc + jce_ref[t * NF + i, j].astype(F32) * diff[i]
        circ.append(acc)
    near_row = jnp.where(rad == 0, CR - 1, 0)
    next_row = jnp.where(rad == 0, CR - 2, 1)
    sign = jnp.where(rad == 0, -0.5, 0.5)
    first, second = [halo_ref[(2 * t + m) * NF:(2 * t + m + 1) * NF, :] for m in range(2)]
    near = jnp.where(rad == 0, first, second)
    far = jnp.where(rad == 0, second, first)
    dis_near = EPS4 * dis_ref[pl.ds(near_row, 1), :]
    dis_next = EPS4 * dis_ref[pl.ds(next_row, 1), :]
    row_a = dis_near * (far - 4.0 * near)
    for i in range(NF):
        row_a = row_a + jrb_ref[t * NF + i] * (sign * near[i:i + 1])
    row_b = dis_next * near
    riota = lax.broadcasted_iota(jnp.int32, (CR, 128), 0)

    def fix(f, q):
        out = jnp.where(riota == near_row, row_a[f:f + 1, lanes(q)], 0.0)
        out = jnp.where(riota == next_row, row_b[f:f + 1, lanes(q)], out)
        if q == 0:
            out = out + jnp.where(lane < 64, circ[f], 0.0)
        if q == LT - 1:
            out = out + jnp.where(lane >= 64, circ[f], 0.0)
        return out

    return fix


def edge_kernel(rad_ref, psi_hbm, edge_ref, halo_ref, rows_ref, left_ref, right_ref, sem):
    rad = rad_ref[0]
    start = pl.multiple_of(8 * (1 - rad), 8)
    copies = [
        pltpu.make_async_copy(psi_hbm.at[:, pl.ds(start, 8), :], rows_ref, sem.at[0]),
        pltpu.make_async_copy(psi_hbm.at[:, :, pl.ds(0, 128)], left_ref, sem.at[1]),
        pltpu.make_async_copy(psi_hbm.at[:, :, pl.ds(CT - 128, 128)], right_ref, sem.at[2]),
    ]
    for copy in copies:
        copy.start()
    copies[0].wait()
    put_halo(halo_ref, lambda tf: rows_ref[tf], rad)
    copies[1].wait()
    copies[2].wait()
    put_edge(edge_ref, lambda tf: (left_ref[tf], right_ref[tf]))


def put_edge(edge_ref, ends):
    lane = lax.broadcasted_iota(jnp.int32, (CR, 128), 1)
    for t in range(TD):
        packed = None
        for f in range(NF):
            left, right = ends(t * NF + f)
            both = jnp.where(lane < 64, left, right)
            if f == 0:
                packed = both
            else:
                packed = jnp.where((lane >= 4 * f - 2) & (lane < 4 * f + 2), pltpu.roll(both, 4 * f, 1), packed)
        edge_ref[t] = packed


def put_halo(halo_ref, tile, rad):
    for t in range(TD):
        for f in range(NF):
            rows = tile(t * NF + f)
            pair = jnp.where(rad == 0, rows[6:8], rows[0:2])
            for m in range(2):
                at = (2 * t + m) * NF + f
                halo_ref[at:at + 1] = pair[m:m + 1]


def first_kernel(rad_ref, me_ref, dis_hbm, step_hbm, cell_hbm, owner_hbm, local_hbm, psi_hbm, src_hbm, jr_hbm, jc_hbm,
                 part_ref, psi_ref, jrb_ref, jce_ref, dis_ref, step_ref, sig_ref, ids_ref,
                 src_ref, jr_ref, jc_ref, pad_ref, cell_ref, owner_ref, local_ref, sem, sem_small):
    rad = rad_ref[0]
    small = [pltpu.make_async_copy(a, b, sem_small.at[i]) for i, (a, b) in enumerate([
        (dis_hbm, dis_ref), (step_hbm, step_ref), (cell_hbm, cell_ref), (owner_hbm, owner_ref), (local_hbm, local_ref)])]
    copies = []
    for t in range(TD):
        tf = pl.ds(t * NF, NF)
        copies.append([
            pltpu.make_async_copy(psi_hbm.at[tf], psi_ref.at[tf], sem.at[t, 0]),
            pltpu.make_async_copy(jr_hbm.at[t], jr_ref.at[t], sem.at[t, 1]),
            pltpu.make_async_copy(jc_hbm.at[t], jc_ref.at[t], sem.at[t, 2]),
            pltpu.make_async_copy(src_hbm.at[tf], src_ref.at[tf], sem.at[t, 3]),
        ])
    for copy in small + copies[0] + copies[1]:
        copy.start()
    clear_pad(pad_ref)
    lane = lax.broadcasted_iota(jnp.int32, (CR, 128), 1)
    for copy in small:
        copy.wait()
    ids_ref[0:1] = cell_ref[...] % CT
    ids_ref[1:2] = cell_ref[...] // CT
    ids_ref[2:3] = owner_ref[...]
    ids_ref[3:4] = local_ref[...]
    me = me_ref[0]
    sig = jnp.zeros((2, 128), F32)
    for p in range(8):
        for q in range(LT):
            here = jnp.concatenate([step_ref[p:p + 1, lanes(q)], step_ref[p + 8:p + 9, lanes(q)]], axis=0)
            sig = jnp.where(me == 8 * q + p, here, sig)
    sig_ref[...] = sig
    for t in range(TD):
        for copy in copies[t]:
            copy.wait()
        for q in range(LT):
            cell = lambda f, qq: psi_ref[t * NF + f, :, lanes(qq)]
            jr = lambda i, j: jr_ref[t, i, j, :, lanes(q)]
            jc = lambda i, j: jc_ref[t, i, j, :, lanes(q)]
            res = interior(cell, pad_ref, jr, jc, dis_ref[:, lanes(q)], q)
            sigma = step_ref[:, lanes(q)]
            for f in range(NF):
                part_ref[t * NF + f, :, lanes(q)] = cell(f, q) - sigma * (res[f] - src_ref[t * NF + f, :, lanes(q)])
        for i in range(NF):
            for j in range(NF):
                whole = jr_ref[t, i, j].astype(F32)
                jrb_ref[t * NF + i, j:j + 1] = jnp.where(rad == 0, whole[CR - 1:CR], whole[0:1])
                jce_ref[t * NF + i, j] = jnp.where(
                    lane < 64, jc_ref[t, i, j, :, lanes(0)].astype(F32), jc_ref[t, i, j, :, lanes(LT - 1)].astype(F32)).astype(BF)


def send_kernel(rad_ref, psi_ref, part_ref, edge_ref, halo_ref, jrb_ref, jce_ref, dis_ref, step_ref, x_ref, w_ref):
    rad = rad_ref[0]
    for t in range(TD):
        fix = corrections(rad, edge_ref, halo_ref, jrb_ref, jce_ref, dis_ref, t)
        for f in range(NF):
            for q in range(LT):
                mid = psi_ref[t * NF + f, :, lanes(q)]
                w = part_ref[t * NF + f, :, lanes(q)] - step_ref[:, lanes(q)] * fix(f, q)
                w_ref[t * NF + f, :, lanes(q)] = w
                for h in range(HB):
                    x_ref[pl.ds(q * GRP + row_of(t, 0, f, h), 8, stride=ROWS), :] = mid[8 * h:8 * h + 8]
                    x_ref[pl.ds(q * GRP + row_of(t, 1, f, h), 8, stride=ROWS), :] = w[8 * h:8 * h + 8]


def time_kernel(table_ref, sig_ref, y_ref, v_ref):
    table = table_ref[...]

    def apply(x):
        high = x.astype(BF)
        low = (x - high.astype(F32)).astype(BF)
        return jnp.dot(table, jnp.concatenate([high, low, high], axis=0), preferred_element_type=F32)

    def gather(what):
        cols = []
        for f in range(NF):
            for h in range(HB):
                cols.append(jnp.concatenate(
                    [y_ref[pl.ds(row_of(t, what, f, h), 32, stride=ROWS), :] for t in range(TD)], axis=0))
        return jnp.concatenate(cols, axis=1)

    def scatter(what, value):
        for f in range(NF):
            for h in range(HB):
                for t in range(TD):
                    v_ref[pl.ds(row_of(t, what, f, h), 32, stride=ROWS), :] = value[32 * t:32 * t + 32, lanes(f * HB + h)]

    sigma = jnp.concatenate([sig_ref[0:1, :], sig_ref[1:2, :]] * NF, axis=1)
    time0 = apply(gather(0))
    scatter(0, time0)
    psi1 = gather(1) - sigma * time0
    scatter(1, apply(psi1))


def plane(ref, what, t, f, q):
    return jnp.concatenate([ref[pl.ds(q * GRP + row_of(t, what, f, h), 8, stride=ROWS), :] for h in range(HB)], axis=0)


def rim_kernel(rad_ref, w_ref, u_ref, step_ref, edge_ref, halo_ref):
    rad = rad_ref[0]

    def ends(tf):
        return [w_ref[tf, :, lanes(q)] - step_ref[:, lanes(q)] * plane(u_ref, 0, tf // NF, tf % NF, q) for q in (0, LT - 1)]

    put_edge(edge_ref, ends)
    start = pl.multiple_of(8 * (1 - rad), 8)

    def rows(tf):
        t, f = tf // NF, tf % NF
        time = jnp.concatenate(
            [u_ref[pl.ds(q * GRP + row_of(t, 0, f, 0) + (1 - rad), 8, stride=ROWS), :] for q in range(LT)], axis=1)
        return w_ref[tf, pl.ds(start, 8), :] - step_ref[pl.ds(start, 8), :] * time

    put_halo(halo_ref, rows, rad)


def middle_kernel(w_ref, u_ref, jr_ref, jc_ref, dis_ref, step_ref, src_ref, ids_ref, base_ref, pick_ref, psi_ref, pad_ref):
    clear_pad(pad_ref)
    for t in range(TD):
        for f in range(NF):
            for q in range(LT):
                psi_ref[t * NF + f, :, lanes(q)] = (
                    w_ref[t * NF + f, :, lanes(q)] - step_ref[:, lanes(q)] * plane(u_ref, 0, t, f, q))
        for q in range(LT):
            cell = lambda f, qq: psi_ref[t * NF + f, :, lanes(qq)]
            jr = lambda i, j: jr_ref[t, i, j, :, lanes(q)]
            jc = lambda i, j: jc_ref[t, i, j, :, lanes(q)]
            res = interior(cell, pad_ref, jr, jc, dis_ref[:, lanes(q)], q)
            sigma = step_ref[:, lanes(q)]
            for f in range(NF):
                base_ref[t * NF + f, :, lanes(q)] = cell(f, q) - sigma * (
                    res[f] + plane(u_ref, 1, t, f, q) - src_ref[t * NF + f, :, lanes(q)])
    col = ids_ref[0:1]
    pick_ref[...] = (lax.broadcasted_iota(jnp.int32, (CT, NODES), 0) == col).astype(F32).astype(BF)


def last_kernel(rad_ref, base_ref, edge_ref, halo_ref, jrb_ref, jce_ref, dis_ref, step_ref, pick_ref, ids_ref, sd_ref,
                 out_hbm, sens_ref, psi_ref, sem):
    rad = rad_ref[0]
    row = ids_ref[1:2]
    pick = pick_ref[...]
    mask = (lax.broadcasted_iota(jnp.int32, (CR, NODES), 0) == row).astype(F32)
    acc = [jnp.zeros((CR, NODES), F32) for _ in range(3)]
    copies = []
    for t in range(TD):
        fix = corrections(rad, edge_ref, halo_ref, jrb_ref, jce_ref, dis_ref, t)
        for f in range(NF):
            for q in range(LT):
                psi_ref[t * NF + f, :, lanes(q)] = base_ref[t * NF + f, :, lanes(q)] - step_ref[:, lanes(q)] * fix(f, q)
        tf = pl.ds(t * NF, NF)
        copies.append(pltpu.make_async_copy(psi_ref.at[tf], out_hbm.at[tf], sem.at[t]))
        copies[t].start()
    for t in range(TD):
        whole = psi_ref[t * NF:(t + 1) * NF].reshape(NF * CR, CT)
        high = whole.astype(BF)
        low = (whole - high.astype(F32)).astype(BF)
        both = jnp.dot(jnp.concatenate([high, low], axis=0), pick, preferred_element_type=F32)
        value = both[:NF * CR] + both[NF * CR:]
        for f in range(NF):
            here = value[f * CR:(f + 1) * CR]
            for k in range(3):
                weight = sd_ref[t * NF + f, k:k + 1, :].astype(F32)
                acc[k] = acc[k] + here * weight
    owner = ids_ref[2:3]
    parts = []
    for k in range(3):
        kept = acc[k] * mask
        for s in range(2):
            parts.append(kept * (owner == s).astype(F32))
    stack = jnp.concatenate(parts, axis=0)
    high = stack.astype(BF)
    low = (stack - high.astype(F32)).astype(BF)
    label = (lax.broadcasted_iota(jnp.int32, (128, NODES), 0) % VAR_DEV == ids_ref[3:4]).astype(F32).astype(BF)
    dims = (((1,), (1,)), ((), ()))
    total = lax.dot_general(high, label, dims, preferred_element_type=F32) + lax.dot_general(
        low, label, dims, preferred_element_type=F32)
    lane = lax.broadcasted_iota(jnp.int32, (1, 128), 1)
    line = []
    for s in range(2):
        full = jnp.zeros((1, 128), F32)
        for k in range(3):
            at = (k * 2 + s) * CR
            part = jnp.sum(total[at:at + CR], axis=0, keepdims=True)
            full = jnp.where(lane // VAR_DEV == k, part, full)
        line.append(full)
    peer = lax.broadcasted_iota(jnp.int32, (128, 128), 0)
    sens_ref[...] = jnp.where((peer // 2) % 2 == 0, line[0], line[1])
    for copy in copies:
        copy.wait()


VM, SM, HM = pltpu.VMEM, pltpu.SMEM, pltpu.HBM


def call(kernel, ins, outs, scratch=(), micros=1):
    return pl.pallas_call(
        kernel,
        out_shape=[shape for shape, _ in outs],
        in_specs=[pl.BlockSpec(memory_space=space) for space in ins],
        out_specs=[pl.BlockSpec(memory_space=space) for _, space in outs],
        scratch_shapes=list(scratch),
        cost_estimate=pl.CostEstimate(flops=0, bytes_accessed=int(micros * 3.0e6), transcendentals=0),
        compiler_params=pltpu.CompilerParams(vmem_limit_bytes=24 * 1024 * 1024),
    )


def f32(*shape):
    return jax.ShapeDtypeStruct(shape, F32)


def swap_halos(edge, halo):
    halo = lax.ppermute(halo, "rad", SWAP)
    edge = lax.ppermute(edge, "span", SWAP)
    return edge, halo


def body(adjoint_start, jac_rad, jac_circ, dissip, pseudo_step, source, node_cell, node_owner, node_local, shape_deriv):
    me = lax.axis_index("inst").astype(jnp.int32).reshape(1)
    rad = lax.axis_index("rad").astype(jnp.int32).reshape(1)
    n = TD * NF
    psi0 = adjoint_start.reshape(n, CR, CT)
    src = source.reshape(n, CR, CT)
    full = f32(n, CR, CT)
    line = (1, NODES)
    flat = f32(CR, CT)
    edges = [(f32(TD, CR, 128), VM), (f32(2 * n, CT), VM)]
    dma = pltpu.SemaphoreType.DMA
    pad = VM((NF * 32, 128), F32)
    held = [pltpu.with_memory_space_constraint(a, pltpu.HBM) for a in (
        dissip, pseudo_step, node_cell.reshape(line), node_owner.reshape(line), node_local.reshape(line), psi0, src, jac_rad, jac_circ)]
    edge, halo = call(edge_kernel, [SM, HM], edges,
                      [VM((n, 8, CT), F32), VM((n, CR, 128), F32), VM((n, CR, 128), F32), dma((3,))])(rad, held[5])
    edge, halo = swap_halos(edge, halo)
    part, psi, jrb, jce, dis, step, sig, ids = call(
        first_kernel, [SM, SM] + [HM] * 9,
        [(full, VM), (full, VM), (f32(n, NF, CT), VM), (jax.ShapeDtypeStruct((n, NF, CR, 128), BF), VM), (flat, VM), (flat, VM),
         (f32(2, 128), VM), (jax.ShapeDtypeStruct((8, NODES), jnp.int32), VM)],
        [VM((n, CR, CT), F32), VM(jac_rad.shape, BF), VM(jac_circ.shape, BF), pad] + [VM(line, jnp.int32)] * 3 + [dma((TD, 4)), dma((5,))],
        micros=3)(rad, me, *held)
    x, w = call(send_kernel, [SM] + [VM] * 8, [(f32(32 * ROWS, 128), VM), (full, VM)])(
        rad, psi, part, edge, halo, jrb, jce, dis, step)
    y = lax.all_to_all(x, "inst", 0, 0, tiled=True)
    v, = call(time_kernel, [VM] * 3, [(f32(32 * ROWS, 128), VM)])(jnp.asarray(spectral_blocks()), sig, y)
    u = lax.all_to_all(v, "inst", 0, 0, tiled=True)
    edge, halo = call(rim_kernel, [SM] + [VM] * 3, edges)(rad, w, u, step)
    edge, halo = swap_halos(edge, halo)
    base, pick = call(
        middle_kernel, [VM] * 8, [(full, VM), (jax.ShapeDtypeStruct((CT, NODES), BF), VM)], [VM((n, CR, CT), F32), pad],
        micros=3)(w, u, jac_rad, jac_circ, dis, step, src, ids)
    psi2, parts = call(last_kernel, [SM] + [VM] * 10, [(full, HM), (f32(128, 128), VM)], [VM((n, CR, CT), F32), dma((TD,))])(
        rad, base, edge, halo, jrb, jce, dis, step, pick, ids, shape_deriv.reshape(n, 3, NODES))
    got = lax.all_to_all(parts, ALL, 0, 0, tiled=True)
    sens = jnp.sum(got, axis=0)[:3 * VAR_DEV].reshape(3, VAR_DEV)
    return psi2.reshape(TD, NF, CR, CT), sens


def solution(mesh):
    in_specs = (
        P("inst", None, "rad", "span"),
        P("inst", None, None, "rad", "span"),
        P("inst", None, None, "rad", "span"),
        P("rad", "span"),
        P("rad", "span"),
        P("inst", None, "rad", "span"),
        P(("span", "rad")),
        P(("span", "rad"), None),
        P(("span", "rad")),
        P("inst", None, None, ("span", "rad")),
    )
    out_specs = (P("inst", None, "rad", "span"), P(None, "span"))
    return jax.shard_map(body, mesh=mesh, in_specs=in_specs, out_specs=out_specs, check_vma=False)
```

time: 80.2 us -> 71.1 us (0.89)
  blocking collectives: 30.9 us -> 57 us
  waiting for transfers between devices: 20.9 us -> 1.71 us
  starting transfers between devices: 13.4 us -> 2.01 us
  local copies, waits for them, and re-layouts: 4.71 us -> 1.38 us
  other arithmetic: 2.17 us -> 0.15 us
  Pallas kernels: 6.02 us -> 7 us
    all_to_all x0 -> x1, blocking collectives: none -> 26.1 us  [body(): y = lax.all_to_all(x, 'inst', 0, 0, tiled=True)]
    all_to_all x1 -> x0, waiting for transfers between devices: 14.9 us -> none  [body(): y = lax.all_to_all(x, 'inst', 0, 0, tiled=True)]
    all_to_all x1 -> x0, starting transfers between devices: 10.9 us -> none  [body(): y = lax.all_to_all(x, 'inst', 0, 0, tiled=True)]
    ppermute x4, waiting for transfers between devices: 5.98 us -> 1.71 us  [the longest x2 1.7 us: swap_halos(): halo = lax.ppermute(halo, 'rad', SWAP)]
    unnamed x27 -> x11, local copies, waits for them, and re-layouts: 4.01 us -> 0.72 us
    select_n x2 -> x0, other arithmetic: 2.01 us -> none  [the longest x1 1.02 us: body(): halo = jnp.where(rad == 0, psi0[:, 14:16], psi0[:, 0:2]).reshape(2 * n, CT)]
    pallas_call x4 -> x7, Pallas kernels: 6.02 us -> 7 us  [the longest x1 2.5 us: body(): call(first_kernel, [SM, SM] + [HM] * 9, [(full, VM), (full, VM), (f32(n,...]
  transfers between devices with their start and end apart: 5 -> 4, of which waited for: 3 -> 1; matrix products, arithmetic and copies ran while one was open for 1% -> 0% of each run, Pallas kernels for 0% -> 6%
where the time goes in v2:
time: 71.1 us; the launch traced here: 70 us
  blocking collectives  57 us (80%)
  Pallas kernels  7 us (10%)
  starting transfers between devices  2.01 us (3%)
  waiting for transfers between devices  1.71 us (2%)
  local copies, waits for them, and re-layouts  1.38 us (2%)
  between operations  0.74 us (1%)
    all_to_all x1, blocking collectives, body(): y = lax.all_to_all(x, 'inst', 0, 0, tiled=True)  26.1 us
    all_to_all x1, blocking collectives, body(): u = lax.all_to_all(v, 'inst', 0, 0, tiled=True)  17.7 us
    all_to_all x1, blocking collectives, body(): got = lax.all_to_all(parts, ALL, 0, 0, tiled=True)  13.3 us
    pallas_call x1, Pallas kernels, body(): call(first_kernel, [SM, SM] + [HM] * 9, [(full, VM), (full, VM), (f32(n,...  2.5 us
    ppermute x2, starting transfers between devices, swap_halos(): halo = lax.ppermute(halo, 'rad', SWAP)  2 us
    ppermute x2, waiting for transfers between devices, swap_halos(): halo = lax.ppermute(halo, 'rad', SWAP)  1.7 us
  transfers between devices with their start and end apart: 4, of which 1 were waited for; matrix products, arithmetic and copies ran while one was open for 0% of the time, Pallas kernels for 6%

profile of v2, /device:TPU:0, one launch (start us, length us, event | category | flops | bytes accessed | tf_op | source)
XLA Modules:
  0.0 70.0 jit_solution(16644963994832275180)
XLA Ops:
  0.6 1.1 %shard_map.123 = (f32[2,16,128]{2,1,0:T(8,128)S(1)}, f32[20,512]{1,0:T(8,128)S(1)}) custom-call(s32[1]{0:T(128)} %bitcast.rad_ref, f32[10,16,512]{2,1,0:T(8,128)} %bitcast.26), custom_call_target="tpu_custom_call" | custom-call | bytes 3000000 | tf_op jit(solution)/shard_map/pallas_call | solution.py:398
  1.8 1.7 %collective-permute-start.1 = (f32[20,512]{1,0:T(8,128)S(1)}, f32[20,512]{1,0:T(8,128)S(1)}, u32[]{:S(2)}, u32[]{:S(2)}) collective-permute-start(f32[20,512]{1,0:T(8,128)S(1)} %get-tuple-element.23), channel_id=1, source_target_pairs={{0,1},{1,0},{2,3},{3,2},{4,5},{5,4},{6,7},{7,6},{8,9},{9,8},{10,11... | collective-permute-start | bytes 122888 | tf_op jit(solution)/shard_map/ppermute | solution.py:379
  3.4 0.0 collective-permute-start
  3.4 2.5 %shard_map.122 = (f32[10,16,512]{2,1,0:T(8,128)S(1)}, f32[10,16,512]{2,1,0:T(8,128)S(1)}, f32[10,5,512]{2,1,0:T(8,128)S(1)}, bf16[10,5,16,128]{3,2,1,0:T(8,128)(...) custom-call(s32[1]{0:T(128)} %bitcast.rad_ref, ...), custom_call_target="tpu_custom_call" | custom-call | bytes 9000000 | tf_op jit(solution)/shard_map/pallas_call | solution.py:401
  5.9 0.0 collective-permute-done.edge_ref
  5.9 0.0 collective-permute-done.1.halo_ref
  6.0 0.3 shard_map.124
  6.2 0.0 copy-start.3
  6.3 26.1 %all_to_all.31 = f32[32,40,128]{2,1,0:T(8,128)S(1)} all-to-all(f32[32,40,128]{2,1,0:T(8,128)S(1)} %bitcast.23), channel_id=1, replica_groups=mesh['inst'=32,'span'=2,'rad'=2] {'inst'}, dimensions={0} | all-to-all | bytes 1310720 | tf_op jit(solution)/shard_map/all_to_all | solution.py:409
  32.4 0.0 copy-done.3
  32.4 0.4 shard_map.125
  32.8 0.0 copy-start.4
  32.8 0.0 copy-start.1
  32.8 17.7 %all_to_all.32 = f32[32,40,128]{2,1,0:T(8,128)S(1)} all-to-all(f32[32,40,128]{2,1,0:T(8,128)S(1)} %bitcast.20), channel_id=1, replica_groups=mesh['inst'=32,'span'=2,'rad'=2] {'inst'}, dimensions={0} | all-to-all | bytes 1310720 | tf_op jit(solution)/shard_map/all_to_all | solution.py:411
  50.5 0.0 copy-start
  50.5 0.0 copy-start.2
  50.5 0.1 shard_map.127
  50.6 0.3 collective-permute-start.3
  51.0 0.0 collective-permute-start.2
  51.0 0.0 copy-done.4
  51.0 0.0 copy-done.1
  51.0 0.6 copy-done
  51.6 0.1 copy-done.2
  51.7 1.4 %shard_map.126 = (f32[10,16,512]{2,1,0:T(8,128)S(1)}, bf16[512,1024]{1,0:T(8,128)(2,1)S(1)}) custom-call(f32[10,16,512]{2,1,0:T(8,128)S(1)} %get-tuple-element.28.w_ref, f32[1280,128]{1,0:T(8,128)S(1)} %bitcast.18, bf16[2,5,5,16,512]{4,3,2,1,0:T(8,128)(2,1)S(1)} %copy-done, bf16[2,5,5,16,512]{4,3,2,1,0:T(8,128)(2,1)S(1)} %copy-done.1, ...), custom_call_target="tpu_custom_call" | custom-call | bytes 9000000 | tf_op jit(solution)/shard_map/pallas_call | solution.py:414
  53.1 0.0 collective-permute-done.2.edge_ref
  53.1 1.7 %collective-permute-done.3.halo_ref = f32[20,512]{1,0:T(8,128)S(1)} collective-permute-done((f32[20,512]{1,0:T(8,128)S(1)}, f32[20,512]{1,0:T(8,128)S(1)}, u32[]{:S(2)}, u32[]{:S(2)}) %collective-permute-start.3) | collective-permute-done | bytes 40992 | tf_op jit(solution)/shard_map/ppermute | solution.py:379
  54.8 1.1 %shard_map.128 = (f32[10,16,512]{2,1,0:T(8,128)}, f32[128,128]{1,0:T(8,128)S(1)}) custom-call(s32[1]{0:T(128)} %bitcast.rad_ref, f32[10,16,512]{2,1,0:T(8,128)S(1)} %get-tuple-element.32.base_ref, f32[2,16,128]{2,1,0:T(8,128)S(1)} %collective-permute-done.2.edge_ref, f32[20,512]{1,0:T(8,128)S(1)} %collective-permute-done.3.halo_ref, ...), custom_call_target="tpu_custom_call" | custom-call | bytes 3000000 | tf_op jit(solution)/shard_map/pallas_call | solution.py:417
  56.0 13.3 %all_to_all.33 = f32[128,1,128]{2,1,0:T(1,128)S(1)} all-to-all(f32[128,1,128]{2,1,0:T(1,128)S(1)} %bitcast.25), channel_id=1, replica_groups=mesh['inst'=32,'span'=2,'rad'=2] {'inst','span','rad'}, dimensions={0} | all-to-all | bytes 131072 | tf_op jit(solution)/shard_map/all_to_all | solution.py:419
  69.2 0.2 reduce_sum.9
  69.4 0.7 reshape.57
  (1 shorter events, 0.0 us)
Async XLA Ops:
  1.8 4.2 %collective-permute-start.1 = (f32[20,512]{1,0:T(8,128)S(1)}, f32[20,512]{1,0:T(8,128)S(1)}, u32[]{:S(2)}, u32[]{:S(2)}) collective-permute-start(f32[20,512]{1,0:T(8,128)S(1)} %get-tuple-element.23), channel_id=1, source_target_pairs={{0,1},{1,0},{2,3},{3,2},{4,5},{5,4},{6,7},{7,6},{8,9},{9,8},{10,11... | collective-permute-start | bytes 122888 | tf_op jit(solution)/shard_map/ppermute | solution.py:379
  3.4 2.5 %collective-permute-start = (f32[2,16,128]{2,1,0:T(8,128)S(1)}, f32[2,16,128]{2,1,0:T(8,128)S(1)}, u32[]{:S(2)}, u32[]{:S(2)}) collective-permute-start(f32[2,16,128]{2,1,0:T(8,128)S(1)} %get-tuple-element.22), channel_id=1, source_target_pairs={{0,2},{2,0},{1,3},{3,1},{4,6},{6,4},{5,7},{7,5},{8,10},{10,8},{9,1... | collective-permute-start | bytes 49160 | tf_op jit(solution)/shard_map/ppermute | solution.py:380
  6.2 26.1 %copy-start.3 = (bf16[64,192]{1,0:T(8,128)(2,1)S(1)}, bf16[64,192]{1,0:T(8,128)(2,1)}, u32[]{:S(2)}) copy-start(bf16[64,192]{1,0:T(8,128)(2,1)} %constant.14.clone.table_ref) | copy-start | bytes 73732
  32.8 18.2 %copy-start.4 = (bf16[2,5,3,1024]{3,0,2,1:T(2,128)(2,1)S(1)}, bf16[2,5,3,1024]{3,0,2,1:T(2,128)(2,1)}, u32[]{:S(2)}) copy-start(bf16[2,5,3,1024]{3,0,2,1:T(2,128)(2,1)} %param.20) | copy-start | bytes 184324
  32.8 18.2 %copy-start.1 = (bf16[2,5,5,16,512]{4,3,2,1,0:T(8,128)(2,1)S(1)}, bf16[2,5,5,16,512]{4,3,2,1,0:T(8,128)(2,1)}, u32[]{:S(2)}) copy-start(bf16[2,5,5,16,512]{4,3,2,1,0:T(8,128)(2,1)} %jc_ref.1) | copy-start | bytes 2457604
  50.5 1.1 %copy-start = (bf16[2,5,5,16,512]{4,3,2,1,0:T(8,128)(2,1)S(1)}, bf16[2,5,5,16,512]{4,3,2,1,0:T(8,128)(2,1)}, u32[]{:S(2)}) copy-start(bf16[2,5,5,16,512]{4,3,2,1,0:T(8,128)(2,1)} %jr_ref.1) | copy-start | bytes 2457604
  50.5 1.2 %copy-start.2 = (f32[2,5,16,512]{3,2,1,0:T(8,128)S(1)}, f32[2,5,16,512]{3,2,1,0:T(8,128)}, u32[]{:S(2)}) copy-start(f32[2,5,16,512]{3,2,1,0:T(8,128)} %param.16) | copy-start | bytes 983044
  50.6 4.2 %collective-permute-start.3 = (f32[20,512]{1,0:T(8,128)S(1)}, f32[20,512]{1,0:T(8,128)S(1)}, u32[]{:S(2)}, u32[]{:S(2)}) collective-permute-start(f32[20,512]{1,0:T(8,128)S(1)} %get-tuple-element.34), channel_id=1, source_target_pairs={{0,1},{1,0},{2,3},{3,2},{4,5},{5,4},{6,7},{7,6},{8,9},{9,8},{10,11... | collective-permute-start | bytes 122888 | tf_op jit(solution)/shard_map/ppermute | solution.py:379
  51.0 2.1 %collective-permute-start.2 = (f32[2,16,128]{2,1,0:T(8,128)S(1)}, f32[2,16,128]{2,1,0:T(8,128)S(1)}, u32[]{:S(2)}, u32[]{:S(2)}) collective-permute-start(f32[2,16,128]{2,1,0:T(8,128)S(1)} %get-tuple-element.33), channel_id=1, source_target_pairs={{0,2},{2,0},{1,3},{3,1},{4,6},{6,4},{5,7},{7,5},{8,10},{10,8},{9,1... | collective-permute-start | bytes 49160 | tf_op jit(solution)/shard_map/ppermute | solution.py:380

commit v3 on v2

--- a/solution.py
+++ b/solution.py
@@ -13,7 +13,8 @@
 CT = 512
 LT = 4
 HB = 2
-ROWS = 40
+BODY = 40
+ROWS = 44
 GRP = 8 * ROWS
 NODES = 1024
 VAR_DEV = 32
@@ -124,35 +125,44 @@
     return fix
 
 
-def edge_kernel(rad_ref, psi_hbm, edge_ref, halo_ref, rows_ref, left_ref, right_ref, sem):
+def edge_kernel(rad_ref, psi_hbm, step_hbm, edge_ref, halo_ref, rows_ref, left_ref, right_ref, step_ref, sem):
     rad = rad_ref[0]
     start = pl.multiple_of(8 * (1 - rad), 8)
     copies = [
         pltpu.make_async_copy(psi_hbm.at[:, pl.ds(start, 8), :], rows_ref, sem.at[0]),
         pltpu.make_async_copy(psi_hbm.at[:, :, pl.ds(0, 128)], left_ref, sem.at[1]),
         pltpu.make_async_copy(psi_hbm.at[:, :, pl.ds(CT - 128, 128)], right_ref, sem.at[2]),
+        pltpu.make_async_copy(step_hbm, step_ref, sem.at[3]),
     ]
     for copy in copies:
         copy.start()
     copies[0].wait()
+    copies[3].wait()
     put_halo(halo_ref, lambda tf: rows_ref[tf], rad)
+    halo_ref[20:22] = jnp.where(rad == 0, step_ref[CR - 2:CR], step_ref[0:2])
+    halo_ref[22:24] = jnp.zeros((2, CT), F32)
     copies[1].wait()
     copies[2].wait()
     put_edge(edge_ref, lambda tf: (left_ref[tf], right_ref[tf]))
+    ends = (step_ref[:, lanes(0)], step_ref[:, lanes(LT - 1)])
+    edge_ref[TD] = pack_edge([ends] * NF)
+
+
+def pack_edge(ends):
+    lane = lax.broadcasted_iota(jnp.int32, (CR, 128), 1)
+    packed = None
+    for f in range(NF):
+        both = jnp.where(lane < 64, ends[f][0], ends[f][1])
+        if f == 0:
+            packed = both
+        else:
+            packed = jnp.where((lane >= 4 * f - 2) & (lane < 4 * f + 2), pltpu.roll(both, 4 * f, 1), packed)
+    return packed
 
 
 def put_edge(edge_ref, ends):
-    lane = lax.broadcasted_iota(jnp.int32, (CR, 128), 1)
-    for t in range(TD):
-        packed = None
-        for f in range(NF):
-            left, right = ends(t * NF + f)
-            both = jnp.where(lane < 64, left, right)
-            if f == 0:
-                packed = both
-            else:
-                packed = jnp.where((lane >= 4 * f - 2) & (lane < 4 * f + 2), pltpu.roll(both, 4 * f, 1), packed)
-        edge_ref[t] = packed
+    for t in range(TD):
+        edge_ref[t] = pack_edge([ends(t * NF + f) for f in range(NF)])
 
 
 def put_halo(halo_ref, tile, rad):
@@ -216,21 +226,51 @@
                     lane < 64, jc_ref[t, i, j, :, lanes(0)].astype(F32), jc_ref[t, i, j, :, lanes(LT - 1)].astype(F32)).astype(BF)
 
 
-def send_kernel(rad_ref, psi_ref, part_ref, edge_ref, halo_ref, jrb_ref, jce_ref, dis_ref, step_ref, x_ref, w_ref):
+def send_kernel(rad_ref, psi_ref, part_ref, edge_ref, halo_ref, jrb_ref, jce_ref, dis_ref, step_ref, x_hbm, w_ref, w_edge_ref,
+                w_halo_ref, rim_ref, x_ref, sem):
     rad = rad_ref[0]
-    for t in range(TD):
-        fix = corrections(rad, edge_ref, halo_ref, jrb_ref, jce_ref, dis_ref, t)
-        for f in range(NF):
-            for q in range(LT):
+    fixes = [corrections(rad, edge_ref, halo_ref, jrb_ref, jce_ref, dis_ref, t) for t in range(TD)]
+    for t in range(TD):
+        for q in range(LT):
+            rim_ref[10 * q:10 * q + 10] = halo_ref[10 * t:10 * t + 10, lanes(q)]
+        rim_ref[40:56] = edge_ref[t]
+        rim_ref[56:64] = jnp.zeros((8, 128), F32)
+        for e in range(2):
+            x_ref[pl.ds(BODY + 2 * t + e, 32, stride=ROWS), :] = rim_ref[pl.ds(e, 32, stride=2), :]
+    copies = []
+    for q in range(LT):
+        for t in range(TD):
+            for f in range(NF):
                 mid = psi_ref[t * NF + f, :, lanes(q)]
-                w = part_ref[t * NF + f, :, lanes(q)] - step_ref[:, lanes(q)] * fix(f, q)
+                w = part_ref[t * NF + f, :, lanes(q)] - step_ref[:, lanes(q)] * fixes[t](f, q)
                 w_ref[t * NF + f, :, lanes(q)] = w
                 for h in range(HB):
                     x_ref[pl.ds(q * GRP + row_of(t, 0, f, h), 8, stride=ROWS), :] = mid[8 * h:8 * h + 8]
                     x_ref[pl.ds(q * GRP + row_of(t, 1, f, h), 8, stride=ROWS), :] = w[8 * h:8 * h + 8]
-
-
-def time_kernel(table_ref, sig_ref, y_ref, v_ref):
+        span = pl.ds(q * GRP, GRP)
+        copies.append(pltpu.make_async_copy(x_ref.at[span], x_hbm.at[span], sem.at[q]))
+        copies[q].start()
+    put_edge(w_edge_ref, lambda tf: (w_ref[tf, :, lanes(0)], w_ref[tf, :, lanes(LT - 1)]))
+    start = pl.multiple_of(8 * (1 - rad), 8)
+    put_halo(w_halo_ref, lambda tf: w_ref[tf, pl.ds(start, 8), :], rad)
+    for copy in copies:
+        copy.wait()
+
+
+def label_kernel(ids_ref, pick_ref, label_ref):
+    pick_ref[...] = (lax.broadcasted_iota(jnp.int32, (CT, NODES), 0) == ids_ref[0:1]).astype(F32).astype(BF)
+    label_ref[...] = (lax.broadcasted_iota(jnp.int32, (128, NODES), 0) % VAR_DEV == ids_ref[3:4]).astype(F32).astype(BF)
+
+
+def total_kernel(got_ref, sens_ref):
+    line = jnp.sum(got_ref[...], axis=0, keepdims=True)
+    for k in range(3):
+        sens_ref[k:k + 1, :] = pltpu.roll(line, (128 - VAR_DEV * k) % 128, 1)[:, :VAR_DEV]
+
+
+def time_kernel(table_ref, sig_ref, y_ref, edge_ref, halo_ref, pick_ref, label_ref, v_ref, edge_out_ref, halo_out_ref):
+    edge_out_ref[...] = edge_ref[...]
+    halo_out_ref[...] = halo_ref[...]
     table = table_ref[...]
 
     def apply(x):
@@ -238,85 +278,69 @@
         low = (x - high.astype(F32)).astype(BF)
         return jnp.dot(table, jnp.concatenate([high, low, high], axis=0), preferred_element_type=F32)
 
-    def gather(what):
-        cols = []
-        for f in range(NF):
-            for h in range(HB):
-                cols.append(jnp.concatenate(
-                    [y_ref[pl.ds(row_of(t, what, f, h), 32, stride=ROWS), :] for t in range(TD)], axis=0))
-        return jnp.concatenate(cols, axis=1)
-
-    def scatter(what, value):
-        for f in range(NF):
-            for h in range(HB):
-                for t in range(TD):
-                    v_ref[pl.ds(row_of(t, what, f, h), 32, stride=ROWS), :] = value[32 * t:32 * t + 32, lanes(f * HB + h)]
-
+    def row(what, m, t):
+        if m < 2 * NF:
+            return (t * 2 + what) * 2 * NF + m
+        return BODY + 2 * t + m - 2 * NF
+
+    def gather(what, count):
+        return jnp.concatenate([jnp.concatenate(
+            [y_ref[pl.ds(row(what, m, t), 32, stride=ROWS), :] for t in range(TD)], axis=0) for m in range(count)], axis=1)
+
+    def scatter(what, value, count):
+        for m in range(count):
+            for t in range(TD):
+                v_ref[pl.ds(row(what, m, t), 32, stride=ROWS), :] = value[32 * t:32 * t + 32, lanes(m)]
+
+    count = 2 * NF
     sigma = jnp.concatenate([sig_ref[0:1, :], sig_ref[1:2, :]] * NF, axis=1)
-    time0 = apply(gather(0))
-    scatter(0, time0)
-    psi1 = gather(1) - sigma * time0
-    scatter(1, apply(psi1))
+    time0 = apply(gather(0, count + 2))
+    scatter(0, time0, count + 2)
+    psi1 = gather(1, count) - sigma * time0[:, :128 * count]
+    scatter(1, apply(psi1), count)
 
 
 def plane(ref, what, t, f, q):
     return jnp.concatenate([ref[pl.ds(q * GRP + row_of(t, what, f, h), 8, stride=ROWS), :] for h in range(HB)], axis=0)
 
 
-def rim_kernel(rad_ref, w_ref, u_ref, step_ref, edge_ref, halo_ref):
+def last_kernel(rad_ref, w_ref, u_ref, w_edge_ref, w_halo_ref, edge0_ref, halo0_ref, jr_ref, jc_ref, jrb_ref, jce_ref, dis_ref,
+                step_ref, src_ref, ids_ref, pick_ref, label_ref, sd_ref, out_hbm, sens_ref, psi1_ref, psi_ref, edge_ref, halo_ref, rim_ref, pad_ref, sem):
     rad = rad_ref[0]
-
-    def ends(tf):
-        return [w_ref[tf, :, lanes(q)] - step_ref[:, lanes(q)] * plane(u_ref, 0, tf // NF, tf % NF, q) for q in (0, LT - 1)]
-
-    put_edge(edge_ref, ends)
-    start = pl.multiple_of(8 * (1 - rad), 8)
-
-    def rows(tf):
-        t, f = tf // NF, tf % NF
-        time = jnp.concatenate(
-            [u_ref[pl.ds(q * GRP + row_of(t, 0, f, 0) + (1 - rad), 8, stride=ROWS), :] for q in range(LT)], axis=1)
-        return w_ref[tf, pl.ds(start, 8), :] - step_ref[pl.ds(start, 8), :] * time
-
-    put_halo(halo_ref, rows, rad)
-
-
-def middle_kernel(w_ref, u_ref, jr_ref, jc_ref, dis_ref, step_ref, src_ref, ids_ref, base_ref, pick_ref, psi_ref, pad_ref):
     clear_pad(pad_ref)
     for t in range(TD):
+        for e in range(2):
+            rim_ref[pl.ds(e, 32, stride=2), :] = u_ref[pl.ds(BODY + 2 * t + e, 32, stride=ROWS), :]
+        for m in range(2):
+            at = (2 * t + m) * NF
+            for q in range(LT):
+                halo_ref[at:at + NF, lanes(q)] = (
+                    w_halo_ref[at:at + NF, lanes(q)]
+                    - halo0_ref[20 + m:21 + m, lanes(q)] * rim_ref[10 * q + NF * m:10 * q + NF * m + NF])
+        edge_ref[t] = w_edge_ref[t] - edge0_ref[TD] * rim_ref[40:56]
+    copies = []
+    for t in range(TD):
+        fix = corrections(rad, edge_ref, halo_ref, jrb_ref, jce_ref, dis_ref, t)
         for f in range(NF):
             for q in range(LT):
-                psi_ref[t * NF + f, :, lanes(q)] = (
+                psi1_ref[t * NF + f, :, lanes(q)] = (
                     w_ref[t * NF + f, :, lanes(q)] - step_ref[:, lanes(q)] * plane(u_ref, 0, t, f, q))
         for q in range(LT):
-            cell = lambda f, qq: psi_ref[t * NF + f, :, lanes(qq)]
+            cell = lambda f, qq: psi1_ref[t * NF + f, :, lanes(qq)]
             jr = lambda i, j: jr_ref[t, i, j, :, lanes(q)]
             jc = lambda i, j: jc_ref[t, i, j, :, lanes(q)]
             res = interior(cell, pad_ref, jr, jc, dis_ref[:, lanes(q)], q)
             sigma = step_ref[:, lanes(q)]
             for f in range(NF):
-                base_ref[t * NF + f, :, lanes(q)] = cell(f, q) - sigma * (
-                    res[f] + plane(u_ref, 1, t, f, q) - src_ref[t * NF + f, :, lanes(q)])
-    col = ids_ref[0:1]
-    pick_ref[...] = (lax.broadcasted_iota(jnp.int32, (CT, NODES), 0) == col).astype(F32).astype(BF)
-
-
-def last_kernel(rad_ref, base_ref, edge_ref, halo_ref, jrb_ref, jce_ref, dis_ref, step_ref, pick_ref, ids_ref, sd_ref,
-                 out_hbm, sens_ref, psi_ref, sem):
-    rad = rad_ref[0]
-    row = ids_ref[1:2]
-    pick = pick_ref[...]
-    mask = (lax.broadcasted_iota(jnp.int32, (CR, NODES), 0) == row).astype(F32)
-    acc = [jnp.zeros((CR, NODES), F32) for _ in range(3)]
-    copies = []
-    for t in range(TD):
-        fix = corrections(rad, edge_ref, halo_ref, jrb_ref, jce_ref, dis_ref, t)
-        for f in range(NF):
-            for q in range(LT):
-                psi_ref[t * NF + f, :, lanes(q)] = base_ref[t * NF + f, :, lanes(q)] - step_ref[:, lanes(q)] * fix(f, q)
+                psi_ref[t * NF + f, :, lanes(q)] = cell(f, q) - sigma * (
+                    res[f] + fix(f, q) + plane(u_ref, 1, t, f, q) - src_ref[t * NF + f, :, lanes(q)])
         tf = pl.ds(t * NF, NF)
         copies.append(pltpu.make_async_copy(psi_ref.at[tf], out_hbm.at[tf], sem.at[t]))
         copies[t].start()
+    pick = pick_ref[...]
+    mask = (lax.broadcasted_iota(jnp.int32, (CR, NODES), 0) == ids_ref[1:2]).astype(F32)
+    acc = [jnp.zeros((CR, NODES), F32) for _ in range(3)]
+    weights = [sd_ref[m].astype(F32) for m in range(3 * NF)]
     for t in range(TD):
         whole = psi_ref[t * NF:(t + 1) * NF].reshape(NF * CR, CT)
         high = whole.astype(BF)
@@ -326,8 +350,7 @@
         for f in range(NF):
             here = value[f * CR:(f + 1) * CR]
             for k in range(3):
-                weight = sd_ref[t * NF + f, k:k + 1, :].astype(F32)
-                acc[k] = acc[k] + here * weight
+                acc[k] = acc[k] + here * weights[3 * f + k][t:t + 1]
     owner = ids_ref[2:3]
     parts = []
     for k in range(3):
@@ -337,7 +360,7 @@
     stack = jnp.concatenate(parts, axis=0)
     high = stack.astype(BF)
     low = (stack - high.astype(F32)).astype(BF)
-    label = (lax.broadcasted_iota(jnp.int32, (128, NODES), 0) % VAR_DEV == ids_ref[3:4]).astype(F32).astype(BF)
+    label = label_ref[...]
     dims = (((1,), (1,)), ((), ()))
     total = lax.dot_general(high, label, dims, preferred_element_type=F32) + lax.dot_general(
         low, label, dims, preferred_element_type=F32)
@@ -390,34 +413,40 @@
     full = f32(n, CR, CT)
     line = (1, NODES)
     flat = f32(CR, CT)
-    edges = [(f32(TD, CR, 128), VM), (f32(2 * n, CT), VM)]
     dma = pltpu.SemaphoreType.DMA
     pad = VM((NF * 32, 128), F32)
     held = [pltpu.with_memory_space_constraint(a, pltpu.HBM) for a in (
         dissip, pseudo_step, node_cell.reshape(line), node_owner.reshape(line), node_local.reshape(line), psi0, src, jac_rad, jac_circ)]
-    edge, halo = call(edge_kernel, [SM, HM], edges,
-                      [VM((n, 8, CT), F32), VM((n, CR, 128), F32), VM((n, CR, 128), F32), dma((3,))])(rad, held[5])
-    edge, halo = swap_halos(edge, halo)
+    edge0, halo0 = call(
+        edge_kernel, [SM, HM, HM], [(f32(TD + 1, CR, 128), VM), (f32(24, CT), VM)],
+        [VM((n, 8, CT), F32), VM((n, CR, 128), F32), VM((n, CR, 128), F32), VM((CR, CT), F32), dma((4,))])(rad, held[5], held[1])
+    edge0, halo0 = swap_halos(edge0, halo0)
     part, psi, jrb, jce, dis, step, sig, ids = call(
         first_kernel, [SM, SM] + [HM] * 9,
         [(full, VM), (full, VM), (f32(n, NF, CT), VM), (jax.ShapeDtypeStruct((n, NF, CR, 128), BF), VM), (flat, VM), (flat, VM),
          (f32(2, 128), VM), (jax.ShapeDtypeStruct((8, NODES), jnp.int32), VM)],
         [VM((n, CR, CT), F32), VM(jac_rad.shape, BF), VM(jac_circ.shape, BF), pad] + [VM(line, jnp.int32)] * 3 + [dma((TD, 4)), dma((5,))],
         micros=3)(rad, me, *held)
-    x, w = call(send_kernel, [SM] + [VM] * 8, [(f32(32 * ROWS, 128), VM), (full, VM)])(
-        rad, psi, part, edge, halo, jrb, jce, dis, step)
-    y = lax.all_to_all(x, "inst", 0, 0, tiled=True)
-    v, = call(time_kernel, [VM] * 3, [(f32(32 * ROWS, 128), VM)])(jnp.asarray(spectral_blocks()), sig, y)
-    u = lax.all_to_all(v, "inst", 0, 0, tiled=True)
-    edge, halo = call(rim_kernel, [SM] + [VM] * 3, edges)(rad, w, u, step)
-    edge, halo = swap_halos(edge, halo)
-    base, pick = call(
-        middle_kernel, [VM] * 8, [(full, VM), (jax.ShapeDtypeStruct((CT, NODES), BF), VM)], [VM((n, CR, CT), F32), pad],
-        micros=3)(w, u, jac_rad, jac_circ, dis, step, src, ids)
-    psi2, parts = call(last_kernel, [SM] + [VM] * 10, [(full, HM), (f32(128, 128), VM)], [VM((n, CR, CT), F32), dma((TD,))])(
-        rad, base, edge, halo, jrb, jce, dis, step, pick, ids, shape_deriv.reshape(n, 3, NODES))
+    rim = VM((64, 128), F32)
+    x, w, w_edge, w_halo = call(
+        send_kernel, [SM] + [VM] * 8, [(f32(32 * ROWS, 128), HM), (full, VM), (f32(TD, CR, 128), VM), (f32(2 * n, CT), VM)],
+        [rim, VM((32 * ROWS, 128), F32), dma((LT,))])(
+        rad, psi, part, edge0, halo0, jrb, jce, dis, step)
+    w_edge, w_halo = swap_halos(w_edge, w_halo)
+    y = lax.all_to_all(x.reshape(32 * ROWS, 1, 128), "inst", 0, 0, tiled=True).reshape(32 * ROWS, 128)
+    bf16 = lambda *shape: (jax.ShapeDtypeStruct(shape, BF), VM)
+    pick, label = call(label_kernel, [VM], [bf16(CT, NODES), bf16(128, NODES)])(ids)
+    v, w_edge, w_halo = call(
+        time_kernel, [VM] * 5 + [pl.ANY] * 2, [(f32(32 * ROWS, 128), VM), (f32(TD, CR, 128), VM), (f32(2 * n, CT), VM)])(
+        jnp.asarray(spectral_blocks()), sig, y, w_edge, w_halo, pick, label)
+    u = lax.all_to_all(v.reshape(32 * ROWS, 1, 128), "inst", 0, 0, tiled=True).reshape(32 * ROWS, 128)
+    psi2, parts = call(
+        last_kernel, [SM] + [VM] * 17, [(full, HM), (f32(128, 128), VM)],
+        [VM((n, CR, CT), F32), VM((n, CR, CT), F32), VM((TD, CR, 128), F32), VM((2 * n, CT), F32), rim, pad, dma((TD,))])(
+        rad, w, u, w_edge, w_halo, edge0, halo0, jac_rad, jac_circ, jrb, jce, dis, step, src, ids, pick, label,
+        shape_deriv.transpose(1, 2, 0, 3).reshape(3 * NF, TD, NODES))
     got = lax.all_to_all(parts, ALL, 0, 0, tiled=True)
-    sens = jnp.sum(got, axis=0)[:3 * VAR_DEV].reshape(3, VAR_DEV)
+    sens, = call(total_kernel, [VM], [(f32(3, VAR_DEV), VM)])(got)
     return psi2.reshape(TD, NF, CR, CT), sens
 
 

time: 71.1 us -> 69.9 us (0.983)
  blocking collectives: 57 us -> 31 us
  waiting for transfers between devices: 1.71 us -> 15.7 us
  starting transfers between devices: 2.01 us -> 13.2 us
  local copies, waits for them, and re-layouts: 1.38 us -> 0.03 us
  Pallas kernels: 7 us -> 8.07 us
    all_to_all x2 -> x1, blocking collectives: 43.8 us -> 17.8 us  [body(): lax.all_to_all(v.reshape(32 * ROWS, 1, 128), 'inst', 0, 0, tiled=True)]
    all_to_all x0 -> x1, starting transfers between devices: none -> 10.9 us  [body(): lax.all_to_all(x.reshape(32 * ROWS, 1, 128), 'inst', 0, 0, tiled=True)]
    all_to_all x0 -> x1, waiting for transfers between devices: none -> 6.99 us  [body(): lax.all_to_all(x.reshape(32 * ROWS, 1, 128), 'inst', 0, 0, tiled=True)]
    ppermute x2, waiting for transfers between devices: 1.7 us -> 7.81 us  [swap_halos(): halo = lax.ppermute(halo, 'rad', SWAP)]
    pallas_call x6, Pallas kernels: 4.5 us -> 5.59 us  [the longest x1 2.02 us: body(): call(last_kernel, [SM] + [VM] * 17, [(full, HM), (f32(128, 128), VM)], [V...]
    ppermute x2, waiting for transfers between devices: 0.01 us -> 0.95 us  [swap_halos(): edge = lax.ppermute(edge, 'span', SWAP)]
  transfers between devices with their start and end apart: 4 -> 5, of which waited for: 1 -> 3; matrix products, arithmetic and copies ran while one was open for 0% -> 0% of each run, Pallas kernels for 6% -> 4%
where the time goes in v3:
time: 69.9 us; the launch traced here: 68.8 us
  blocking collectives  31 us (44%)
  waiting for transfers between devices  15.7 us (22%)
  starting transfers between devices  13.2 us (19%)
  Pallas kernels  8.07 us (12%)
  between operations  0.73 us (1%)
    all_to_all x1, blocking collectives, body(): lax.all_to_all(v.reshape(32 * ROWS, 1, 128), 'inst', 0, 0, tiled=True)  17.8 us
    all_to_all x1, blocking collectives, body(): got = lax.all_to_all(parts, ALL, 0, 0, tiled=True)  13.3 us
    all_to_all x1, starting transfers between devices, body(): lax.all_to_all(x.reshape(32 * ROWS, 1, 128), 'inst', 0, 0, tiled=True)  10.9 us
    ppermute x2, waiting for transfers between devices, swap_halos(): halo = lax.ppermute(halo, 'rad', SWAP)  7.81 us
    all_to_all x1, waiting for transfers between devices, body(): lax.all_to_all(x.reshape(32 * ROWS, 1, 128), 'inst', 0, 0, tiled=True)  6.99 us
    pallas_call x1, Pallas kernels, body(): call(first_kernel, [SM, SM] + [HM] * 9, [(full, VM), (full, VM), (f32(n,...  2.48 us
    ppermute x2, starting transfers between devices, swap_halos(): halo = lax.ppermute(halo, 'rad', SWAP)  2.33 us
    pallas_call x1, Pallas kernels, body(): call(last_kernel, [SM] + [VM] * 17, [(full, HM), (f32(128, 128), VM)], [V...  2.02 us
  transfers between devices with their start and end apart: 5, of which 3 were waited for; matrix products, arithmetic and copies ran while one was open for 0% of the time, Pallas kernels for 4%

profile of v3, /device:TPU:0, one launch (start us, length us, event | category | flops | bytes accessed | tf_op | source)
XLA Modules:
  0.0 68.8 jit_solution(15768191391027619699)
XLA Ops:
  0.6 1.1 %shard_map.123 = (f32[3,16,128]{2,1,0:T(8,128)S(1)}, f32[24,512]{1,0:T(8,128)S(1)}) custom-call(s32[1]{0:T(128)} %bitcast.rad_ref, f32[10,16,512]{2,1,0:T(8,128)} %bitcast.31, f32[16,512]{1,0:T(8,128)} %step_hbm.3), custom_call_target="tpu_custom_call" | custom-call | bytes 3000000 | tf_op jit(solution)/shard_map/pallas_call | solution.py:420
  1.8 1.7 %collective-permute-start.1 = (f32[24,512]{1,0:T(8,128)S(1)}, f32[24,512]{1,0:T(8,128)S(1)}, u32[]{:S(2)}, u32[]{:S(2)}) collective-permute-start(f32[24,512]{1,0:T(8,128)S(1)} %get-tuple-element.26), channel_id=1, source_target_pairs={{0,1},{1,0},{2,3},{3,2},{4,5},{5,4},{6,7},{7,6},{8,9},{9,8},{10,11... | collective-permute-start | bytes 147464 | tf_op jit(solution)/shard_map/ppermute | solution.py:402
  3.4 0.0 collective-permute-start
  3.4 2.5 %shard_map.122 = (f32[10,16,512]{2,1,0:T(8,128)S(1)}, f32[10,16,512]{2,1,0:T(8,128)S(1)}, f32[10,5,512]{2,1,0:T(8,128)S(1)}, bf16[10,5,16,128]{3,2,1,0:T(8,128)(...) custom-call(s32[1]{0:T(128)} %bitcast.rad_ref, ...), custom_call_target="tpu_custom_call" | custom-call | bytes 9000000 | tf_op jit(solution)/shard_map/pallas_call | solution.py:424
  5.9 0.0 collective-permute-done.edge_ref.edge0_ref
  5.9 0.0 collective-permute-done.1.halo_ref.halo0_ref
  6.0 1.2 %shard_map.124 = (f32[1408,128]{1,0:T(8,128)}, f32[10,16,512]{2,1,0:T(8,128)S(1)}, f32[2,16,128]{2,1,0:T(8,128)S(1)}, f32[20,512]{1,0:T(8,128)S(1)}) custom-call(s32[1]{0:T(128)} %bitcast.rad_ref, f32[10,16,512]{2,1,0:T(8,128)S(1)} %get-tuple-element.23.psi_ref, f32[10,16,512]{2,1,0:T(8,128)S(1)} %get-tuple-element.24.part_ref, ...), custom_call_target="tpu_custom_call" | custom-call | bytes 3000000 | tf_op jit(solution)/shard_map/pallas_call | solution.py:431
  7.1 10.9 %all-to-all-start = ((f32[1408,1,128]{2,1,0:T(1,128)}), f32[1408,1,128]{2,1,0:T(1,128)S(1)}, u32[]{:S(2)}, u32[]{:S(2)}) async-start(f32[1408,1,128]{2,1,0:T(1,128)} %bitcast.8), calls=%async_computation | async-start | bytes 1441792 | tf_op jit(solution)/shard_map/all_to_all | solution.py:436
  18.0 0.0 copy-start.4
  18.0 0.7 collective-permute-start.3
  18.7 0.0 collective-permute-start.2
  18.7 0.2 shard_map.125
  18.9 0.9 %collective-permute-done.2.edge_ref = f32[2,16,128]{2,1,0:T(8,128)S(1)} collective-permute-done((f32[2,16,128]{2,1,0:T(8,128)S(1)}, f32[2,16,128]{2,1,0:T(8,128)S(1)}, u32[]{:S(2)}, u32[]{:S(2)}) %collective-permute-start.2) | collective-permute-done | bytes 16416 | tf_op jit(solution)/shard_map/ppermute | solution.py:403
  19.9 7.8 %collective-permute-done.3.halo_ref = f32[20,512]{1,0:T(8,128)S(1)} collective-permute-done((f32[20,512]{1,0:T(8,128)S(1)}, f32[20,512]{1,0:T(8,128)S(1)}, u32[]{:S(2)}, u32[]{:S(2)}) %collective-permute-start.3) | collective-permute-done | bytes 40992 | tf_op jit(solution)/shard_map/ppermute | solution.py:402
  27.7 7.0 %all-to-all-done = f32[1408,1,128]{2,1,0:T(1,128)S(1)} async-done(((f32[1408,1,128]{2,1,0:T(1,128)}), f32[1408,1,128]{2,1,0:T(1,128)S(1)}, u32[]{:S(2)}, u32[]{:S(2)}) %all-to-all-start) | async-done | bytes 720928 | tf_op jit(solution)/shard_map/all_to_all | solution.py:436
  34.7 0.0 copy-done.4
  34.7 0.0 copy-start.1
  34.7 0.4 shard_map.126
  35.0 0.0 copy-start
  35.0 0.0 copy-start.2
  35.1 0.0 copy-start.3
  35.1 17.8 %all_to_all.21 = f32[1408,1,128]{2,1,0:T(1,128)S(1)} all-to-all(f32[1408,1,128]{2,1,0:T(1,128)S(1)} %bitcast.27), channel_id=1, replica_groups=mesh['inst'=32,'span'=2,'rad'=2] {'inst'}, dimensions={0} | all-to-all | bytes 1441792 | tf_op jit(solution)/shard_map/all_to_all | solution.py:442
  52.8 0.0 copy-done.1
  52.8 0.0 copy-done
  52.8 0.0 copy-done.2
  52.8 0.0 copy-done.3
  52.8 2.0 %shard_map.127 = (f32[10,16,512]{2,1,0:T(8,128)}, f32[128,128]{1,0:T(8,128)S(1)}) custom-call(s32[1]{0:T(128)} %bitcast.rad_ref, f32[10,16,512]{2,1,0:T(8,128)S(1)} %get-tuple-element.31.w_ref, f32[1408,128]{1,0:T(8,128)S(1)} %bitcast.23, f32[2,16,128]{2,1,0:T(8,128)S(1)} %get-tuple-element.40.w_edge_ref, f32[20,512]{1,0:T(8,128)S(1)} %get-tuple-element.41.w_halo_ref, ...), custom_call_target="tpu_custom_call" | custom-call | bytes 3000000 | tf_op jit(solution)/shard_map/pallas_call | solution.py:443
  54.9 13.3 %all_to_all.22 = f32[128,1,128]{2,1,0:T(1,128)S(1)} all-to-all(f32[128,1,128]{2,1,0:T(1,128)S(1)} %bitcast.29), channel_id=1, replica_groups=mesh['inst'=32,'span'=2,'rad'=2] {'inst','span','rad'}, dimensions={0} | all-to-all | bytes 131072 | tf_op jit(solution)/shard_map/all_to_all | solution.py:448
  68.2 0.7 shard_map.128
Async XLA Ops:
  1.8 4.2 %collective-permute-start.1 = (f32[24,512]{1,0:T(8,128)S(1)}, f32[24,512]{1,0:T(8,128)S(1)}, u32[]{:S(2)}, u32[]{:S(2)}) collective-permute-start(f32[24,512]{1,0:T(8,128)S(1)} %get-tuple-element.26), channel_id=1, source_target_pairs={{0,1},{1,0},{2,3},{3,2},{4,5},{5,4},{6,7},{7,6},{8,9},{9,8},{10,11... | collective-permute-start | bytes 147464 | tf_op jit(solution)/shard_map/ppermute | solution.py:402
  3.4 2.5 %collective-permute-start = (f32[3,16,128]{2,1,0:T(8,128)S(1)}, f32[3,16,128]{2,1,0:T(8,128)S(1)}, u32[]{:S(2)}, u32[]{:S(2)}) collective-permute-start(f32[3,16,128]{2,1,0:T(8,128)S(1)} %get-tuple-element.25), channel_id=1, source_target_pairs={{0,2},{2,0},{1,3},{3,1},{4,6},{6,4},{5,7},{7,5},{8,10},{10,8},{9,1... | collective-permute-start | bytes 73736 | tf_op jit(solution)/shard_map/ppermute | solution.py:403
  7.1 27.5 %all-to-all-start = ((f32[1408,1,128]{2,1,0:T(1,128)}), f32[1408,1,128]{2,1,0:T(1,128)S(1)}, u32[]{:S(2)}, u32[]{:S(2)}) async-start(f32[1408,1,128]{2,1,0:T(1,128)} %bitcast.8), calls=%async_computation | async-start | bytes 1441792 | tf_op jit(solution)/shard_map/all_to_all | solution.py:436
  18.0 16.6 %copy-start.4 = (bf16[64,192]{1,0:T(8,128)(2,1)S(1)}, bf16[64,192]{1,0:T(8,128)(2,1)}, u32[]{:S(2)}) copy-start(bf16[64,192]{1,0:T(8,128)(2,1)} %constant.12.clone.table_ref) | copy-start | bytes 73732
  18.0 9.6 %collective-permute-start.3 = (f32[20,512]{1,0:T(8,128)S(1)}, f32[20,512]{1,0:T(8,128)S(1)}, u32[]{:S(2)}, u32[]{:S(2)}) collective-permute-start(f32[20,512]{1,0:T(8,128)S(1)} %get-tuple-element.35), channel_id=1, source_target_pairs={{0,1},{1,0},{2,3},{3,2},{4,5},{5,4},{6,7},{7,6},{8,9},{9,8},{10,11... | collective-permute-start | bytes 122888 | tf_op jit(solution)/shard_map/ppermute | solution.py:402
  18.7 1.2 %collective-permute-start.2 = (f32[2,16,128]{2,1,0:T(8,128)S(1)}, f32[2,16,128]{2,1,0:T(8,128)S(1)}, u32[]{:S(2)}, u32[]{:S(2)}) collective-permute-start(f32[2,16,128]{2,1,0:T(8,128)S(1)} %get-tuple-element.34), channel_id=1, source_target_pairs={{0,2},{2,0},{1,3},{3,1},{4,6},{6,4},{5,7},{7,5},{8,10},{10,8},{9,1... | collective-permute-start | bytes 49160 | tf_op jit(solution)/shard_map/ppermute | solution.py:403
  34.7 18.2 %copy-start.1 = (bf16[2,5,5,16,512]{4,3,2,1,0:T(8,128)(2,1)S(1)}, bf16[2,5,5,16,512]{4,3,2,1,0:T(8,128)(2,1)}, u32[]{:S(2)}) copy-start(bf16[2,5,5,16,512]{4,3,2,1,0:T(8,128)(2,1)} %jc_ref.1) | copy-start | bytes 2457604
  35.0 17.8 %copy-start = (bf16[2,5,5,16,512]{4,3,2,1,0:T(8,128)(2,1)S(1)}, bf16[2,5,5,16,512]{4,3,2,1,0:T(8,128)(2,1)}, u32[]{:S(2)}) copy-start(bf16[2,5,5,16,512]{4,3,2,1,0:T(8,128)(2,1)} %jr_ref.1) | copy-start | bytes 2457604
  35.0 17.8 %copy-start.2 = (f32[2,5,16,512]{3,2,1,0:T(8,128)S(1)}, f32[2,5,16,512]{3,2,1,0:T(8,128)}, u32[]{:S(2)}) copy-start(f32[2,5,16,512]{3,2,1,0:T(8,128)} %param.16) | copy-start | bytes 983044
  35.1 17.8 %copy-start.3 = (bf16[2,5,3,1024]{3,0,2,1:T(2,128)(2,1)S(1)}, bf16[2,5,3,1024]{3,0,2,1:T(2,128)(2,1)}, u32[]{:S(2)}) copy-start(bf16[2,5,3,1024]{3,0,2,1:T(2,128)(2,1)} %param.20) | copy-start | bytes 184324

commit v4 on v3

--- a/solution.py
+++ b/solution.py
@@ -14,7 +14,9 @@
 LT = 4
 HB = 2
 BODY = 40
-ROWS = 44
+RIM = 3
+ROWS = BODY + RIM
+HALF = 256
 GRP = 8 * ROWS
 NODES = 1024
 VAR_DEV = 32
@@ -80,6 +82,10 @@
     pad_ref[...] = jnp.zeros(pad_ref.shape, F32)
 
 
+def halo_rows(ref, at, count):
+    return jnp.concatenate([ref[at:at + count, :], ref[20 + at:20 + at + count, :]], axis=1)
+
+
 def corrections(rad, edge_ref, halo_ref, jrb_ref, jce_ref, dis_ref, t):
     lane = lax.broadcasted_iota(jnp.int32, (CR, 128), 1)
     diff, fourth = [], []
@@ -102,7 +108,7 @@
     near_row = jnp.where(rad == 0, CR - 1, 0)
     next_row = jnp.where(rad == 0, CR - 2, 1)
     sign = jnp.where(rad == 0, -0.5, 0.5)
-    first, second = [halo_ref[(2 * t + m) * NF:(2 * t + m + 1) * NF, :] for m in range(2)]
+    first, second = [halo_rows(halo_ref, (2 * t + m) * NF, NF) for m in range(2)]
     near = jnp.where(rad == 0, first, second)
     far = jnp.where(rad == 0, second, first)
     dis_near = EPS4 * dis_ref[pl.ds(near_row, 1), :]
@@ -125,27 +131,32 @@
     return fix
 
 
-def edge_kernel(rad_ref, psi_hbm, step_hbm, edge_ref, halo_ref, rows_ref, left_ref, right_ref, step_ref, sem):
+def interior_pass(t, psi_ref, src_ref, jr_ref, jc_ref, dis_ref, step_ref, pad_ref, part_ref):
+    for q in range(LT):
+        cell = lambda f, qq: psi_ref[t * NF + f, :, lanes(qq)]
+        jr = lambda i, j: jr_ref[t, i, j, :, lanes(q)]
+        jc = lambda i, j: jc_ref[t, i, j, :, lanes(q)]
+        res = interior(cell, pad_ref, jr, jc, dis_ref[:, lanes(q)], q)
+        sigma = step_ref[:, lanes(q)]
+        for f in range(NF):
+            part_ref[t * NF + f, :, lanes(q)] = cell(f, q) - sigma * (res[f] - src_ref[t * NF + f, :, lanes(q)])
+
+
+def edge_kernel(rad_ref, psi_hbm, edge_ref, halo_ref, rows_ref, left_ref, right_ref, sem):
     rad = rad_ref[0]
     start = pl.multiple_of(8 * (1 - rad), 8)
     copies = [
         pltpu.make_async_copy(psi_hbm.at[:, pl.ds(start, 8), :], rows_ref, sem.at[0]),
         pltpu.make_async_copy(psi_hbm.at[:, :, pl.ds(0, 128)], left_ref, sem.at[1]),
         pltpu.make_async_copy(psi_hbm.at[:, :, pl.ds(CT - 128, 128)], right_ref, sem.at[2]),
-        pltpu.make_async_copy(step_hbm, step_ref, sem.at[3]),
     ]
     for copy in copies:
         copy.start()
     copies[0].wait()
-    copies[3].wait()
     put_halo(halo_ref, lambda tf: rows_ref[tf], rad)
-    halo_ref[20:22] = jnp.where(rad == 0, step_ref[CR - 2:CR], step_ref[0:2])
-    halo_ref[22:24] = jnp.zeros((2, CT), F32)
     copies[1].wait()
     copies[2].wait()
     put_edge(edge_ref, lambda tf: (left_ref[tf], right_ref[tf]))
-    ends = (step_ref[:, lanes(0)], step_ref[:, lanes(LT - 1)])
-    edge_ref[TD] = pack_edge([ends] * NF)
 
 
 def pack_edge(ends):
@@ -171,11 +182,38 @@
             rows = tile(t * NF + f)
             pair = jnp.where(rad == 0, rows[6:8], rows[0:2])
             for m in range(2):
-                at = (2 * t + m) * NF + f
-                halo_ref[at:at + 1] = pair[m:m + 1]
-
-
-def first_kernel(rad_ref, me_ref, dis_hbm, step_hbm, cell_hbm, owner_hbm, local_hbm, psi_hbm, src_hbm, jr_hbm, jc_hbm,
+                put_row(halo_ref, (2 * t + m) * NF + f, pair[m:m + 1])
+
+
+def put_row(halo_ref, at, row):
+    halo_ref[at:at + 1] = row[:, :HALF]
+    halo_ref[20 + at:21 + at] = row[:, HALF:]
+
+
+def rim_of(tile, edge):
+    lane = lax.broadcasted_iota(jnp.int32, (3, 128), 1)
+    turned = pltpu.roll(edge, 2, 1)
+    turned = jnp.concatenate([turned, jnp.zeros((8, 128), F32)], axis=0)
+    dense = jnp.zeros((3, 128), F32)
+    for g in range(6):
+        part = turned[3 * g:3 * g + 3]
+        part = pltpu.roll(part, 20 * g, 1) if g else part
+        dense = jnp.where((lane >= 20 * g) & (lane < 20 * g + 20), part, dense)
+    return jnp.concatenate([tile(q) for q in range(LT)] + [dense, jnp.zeros((5, 128), F32)], axis=0)
+
+
+def edge_of(dense, edge_ref):
+    for g in range(6):
+        edge_ref[3 * g:3 * g + 3] = pltpu.roll(dense, 128 - 20 * g, 1) if g else dense
+    return pltpu.roll(edge_ref[0:CR], 126, 1)
+
+
+def halves(a, b):
+    lane = lax.broadcasted_iota(jnp.int32, a.shape, 1)
+    return jnp.where(lane < 64, a, pltpu.roll(b, 64, 1)), jnp.where(lane < 64, pltpu.roll(a, 64, 1), b)
+
+
+def first_kernel(rad_ref, span_ref, me_ref, dis_hbm, step_hbm, cell_hbm, owner_hbm, local_hbm, psi_hbm, src_hbm, jr_hbm, jc_hbm,
                  part_ref, psi_ref, jrb_ref, jce_ref, dis_ref, step_ref, sig_ref, ids_ref,
                  src_ref, jr_ref, jc_ref, pad_ref, cell_ref, owner_ref, local_ref, sem, sem_small):
     rad = rad_ref[0]
@@ -210,14 +248,11 @@
     for t in range(TD):
         for copy in copies[t]:
             copy.wait()
-        for q in range(LT):
-            cell = lambda f, qq: psi_ref[t * NF + f, :, lanes(qq)]
-            jr = lambda i, j: jr_ref[t, i, j, :, lanes(q)]
-            jc = lambda i, j: jc_ref[t, i, j, :, lanes(q)]
-            res = interior(cell, pad_ref, jr, jc, dis_ref[:, lanes(q)], q)
-            sigma = step_ref[:, lanes(q)]
-            for f in range(NF):
-                part_ref[t * NF + f, :, lanes(q)] = cell(f, q) - sigma * (res[f] - src_ref[t * NF + f, :, lanes(q)])
+
+        @pl.when((span_ref[0] == 1) | (t == 0))
+        def _():
+            interior_pass(t, psi_ref, src_ref, jr_ref, jc_ref, dis_ref, step_ref, pad_ref, part_ref)
+
         for i in range(NF):
             for j in range(NF):
                 whole = jr_ref[t, i, j].astype(F32)
@@ -226,23 +261,38 @@
                     lane < 64, jc_ref[t, i, j, :, lanes(0)].astype(F32), jc_ref[t, i, j, :, lanes(LT - 1)].astype(F32)).astype(BF)
 
 
-def send_kernel(rad_ref, psi_ref, part_ref, edge_ref, halo_ref, jrb_ref, jce_ref, dis_ref, step_ref, x_hbm, w_ref, w_edge_ref,
-                w_halo_ref, rim_ref, x_ref, sem):
+def send_kernel(rad_ref, span_ref, psi_ref, part_ref, edge_ref, halo_ref, jrb_ref, jce_ref, dis_ref, step_ref, src_hbm, jr_hbm, jc_hbm,
+                x_hbm, w_ref, w_edge_ref, w_halo_ref, rim_ref, x_ref, src_ref, jr_ref, jc_ref, pad_ref, late_ref, sem, sem_in):
     rad = rad_ref[0]
+
+    late_ref[...] = part_ref[...]
+
+    @pl.when(span_ref[0] == 0)
+    def _():
+        last = pl.ds((TD - 1) * NF, NF)
+        loads = [pltpu.make_async_copy(a, b, sem_in.at[i]) for i, (a, b) in enumerate(
+            [(src_hbm.at[last], src_ref.at[last]), (jr_hbm.at[TD - 1], jr_ref.at[TD - 1]), (jc_hbm.at[TD - 1], jc_ref.at[TD - 1])])]
+        for load in loads:
+            load.start()
+        clear_pad(pad_ref)
+        for load in loads:
+            load.wait()
+        interior_pass(TD - 1, psi_ref, src_ref, jr_ref, jc_ref, dis_ref, step_ref, pad_ref, late_ref)
+
     fixes = [corrections(rad, edge_ref, halo_ref, jrb_ref, jce_ref, dis_ref, t) for t in range(TD)]
-    for t in range(TD):
-        for q in range(LT):
-            rim_ref[10 * q:10 * q + 10] = halo_ref[10 * t:10 * t + 10, lanes(q)]
-        rim_ref[40:56] = edge_ref[t]
-        rim_ref[56:64] = jnp.zeros((8, 128), F32)
-        for e in range(2):
-            x_ref[pl.ds(BODY + 2 * t + e, 32, stride=ROWS), :] = rim_ref[pl.ds(e, 32, stride=2), :]
+    rims = [rim_of(lambda q: halo_ref[20 * (q // 2) + 10 * t:20 * (q // 2) + 10 * t + 10, lanes(q % 2)], edge_ref[t])
+            for t in range(TD)]
+    low, high = halves(*rims)
+    rim_ref[0:48] = low
+    rim_ref[48:96] = high
+    for e in range(RIM):
+        x_ref[pl.ds(BODY + e, 32, stride=ROWS), :] = rim_ref[32 * e:32 * e + 32]
     copies = []
     for q in range(LT):
         for t in range(TD):
             for f in range(NF):
                 mid = psi_ref[t * NF + f, :, lanes(q)]
-                w = part_ref[t * NF + f, :, lanes(q)] - step_ref[:, lanes(q)] * fixes[t](f, q)
+                w = late_ref[t * NF + f, :, lanes(q)] - step_ref[:, lanes(q)] * fixes[t](f, q)
                 w_ref[t * NF + f, :, lanes(q)] = w
                 for h in range(HB):
                     x_ref[pl.ds(q * GRP + row_of(t, 0, f, h), 8, stride=ROWS), :] = mid[8 * h:8 * h + 8]
@@ -253,6 +303,11 @@
     put_edge(w_edge_ref, lambda tf: (w_ref[tf, :, lanes(0)], w_ref[tf, :, lanes(LT - 1)]))
     start = pl.multiple_of(8 * (1 - rad), 8)
     put_halo(w_halo_ref, lambda tf: w_ref[tf, pl.ds(start, 8), :], rad)
+    w_edge_ref[TD] = pack_edge([(step_ref[:, lanes(0)], step_ref[:, lanes(LT - 1)])] * NF)
+    sigma = jnp.where(rad == 0, step_ref[CR - 2:CR], step_ref[0:2])
+    w_halo_ref[40:42] = sigma[:, :HALF]
+    w_halo_ref[42:44] = sigma[:, HALF:]
+    w_halo_ref[44:48] = jnp.zeros((4, HALF), F32)
     for copy in copies:
         copy.wait()
 
@@ -278,46 +333,58 @@
         low = (x - high.astype(F32)).astype(BF)
         return jnp.dot(table, jnp.concatenate([high, low, high], axis=0), preferred_element_type=F32)
 
+    count = 2 * NF
+
+    def pick(at):
+        return y_ref[pl.ds(at, 32, stride=ROWS), :]
+
+    def put(at, value):
+        v_ref[pl.ds(at, 32, stride=ROWS), :] = value
+
     def row(what, m, t):
-        if m < 2 * NF:
-            return (t * 2 + what) * 2 * NF + m
-        return BODY + 2 * t + m - 2 * NF
-
-    def gather(what, count):
-        return jnp.concatenate([jnp.concatenate(
-            [y_ref[pl.ds(row(what, m, t), 32, stride=ROWS), :] for t in range(TD)], axis=0) for m in range(count)], axis=1)
-
-    def scatter(what, value, count):
+        return (t * 2 + what) * count + m
+
+    def gather(what):
+        return [jnp.concatenate([pick(row(what, m, t)) for t in range(TD)], axis=0) for m in range(count)]
+
+    def scatter(what, value):
         for m in range(count):
             for t in range(TD):
-                v_ref[pl.ds(row(what, m, t), 32, stride=ROWS), :] = value[32 * t:32 * t + 32, lanes(m)]
-
-    count = 2 * NF
+                put(row(what, m, t), value[32 * t:32 * t + 32, lanes(m)])
+
+    rims = [pick(BODY + e) for e in range(RIM)]
+    rims = [jnp.concatenate(halves(rims[0], rims[1]), axis=0), jnp.concatenate([rims[2], pltpu.roll(rims[2], 64, 1)], axis=0)]
     sigma = jnp.concatenate([sig_ref[0:1, :], sig_ref[1:2, :]] * NF, axis=1)
-    time0 = apply(gather(0, count + 2))
-    scatter(0, time0, count + 2)
-    psi1 = gather(1, count) - sigma * time0[:, :128 * count]
-    scatter(1, apply(psi1), count)
+    time0 = apply(jnp.concatenate(gather(0) + rims, axis=1))
+    scatter(0, time0)
+    pair, single = [time0[:, lanes(count + m)] for m in range(2)]
+    for e, value in enumerate(halves(pair[:32], pair[32:]) + halves(single[:32], single[32:])[:1]):
+        put(BODY + e, value)
+    psi1 = jnp.concatenate(gather(1), axis=1) - sigma * time0[:, :128 * count]
+    scatter(1, apply(psi1))
 
 
 def plane(ref, what, t, f, q):
     return jnp.concatenate([ref[pl.ds(q * GRP + row_of(t, what, f, h), 8, stride=ROWS), :] for h in range(HB)], axis=0)
 
 
-def last_kernel(rad_ref, w_ref, u_ref, w_edge_ref, w_halo_ref, edge0_ref, halo0_ref, jr_ref, jc_ref, jrb_ref, jce_ref, dis_ref,
-                step_ref, src_ref, ids_ref, pick_ref, label_ref, sd_ref, out_hbm, sens_ref, psi1_ref, psi_ref, edge_ref, halo_ref, rim_ref, pad_ref, sem):
+def last_kernel(rad_ref, w_ref, u_ref, w_edge_ref, w_halo_ref, jr_ref, jc_ref, jrb_ref, jce_ref, dis_ref,
+                step_ref, src_ref, ids_ref, pick_ref, label_ref, sd_ref, out_hbm, sens_ref, psi1_ref, psi_ref, edge_ref, halo_ref, rim_ref, turn_ref, pad_ref, sem):
     rad = rad_ref[0]
     clear_pad(pad_ref)
-    for t in range(TD):
-        for e in range(2):
-            rim_ref[pl.ds(e, 32, stride=2), :] = u_ref[pl.ds(BODY + 2 * t + e, 32, stride=ROWS), :]
+    for e in range(RIM):
+        rim_ref[32 * e:32 * e + 32] = u_ref[pl.ds(BODY + e, 32, stride=ROWS), :]
+    rims = halves(rim_ref[0:48], rim_ref[48:96])
+    for t in range(TD):
         for m in range(2):
             at = (2 * t + m) * NF
             for q in range(LT):
-                halo_ref[at:at + NF, lanes(q)] = (
-                    w_halo_ref[at:at + NF, lanes(q)]
-                    - halo0_ref[20 + m:21 + m, lanes(q)] * rim_ref[10 * q + NF * m:10 * q + NF * m + NF])
-        edge_ref[t] = w_edge_ref[t] - edge0_ref[TD] * rim_ref[40:56]
+                side = q // 2
+                here = slice(20 * side + at, 20 * side + at + NF)
+                sigma = w_halo_ref[40 + 2 * side + m:41 + 2 * side + m, lanes(q % 2)]
+                halo_ref[here, lanes(q % 2)] = (
+                    w_halo_ref[here, lanes(q % 2)] - sigma * rims[t][10 * q + NF * m:10 * q + NF * m + NF])
+        edge_ref[t] = w_edge_ref[t] - w_edge_ref[TD] * edge_of(rims[t][40:43], turn_ref)
     copies = []
     for t in range(TD):
         fix = corrections(rad, edge_ref, halo_ref, jrb_ref, jce_ref, dis_ref, t)
@@ -407,6 +474,7 @@
 def body(adjoint_start, jac_rad, jac_circ, dissip, pseudo_step, source, node_cell, node_owner, node_local, shape_deriv):
     me = lax.axis_index("inst").astype(jnp.int32).reshape(1)
     rad = lax.axis_index("rad").astype(jnp.int32).reshape(1)
+    span = lax.axis_index("span").astype(jnp.int32).reshape(1)
     n = TD * NF
     psi0 = adjoint_start.reshape(n, CR, CT)
     src = source.reshape(n, CR, CT)
@@ -418,32 +486,34 @@
     held = [pltpu.with_memory_space_constraint(a, pltpu.HBM) for a in (
         dissip, pseudo_step, node_cell.reshape(line), node_owner.reshape(line), node_local.reshape(line), psi0, src, jac_rad, jac_circ)]
     edge0, halo0 = call(
-        edge_kernel, [SM, HM, HM], [(f32(TD + 1, CR, 128), VM), (f32(24, CT), VM)],
-        [VM((n, 8, CT), F32), VM((n, CR, 128), F32), VM((n, CR, 128), F32), VM((CR, CT), F32), dma((4,))])(rad, held[5], held[1])
+        edge_kernel, [SM, HM], [(f32(TD, CR, 128), VM), (f32(40, HALF), VM)],
+        [VM((n, 8, CT), F32), VM((n, CR, 128), F32), VM((n, CR, 128), F32), dma((3,))])(rad, held[5])
     edge0, halo0 = swap_halos(edge0, halo0)
     part, psi, jrb, jce, dis, step, sig, ids = call(
-        first_kernel, [SM, SM] + [HM] * 9,
+        first_kernel, [SM, SM, SM] + [HM] * 9,
         [(full, VM), (full, VM), (f32(n, NF, CT), VM), (jax.ShapeDtypeStruct((n, NF, CR, 128), BF), VM), (flat, VM), (flat, VM),
          (f32(2, 128), VM), (jax.ShapeDtypeStruct((8, NODES), jnp.int32), VM)],
         [VM((n, CR, CT), F32), VM(jac_rad.shape, BF), VM(jac_circ.shape, BF), pad] + [VM(line, jnp.int32)] * 3 + [dma((TD, 4)), dma((5,))],
-        micros=3)(rad, me, *held)
-    rim = VM((64, 128), F32)
+        micros=3)(rad, span, me, *held)
+    rim = VM((96, 128), F32)
+    swapped = [(f32(TD + 1, CR, 128), VM), (f32(48, HALF), VM)]
     x, w, w_edge, w_halo = call(
-        send_kernel, [SM] + [VM] * 8, [(f32(32 * ROWS, 128), HM), (full, VM), (f32(TD, CR, 128), VM), (f32(2 * n, CT), VM)],
-        [rim, VM((32 * ROWS, 128), F32), dma((LT,))])(
-        rad, psi, part, edge0, halo0, jrb, jce, dis, step)
+        send_kernel, [SM, SM] + [VM] * 8 + [HM] * 3, [(f32(32 * ROWS, 128), HM), (full, VM)] + swapped,
+        [rim, VM((32 * ROWS, 128), F32), VM((n, CR, CT), F32), VM(jac_rad.shape, BF), VM(jac_circ.shape, BF), pad, VM((n, CR, CT), F32),
+         dma((LT,)), dma((3,))])(
+        rad, span, psi, part, edge0, halo0, jrb, jce, dis, step, *held[6:])
     w_edge, w_halo = swap_halos(w_edge, w_halo)
     y = lax.all_to_all(x.reshape(32 * ROWS, 1, 128), "inst", 0, 0, tiled=True).reshape(32 * ROWS, 128)
     bf16 = lambda *shape: (jax.ShapeDtypeStruct(shape, BF), VM)
     pick, label = call(label_kernel, [VM], [bf16(CT, NODES), bf16(128, NODES)])(ids)
     v, w_edge, w_halo = call(
-        time_kernel, [VM] * 5 + [pl.ANY] * 2, [(f32(32 * ROWS, 128), VM), (f32(TD, CR, 128), VM), (f32(2 * n, CT), VM)])(
+        time_kernel, [VM] * 5 + [pl.ANY] * 2, [(f32(32 * ROWS, 128), VM)] + swapped)(
         jnp.asarray(spectral_blocks()), sig, y, w_edge, w_halo, pick, label)
     u = lax.all_to_all(v.reshape(32 * ROWS, 1, 128), "inst", 0, 0, tiled=True).reshape(32 * ROWS, 128)
     psi2, parts = call(
-        last_kernel, [SM] + [VM] * 17, [(full, HM), (f32(128, 128), VM)],
-        [VM((n, CR, CT), F32), VM((n, CR, CT), F32), VM((TD, CR, 128), F32), VM((2 * n, CT), F32), rim, pad, dma((TD,))])(
-        rad, w, u, w_edge, w_halo, edge0, halo0, jac_rad, jac_circ, jrb, jce, dis, step, src, ids, pick, label,
+        last_kernel, [SM] + [VM] * 15, [(full, HM), (f32(128, 128), VM)],
+        [VM((n, CR, CT), F32), VM((n, CR, CT), F32), VM((TD, CR, 128), F32), VM((40, HALF), F32), rim, VM((24, 128), F32), pad, dma((TD,))])(
+        rad, w, u, w_edge, w_halo, jac_rad, jac_circ, jrb, jce, dis, step, src, ids, pick, label,
         shape_deriv.transpose(1, 2, 0, 3).reshape(3 * NF, TD, NODES))
     got = lax.all_to_all(parts, ALL, 0, 0, tiled=True)
     sens, = call(total_kernel, [VM], [(f32(3, VAR_DEV), VM)])(got)

time: 69.9 us -> 69 us (0.987)
  Pallas kernels: 8.07 us -> 9.61 us
  waiting for transfers between devices: 15.7 us -> 14.4 us
  blocking collectives: 31 us -> 30 us
    pallas_call x5, Pallas kernels: 7.17 us -> 8.71 us  [the longest x1 2.95 us: body(): call(send_kernel, [SM, SM] + [VM] * 8 + [HM] * 3, [(f32(32 * ROWS, 128),...]
    ppermute x2, waiting for transfers between devices: 7.81 us -> 6.41 us  [swap_halos(): halo = lax.ppermute(halo, 'rad', SWAP)]
    all_to_all x1, blocking collectives: 17.8 us -> 16.7 us  [body(): lax.all_to_all(v.reshape(32 * ROWS, 1, 128), 'inst', 0, 0, tiled=True)]
  transfers between devices with their start and end apart: 5 -> 5, of which waited for: 3 -> 4; matrix products, arithmetic and copies ran while one was open for 0% -> 0% of each run, Pallas kernels for 4% -> 3%
where the time goes in v4:
time: 69 us; the launch traced here: 67.9 us
  blocking collectives  30 us (43%)
  waiting for transfers between devices  14.4 us (21%)
  starting transfers between devices  13.2 us (19%)
  Pallas kernels  9.61 us (14%)
  between operations  0.73 us (1%)
    all_to_all x1, blocking collectives, body(): lax.all_to_all(v.reshape(32 * ROWS, 1, 128), 'inst', 0, 0, tiled=True)  16.7 us
    all_to_all x1, blocking collectives, body(): got = lax.all_to_all(parts, ALL, 0, 0, tiled=True)  13.3 us
    all_to_all x1, starting transfers between devices, body(): lax.all_to_all(x.reshape(32 * ROWS, 1, 128), 'inst', 0, 0, tiled=True)  10.9 us
    all_to_all x1, waiting for transfers between devices, body(): lax.all_to_all(x.reshape(32 * ROWS, 1, 128), 'inst', 0, 0, tiled=True)  6.99 us
    ppermute x2, waiting for transfers between devices, swap_halos(): halo = lax.ppermute(halo, 'rad', SWAP)  6.41 us
    pallas_call x1, Pallas kernels, body(): call(send_kernel, [SM, SM] + [VM] * 8 + [HM] * 3, [(f32(32 * ROWS, 128),...  2.95 us
    ppermute x2, starting transfers between devices, swap_halos(): halo = lax.ppermute(halo, 'rad', SWAP)  2.33 us
    pallas_call x1, Pallas kernels, body(): call(first_kernel, [SM, SM, SM] + [HM] * 9, [(full, VM), (full, VM), (f32...  2.14 us
  transfers between devices with their start and end apart: 5, of which 4 were waited for; matrix products, arithmetic and copies ran while one was open for 0% of the time, Pallas kernels for 3%

profile of v4, /device:TPU:0, one launch (start us, length us, event | category | flops | bytes accessed | tf_op | source)
XLA Modules:
  0.0 67.9 jit_solution(100712612892240389)
XLA Ops:
  0.6 1.1 %shard_map.123 = (f32[2,16,128]{2,1,0:T(8,128)S(1)}, f32[40,256]{1,0:T(8,128)S(1)}) custom-call(s32[1]{0:T(128)} %bitcast.rad_ref, f32[10,16,512]{2,1,0:T(8,128)} %bitcast.33), custom_call_target="tpu_custom_call" | custom-call | bytes 3000000 | tf_op jit(solution)/shard_map/pallas_call | solution.py:488
  1.8 1.7 %collective-permute-start.1 = (f32[40,256]{1,0:T(8,128)S(1)}, f32[40,256]{1,0:T(8,128)S(1)}, u32[]{:S(2)}, u32[]{:S(2)}) collective-permute-start(f32[40,256]{1,0:T(8,128)S(1)} %get-tuple-element.26), channel_id=1, source_target_pairs={{0,1},{1,0},{2,3},{3,2},{4,5},{5,4},{6,7},{7,6},{8,9},{9,8},{10,11... | collective-permute-start | bytes 122888 | tf_op jit(solution)/shard_map/ppermute | solution.py:469
  3.4 0.0 collective-permute-start
  3.4 2.1 %shard_map.122 = (f32[10,16,512]{2,1,0:T(8,128)S(1)}, f32[10,16,512]{2,1,0:T(8,128)S(1)}, f32[10,5,512]{2,1,0:T(8,128)S(1)}, bf16[10,5,16,128]{3,2,1,0:T(8,128)(...) custom-call(s32[1]{0:T(128)} %bitcast.rad_ref, ...), custom_call_target="tpu_custom_call" | custom-call | bytes 9000000 | tf_op jit(solution)/shard_map/pallas_call | solution.py:492
  5.6 0.0 collective-permute-done.edge_ref
  5.6 0.3 collective-permute-done.1.halo_ref
  5.8 3.0 %shard_map.124 = (f32[1376,128]{1,0:T(8,128)}, f32[10,16,512]{2,1,0:T(8,128)S(1)}, f32[3,16,128]{2,1,0:T(8,128)S(1)}, f32[48,256]{1,0:T(8,128)S(1)}) custom-call(s32[1]{0:T(128)} %bitcast.rad_ref, s32[1]{0:T(128)} %bitcast.1.span_ref, f32[10,16,512]{2,1,0:T(8,128)S(1)} %get-tuple-element.23.psi_ref, f32[10,16,512]{2,1,0:T(8,128)S(1)} %get-tuple-element.24.part_ref, ...), custom_call_target="tpu_custom_call" | custom-call | bytes 3000000 | tf_op jit(solution)/shard_map/pallas_call | solution.py:500
  8.8 10.9 %all-to-all-start = ((f32[1376,1,128]{2,1,0:T(1,128)}), f32[1376,1,128]{2,1,0:T(1,128)S(1)}, u32[]{:S(2)}, u32[]{:S(2)}) async-start(f32[1376,1,128]{2,1,0:T(1,128)} %bitcast.9), calls=%async_computation | async-start | bytes 1409024 | tf_op jit(solution)/shard_map/all_to_all | solution.py:506
  19.7 0.0 copy-start.4
  19.7 0.7 collective-permute-start.3
  20.4 0.0 collective-permute-start.2
  20.4 0.2 shard_map.125
  20.6 1.0 %collective-permute-done.2.edge_ref = f32[3,16,128]{2,1,0:T(8,128)S(1)} collective-permute-done((f32[3,16,128]{2,1,0:T(8,128)S(1)}, f32[3,16,128]{2,1,0:T(8,128)S(1)}, u32[]{:S(2)}, u32[]{:S(2)}) %collective-permute-start.2) | collective-permute-done | bytes 24608 | tf_op jit(solution)/shard_map/ppermute | solution.py:470
  21.6 6.1 %collective-permute-done.3.halo_ref = f32[48,256]{1,0:T(8,128)S(1)} collective-permute-done((f32[48,256]{1,0:T(8,128)S(1)}, f32[48,256]{1,0:T(8,128)S(1)}, u32[]{:S(2)}, u32[]{:S(2)}) %collective-permute-start.3) | collective-permute-done | bytes 49184 | tf_op jit(solution)/shard_map/ppermute | solution.py:469
  27.7 7.0 %all-to-all-done = f32[1376,1,128]{2,1,0:T(1,128)S(1)} async-done(((f32[1376,1,128]{2,1,0:T(1,128)}), f32[1376,1,128]{2,1,0:T(1,128)S(1)}, u32[]{:S(2)}, u32[]{:S(2)}) %all-to-all-start) | async-done | bytes 704544 | tf_op jit(solution)/shard_map/all_to_all | solution.py:506
  34.7 0.0 copy-done.4
  34.7 0.0 copy-start.1
  34.7 0.4 shard_map.126
  35.1 0.0 copy-start
  35.1 0.0 copy-start.2
  35.1 0.0 copy-start.3
  35.1 16.7 %all_to_all.21 = f32[1376,1,128]{2,1,0:T(1,128)S(1)} all-to-all(f32[1376,1,128]{2,1,0:T(1,128)S(1)} %bitcast.29), channel_id=1, replica_groups=mesh['inst'=32,'span'=2,'rad'=2] {'inst'}, dimensions={0} | all-to-all | bytes 1409024 | tf_op jit(solution)/shard_map/all_to_all | solution.py:512
  51.9 0.0 copy-done.1
  51.9 0.0 copy-done
  51.9 0.0 copy-done.2
  51.9 0.0 copy-done.3
  51.9 2.1 %shard_map.127 = (f32[10,16,512]{2,1,0:T(8,128)}, f32[128,128]{1,0:T(8,128)S(1)}) custom-call(s32[1]{0:T(128)} %bitcast.rad_ref, f32[10,16,512]{2,1,0:T(8,128)S(1)} %get-tuple-element.31.w_ref, f32[1376,128]{1,0:T(8,128)S(1)} %bitcast.28, f32[3,16,128]{2,1,0:T(8,128)S(1)} %get-tuple-element.40.w_edge_ref, f32[48,256]{1,0:T(8,128)S(1)} %get-tuple-element.41.w_halo_ref, ...), custom_call_target="tpu_custom_call" | custom-call | bytes 3000000 | tf_op jit(solution)/shard_map/pallas_call | solution.py:513
  54.0 13.3 %all_to_all.22 = f32[128,1,128]{2,1,0:T(1,128)S(1)} all-to-all(f32[128,1,128]{2,1,0:T(1,128)S(1)} %bitcast.31), channel_id=1, replica_groups=mesh['inst'=32,'span'=2,'rad'=2] {'inst','span','rad'}, dimensions={0} | all-to-all | bytes 131072 | tf_op jit(solution)/shard_map/all_to_all | solution.py:518
  67.3 0.7 shard_map.128
Async XLA Ops:
  1.8 4.1 %collective-permute-start.1 = (f32[40,256]{1,0:T(8,128)S(1)}, f32[40,256]{1,0:T(8,128)S(1)}, u32[]{:S(2)}, u32[]{:S(2)}) collective-permute-start(f32[40,256]{1,0:T(8,128)S(1)} %get-tuple-element.26), channel_id=1, source_target_pairs={{0,1},{1,0},{2,3},{3,2},{4,5},{5,4},{6,7},{7,6},{8,9},{9,8},{10,11... | collective-permute-start | bytes 122888 | tf_op jit(solution)/shard_map/ppermute | solution.py:469
  3.4 2.1 %collective-permute-start = (f32[2,16,128]{2,1,0:T(8,128)S(1)}, f32[2,16,128]{2,1,0:T(8,128)S(1)}, u32[]{:S(2)}, u32[]{:S(2)}) collective-permute-start(f32[2,16,128]{2,1,0:T(8,128)S(1)} %get-tuple-element.25), channel_id=1, source_target_pairs={{0,2},{2,0},{1,3},{3,1},{4,6},{6,4},{5,7},{7,5},{8,10},{10,8},{9,1... | collective-permute-start | bytes 49160 | tf_op jit(solution)/shard_map/ppermute | solution.py:470
  8.8 25.9 %all-to-all-start = ((f32[1376,1,128]{2,1,0:T(1,128)}), f32[1376,1,128]{2,1,0:T(1,128)S(1)}, u32[]{:S(2)}, u32[]{:S(2)}) async-start(f32[1376,1,128]{2,1,0:T(1,128)} %bitcast.9), calls=%async_computation | async-start | bytes 1409024 | tf_op jit(solution)/shard_map/all_to_all | solution.py:506
  19.7 15.0 %copy-start.4 = (bf16[64,192]{1,0:T(8,128)(2,1)S(1)}, bf16[64,192]{1,0:T(8,128)(2,1)}, u32[]{:S(2)}) copy-start(bf16[64,192]{1,0:T(8,128)(2,1)} %constant.14.clone.table_ref) | copy-start | bytes 73732
  19.7 8.0 %collective-permute-start.3 = (f32[48,256]{1,0:T(8,128)S(1)}, f32[48,256]{1,0:T(8,128)S(1)}, u32[]{:S(2)}, u32[]{:S(2)}) collective-permute-start(f32[48,256]{1,0:T(8,128)S(1)} %get-tuple-element.35), channel_id=1, source_target_pairs={{0,1},{1,0},{2,3},{3,2},{4,5},{5,4},{6,7},{7,6},{8,9},{9,8},{10,11... | collective-permute-start | bytes 147464 | tf_op jit(solution)/shard_map/ppermute | solution.py:469
  20.4 1.2 %collective-permute-start.2 = (f32[3,16,128]{2,1,0:T(8,128)S(1)}, f32[3,16,128]{2,1,0:T(8,128)S(1)}, u32[]{:S(2)}, u32[]{:S(2)}) collective-permute-start(f32[3,16,128]{2,1,0:T(8,128)S(1)} %get-tuple-element.34), channel_id=1, source_target_pairs={{0,2},{2,0},{1,3},{3,1},{4,6},{6,4},{5,7},{7,5},{8,10},{10,8},{9,1... | collective-permute-start | bytes 73736 | tf_op jit(solution)/shard_map/ppermute | solution.py:470
  34.7 17.2 %copy-start.1 = (bf16[2,5,5,16,512]{4,3,2,1,0:T(8,128)(2,1)S(1)}, bf16[2,5,5,16,512]{4,3,2,1,0:T(8,128)(2,1)}, u32[]{:S(2)}) copy-start(bf16[2,5,5,16,512]{4,3,2,1,0:T(8,128)(2,1)} %jc_ref.1) | copy-start | bytes 2457604
  35.1 16.8 %copy-start = (bf16[2,5,5,16,512]{4,3,2,1,0:T(8,128)(2,1)S(1)}, bf16[2,5,5,16,512]{4,3,2,1,0:T(8,128)(2,1)}, u32[]{:S(2)}) copy-start(bf16[2,5,5,16,512]{4,3,2,1,0:T(8,128)(2,1)} %jr_ref.1) | copy-start | bytes 2457604
  35.1 16.8 %copy-start.2 = (f32[2,5,16,512]{3,2,1,0:T(8,128)S(1)}, f32[2,5,16,512]{3,2,1,0:T(8,128)}, u32[]{:S(2)}) copy-start(f32[2,5,16,512]{3,2,1,0:T(8,128)} %param.16) | copy-start | bytes 983044
  35.1 16.8 %copy-start.3 = (bf16[2,5,3,1024]{3,0,2,1:T(2,128)(2,1)S(1)}, bf16[2,5,3,1024]{3,0,2,1:T(2,128)(2,1)}, u32[]{:S(2)}) copy-start(bf16[2,5,3,1024]{3,0,2,1:T(2,128)(2,1)} %param.20) | copy-start | bytes 184324

commit v5 on v4

--- a/solution.py
+++ b/solution.py
@@ -34,9 +34,25 @@
     table = np.where(diff == 0, 0.0, 0.5 * np.where(diff % 2 == 0, 1.0, -1.0) / np.tan(np.pi * safe / NT))
     order = np.concatenate([index[0::2], index[1::2]])
     apply = table.T[order][:, order].astype(np.float32)
-    high = apply.astype(BF)
-    low = (apply - high.astype(np.float32)).astype(BF)
-    return np.concatenate([high, high, low], axis=1)
+    pieces = []
+    for _ in range(3):
+        pieces.append(apply.astype(BF))
+        apply = apply - pieces[-1].astype(np.float32)
+    high, mid, low = pieces
+    return np.concatenate([high, high, mid, mid, high, low], axis=1)
+
+
+def split(x):
+    pieces = []
+    for _ in range(3):
+        pieces.append(x.astype(BF))
+        x = x - pieces[-1].astype(F32)
+    return pieces
+
+
+def pair_up(x):
+    high, mid, low = split(x)
+    return jnp.concatenate([high, mid, high, mid, low, high], axis=0)
 
 
 def row_of(t, what, f, h):
@@ -329,9 +345,7 @@
     table = table_ref[...]
 
     def apply(x):
-        high = x.astype(BF)
-        low = (x - high.astype(F32)).astype(BF)
-        return jnp.dot(table, jnp.concatenate([high, low, high], axis=0), preferred_element_type=F32)
+        return jnp.dot(table, pair_up(x), preferred_element_type=F32)
 
     count = 2 * NF
 
@@ -410,10 +424,8 @@
     weights = [sd_ref[m].astype(F32) for m in range(3 * NF)]
     for t in range(TD):
         whole = psi_ref[t * NF:(t + 1) * NF].reshape(NF * CR, CT)
-        high = whole.astype(BF)
-        low = (whole - high.astype(F32)).astype(BF)
-        both = jnp.dot(jnp.concatenate([high, low], axis=0), pick, preferred_element_type=F32)
-        value = both[:NF * CR] + both[NF * CR:]
+        got = jnp.dot(jnp.concatenate(split(whole), axis=0), pick, preferred_element_type=F32)
+        value = got[:NF * CR] + got[NF * CR:2 * NF * CR] + got[2 * NF * CR:]
         for f in range(NF):
             here = value[f * CR:(f + 1) * CR]
             for k in range(3):
@@ -425,12 +437,9 @@
         for s in range(2):
             parts.append(kept * (owner == s).astype(F32))
     stack = jnp.concatenate(parts, axis=0)
-    high = stack.astype(BF)
-    low = (stack - high.astype(F32)).astype(BF)
     label = label_ref[...]
     dims = (((1,), (1,)), ((), ()))
-    total = lax.dot_general(high, label, dims, preferred_element_type=F32) + lax.dot_general(
-        low, label, dims, preferred_element_type=F32)
+    total = sum(lax.dot_general(piece, label, dims, preferred_element_type=F32) for piece in split(stack))
     lane = lax.broadcasted_iota(jnp.int32, (1, 128), 1)
     line = []
     for s in range(2):

time: 69 us -> 69.5 us (level)
  no operation moved by 1% of the time
where the time goes in v5:
time: 69.5 us; the launch traced here: 68.4 us
  blocking collectives  30 us (43%)
  waiting for transfers between devices  14.4 us (21%)
  starting transfers between devices  13.4 us (19%)
  Pallas kernels  9.89 us (14%)
  between operations  0.74 us (1%)
    all_to_all x1, blocking collectives, body(): lax.all_to_all(v.reshape(32 * ROWS, 1, 128), 'inst', 0, 0, tiled=True)  16.7 us
    all_to_all x1, blocking collectives, body(): got = lax.all_to_all(parts, ALL, 0, 0, tiled=True)  13.3 us
    all_to_all x1, starting transfers between devices, body(): lax.all_to_all(x.reshape(32 * ROWS, 1, 128), 'inst', 0, 0, tiled=True)  11 us
    all_to_all x1, waiting for transfers between devices, body(): lax.all_to_all(x.reshape(32 * ROWS, 1, 128), 'inst', 0, 0, tiled=True)  6.99 us
    ppermute x2, waiting for transfers between devices, swap_halos(): halo = lax.ppermute(halo, 'rad', SWAP)  6.42 us
    pallas_call x1, Pallas kernels, body(): call(send_kernel, [SM, SM] + [VM] * 8 + [HM] * 3, [(f32(32 * ROWS, 128),...  2.95 us
    ppermute x2, starting transfers between devices, swap_halos(): halo = lax.ppermute(halo, 'rad', SWAP)  2.33 us
    pallas_call x1, Pallas kernels, body(): call(last_kernel, [SM] + [VM] * 15, [(full, HM), (f32(128, 128), VM)], [V...  2.25 us
  transfers between devices with their start and end apart: 5, of which 4 were waited for; matrix products, arithmetic and copies ran while one was open for 0% of the time, Pallas kernels for 3%

profile of v5, /device:TPU:0, one launch (start us, length us, event | category | flops | bytes accessed | tf_op | source)
XLA Modules:
  0.0 68.4 jit_solution(2330035694318998947)
XLA Ops:
  0.6 1.1 %shard_map.123 = (f32[2,16,128]{2,1,0:T(8,128)S(1)}, f32[40,256]{1,0:T(8,128)S(1)}) custom-call(s32[1]{0:T(128)} %bitcast.rad_ref, f32[10,16,512]{2,1,0:T(8,128)} %bitcast.33), custom_call_target="tpu_custom_call" | custom-call | bytes 3000000 | tf_op jit(solution)/shard_map/pallas_call | solution.py:497
  1.8 1.7 %collective-permute-start.1 = (f32[40,256]{1,0:T(8,128)S(1)}, f32[40,256]{1,0:T(8,128)S(1)}, u32[]{:S(2)}, u32[]{:S(2)}) collective-permute-start(f32[40,256]{1,0:T(8,128)S(1)} %get-tuple-element.26), channel_id=1, source_target_pairs={{0,1},{1,0},{2,3},{3,2},{4,5},{5,4},{6,7},{7,6},{8,9},{9,8},{10,11... | collective-permute-start | bytes 122888 | tf_op jit(solution)/shard_map/ppermute | solution.py:478
  3.4 0.0 collective-permute-start
  3.4 2.1 %shard_map.122 = (f32[10,16,512]{2,1,0:T(8,128)S(1)}, f32[10,16,512]{2,1,0:T(8,128)S(1)}, f32[10,5,512]{2,1,0:T(8,128)S(1)}, bf16[10,5,16,128]{3,2,1,0:T(8,128)(...) custom-call(s32[1]{0:T(128)} %bitcast.rad_ref, ...), custom_call_target="tpu_custom_call" | custom-call | bytes 9000000 | tf_op jit(solution)/shard_map/pallas_call | solution.py:501
  5.6 0.0 collective-permute-done.edge_ref
  5.6 0.3 collective-permute-done.1.halo_ref
  5.8 3.0 %shard_map.124 = (f32[1376,128]{1,0:T(8,128)}, f32[10,16,512]{2,1,0:T(8,128)S(1)}, f32[3,16,128]{2,1,0:T(8,128)S(1)}, f32[48,256]{1,0:T(8,128)S(1)}) custom-call(s32[1]{0:T(128)} %bitcast.rad_ref, s32[1]{0:T(128)} %bitcast.1.span_ref, f32[10,16,512]{2,1,0:T(8,128)S(1)} %get-tuple-element.23.psi_ref, f32[10,16,512]{2,1,0:T(8,128)S(1)} %get-tuple-element.24.part_ref, ...), custom_call_target="tpu_custom_call" | custom-call | bytes 3000000 | tf_op jit(solution)/shard_map/pallas_call | solution.py:509
  8.8 0.0 copy-start.4
  8.8 11.0 %all-to-all-start = ((f32[1376,1,128]{2,1,0:T(1,128)}), f32[1376,1,128]{2,1,0:T(1,128)S(1)}, u32[]{:S(2)}, u32[]{:S(2)}) async-start(f32[1376,1,128]{2,1,0:T(1,128)} %bitcast.9), calls=%async_computation | async-start | bytes 1409024 | tf_op jit(solution)/shard_map/all_to_all | solution.py:515
  19.8 0.7 collective-permute-start.3
  20.5 0.0 collective-permute-start.2
  20.5 0.2 shard_map.125
  20.8 1.0 %collective-permute-done.2.edge_ref = f32[3,16,128]{2,1,0:T(8,128)S(1)} collective-permute-done((f32[3,16,128]{2,1,0:T(8,128)S(1)}, f32[3,16,128]{2,1,0:T(8,128)S(1)}, u32[]{:S(2)}, u32[]{:S(2)}) %collective-permute-start.2) | collective-permute-done | bytes 24608 | tf_op jit(solution)/shard_map/ppermute | solution.py:479
  21.7 6.2 %collective-permute-done.3.halo_ref = f32[48,256]{1,0:T(8,128)S(1)} collective-permute-done((f32[48,256]{1,0:T(8,128)S(1)}, f32[48,256]{1,0:T(8,128)S(1)}, u32[]{:S(2)}, u32[]{:S(2)}) %collective-permute-start.3) | collective-permute-done | bytes 49184 | tf_op jit(solution)/shard_map/ppermute | solution.py:478
  27.9 7.0 %all-to-all-done = f32[1376,1,128]{2,1,0:T(1,128)S(1)} async-done(((f32[1376,1,128]{2,1,0:T(1,128)}), f32[1376,1,128]{2,1,0:T(1,128)S(1)}, u32[]{:S(2)}, u32[]{:S(2)}) %all-to-all-start) | async-done | bytes 704544 | tf_op jit(solution)/shard_map/all_to_all | solution.py:515
  34.9 0.0 copy-done.4
  34.9 0.0 copy-start.1
  34.9 0.5 shard_map.126
  35.4 0.0 copy-start
  35.4 0.0 copy-start.2
  35.4 0.0 copy-start.3
  35.4 16.7 %all_to_all.21 = f32[1376,1,128]{2,1,0:T(1,128)S(1)} all-to-all(f32[1376,1,128]{2,1,0:T(1,128)S(1)} %bitcast.29), channel_id=1, replica_groups=mesh['inst'=32,'span'=2,'rad'=2] {'inst'}, dimensions={0} | all-to-all | bytes 1409024 | tf_op jit(solution)/shard_map/all_to_all | solution.py:521
  52.2 0.0 copy-done.1
  52.2 0.0 copy-done
  52.2 0.0 copy-done.2
  52.2 0.0 copy-done.3
  52.2 2.3 %shard_map.127 = (f32[10,16,512]{2,1,0:T(8,128)}, f32[128,128]{1,0:T(8,128)S(1)}) custom-call(s32[1]{0:T(128)} %bitcast.rad_ref, f32[10,16,512]{2,1,0:T(8,128)S(1)} %get-tuple-element.31.w_ref, f32[1376,128]{1,0:T(8,128)S(1)} %bitcast.28, f32[3,16,128]{2,1,0:T(8,128)S(1)} %get-tuple-element.40.w_edge_ref, f32[48,256]{1,0:T(8,128)S(1)} %get-tuple-element.41.w_halo_ref, ...), custom_call_target="tpu_custom_call" | custom-call | bytes 3000000 | tf_op jit(solution)/shard_map/pallas_call | solution.py:522
  54.4 13.3 %all_to_all.22 = f32[128,1,128]{2,1,0:T(1,128)S(1)} all-to-all(f32[128,1,128]{2,1,0:T(1,128)S(1)} %bitcast.31), channel_id=1, replica_groups=mesh['inst'=32,'span'=2,'rad'=2] {'inst','span','rad'}, dimensions={0} | all-to-all | bytes 131072 | tf_op jit(solution)/shard_map/all_to_all | solution.py:527
  67.7 0.7 shard_map.128
Async XLA Ops:
  1.8 4.1 %collective-permute-start.1 = (f32[40,256]{1,0:T(8,128)S(1)}, f32[40,256]{1,0:T(8,128)S(1)}, u32[]{:S(2)}, u32[]{:S(2)}) collective-permute-start(f32[40,256]{1,0:T(8,128)S(1)} %get-tuple-element.26), channel_id=1, source_target_pairs={{0,1},{1,0},{2,3},{3,2},{4,5},{5,4},{6,7},{7,6},{8,9},{9,8},{10,11... | collective-permute-start | bytes 122888 | tf_op jit(solution)/shard_map/ppermute | solution.py:478
  3.4 2.1 %collective-permute-start = (f32[2,16,128]{2,1,0:T(8,128)S(1)}, f32[2,16,128]{2,1,0:T(8,128)S(1)}, u32[]{:S(2)}, u32[]{:S(2)}) collective-permute-start(f32[2,16,128]{2,1,0:T(8,128)S(1)} %get-tuple-element.25), channel_id=1, source_target_pairs={{0,2},{2,0},{1,3},{3,1},{4,6},{6,4},{5,7},{7,5},{8,10},{10,8},{9,1... | collective-permute-start | bytes 49160 | tf_op jit(solution)/shard_map/ppermute | solution.py:479
  8.8 26.1 %copy-start.4 = (bf16[64,384]{1,0:T(8,128)(2,1)S(1)}, bf16[64,384]{1,0:T(8,128)(2,1)}, u32[]{:S(2)}) copy-start(bf16[64,384]{1,0:T(8,128)(2,1)} %constant.14.clone.table_ref) | copy-start | bytes 147460
  8.8 26.0 %all-to-all-start = ((f32[1376,1,128]{2,1,0:T(1,128)}), f32[1376,1,128]{2,1,0:T(1,128)S(1)}, u32[]{:S(2)}, u32[]{:S(2)}) async-start(f32[1376,1,128]{2,1,0:T(1,128)} %bitcast.9), calls=%async_computation | async-start | bytes 1409024 | tf_op jit(solution)/shard_map/all_to_all | solution.py:515
  19.8 8.0 %collective-permute-start.3 = (f32[48,256]{1,0:T(8,128)S(1)}, f32[48,256]{1,0:T(8,128)S(1)}, u32[]{:S(2)}, u32[]{:S(2)}) collective-permute-start(f32[48,256]{1,0:T(8,128)S(1)} %get-tuple-element.35), channel_id=1, source_target_pairs={{0,1},{1,0},{2,3},{3,2},{4,5},{5,4},{6,7},{7,6},{8,9},{9,8},{10,11... | collective-permute-start | bytes 147464 | tf_op jit(solution)/shard_map/ppermute | solution.py:478
  20.5 1.2 %collective-permute-start.2 = (f32[3,16,128]{2,1,0:T(8,128)S(1)}, f32[3,16,128]{2,1,0:T(8,128)S(1)}, u32[]{:S(2)}, u32[]{:S(2)}) collective-permute-start(f32[3,16,128]{2,1,0:T(8,128)S(1)} %get-tuple-element.34), channel_id=1, source_target_pairs={{0,2},{2,0},{1,3},{3,1},{4,6},{6,4},{5,7},{7,5},{8,10},{10,8},{9,1... | collective-permute-start | bytes 73736 | tf_op jit(solution)/shard_map/ppermute | solution.py:479
  34.9 17.3 %copy-start.1 = (bf16[2,5,5,16,512]{4,3,2,1,0:T(8,128)(2,1)S(1)}, bf16[2,5,5,16,512]{4,3,2,1,0:T(8,128)(2,1)}, u32[]{:S(2)}) copy-start(bf16[2,5,5,16,512]{4,3,2,1,0:T(8,128)(2,1)} %jc_ref.1) | copy-start | bytes 2457604
  35.4 16.8 %copy-start = (bf16[2,5,5,16,512]{4,3,2,1,0:T(8,128)(2,1)S(1)}, bf16[2,5,5,16,512]{4,3,2,1,0:T(8,128)(2,1)}, u32[]{:S(2)}) copy-start(bf16[2,5,5,16,512]{4,3,2,1,0:T(8,128)(2,1)} %jr_ref.1) | copy-start | bytes 2457604
  35.4 16.8 %copy-start.2 = (f32[2,5,16,512]{3,2,1,0:T(8,128)S(1)}, f32[2,5,16,512]{3,2,1,0:T(8,128)}, u32[]{:S(2)}) copy-start(f32[2,5,16,512]{3,2,1,0:T(8,128)} %param.16) | copy-start | bytes 983044
  35.4 16.8 %copy-start.3 = (bf16[2,5,3,1024]{3,0,2,1:T(2,128)(2,1)S(1)}, bf16[2,5,3,1024]{3,0,2,1:T(2,128)(2,1)}, u32[]{:S(2)}) copy-start(bf16[2,5,3,1024]{3,0,2,1:T(2,128)(2,1)} %param.20) | copy-start | bytes 184324

commit v6 on v5

--- a/solution.py
+++ b/solution.py
@@ -147,7 +147,7 @@
     return fix
 
 
-def interior_pass(t, psi_ref, src_ref, jr_ref, jc_ref, dis_ref, step_ref, pad_ref, part_ref):
+def interior_pass(t, psi_ref, src_ref, jr_ref, jc_ref, dis_ref, step_ref, pad_ref, part_ref, first=0):
     for q in range(LT):
         cell = lambda f, qq: psi_ref[t * NF + f, :, lanes(qq)]
         jr = lambda i, j: jr_ref[t, i, j, :, lanes(q)]
@@ -155,7 +155,7 @@
         res = interior(cell, pad_ref, jr, jc, dis_ref[:, lanes(q)], q)
         sigma = step_ref[:, lanes(q)]
         for f in range(NF):
-            part_ref[t * NF + f, :, lanes(q)] = cell(f, q) - sigma * (res[f] - src_ref[t * NF + f, :, lanes(q)])
+            part_ref[t * NF + f - first, :, lanes(q)] = cell(f, q) - sigma * (res[f] - src_ref[t * NF + f, :, lanes(q)])
 
 
 def edge_kernel(rad_ref, psi_hbm, edge_ref, halo_ref, rows_ref, left_ref, right_ref, sem):
@@ -229,12 +229,11 @@
     return jnp.where(lane < 64, a, pltpu.roll(b, 64, 1)), jnp.where(lane < 64, pltpu.roll(a, 64, 1), b)
 
 
-def first_kernel(rad_ref, span_ref, me_ref, dis_hbm, step_hbm, cell_hbm, owner_hbm, local_hbm, psi_hbm, src_hbm, jr_hbm, jc_hbm,
-                 part_ref, psi_ref, jrb_ref, jce_ref, dis_ref, step_ref, sig_ref, ids_ref,
-                 src_ref, jr_ref, jc_ref, pad_ref, cell_ref, owner_ref, local_ref, sem, sem_small):
+def first_kernel(rad_ref, span_ref, dis_hbm, step_hbm, psi_hbm, src_hbm, jr_hbm, jc_hbm,
+                 part_ref, psi_ref, jrb_ref, jce_ref, dis_ref, step_ref, src_ref, jr_ref, jc_ref, pad_ref, sem, sem_small):
     rad = rad_ref[0]
     small = [pltpu.make_async_copy(a, b, sem_small.at[i]) for i, (a, b) in enumerate([
-        (dis_hbm, dis_ref), (step_hbm, step_ref), (cell_hbm, cell_ref), (owner_hbm, owner_ref), (local_hbm, local_ref)])]
+        (dis_hbm, dis_ref), (step_hbm, step_ref)])]
     copies = []
     for t in range(TD):
         tf = pl.ds(t * NF, NF)
@@ -250,17 +249,6 @@
     lane = lax.broadcasted_iota(jnp.int32, (CR, 128), 1)
     for copy in small:
         copy.wait()
-    ids_ref[0:1] = cell_ref[...] % CT
-    ids_ref[1:2] = cell_ref[...] // CT
-    ids_ref[2:3] = owner_ref[...]
-    ids_ref[3:4] = local_ref[...]
-    me = me_ref[0]
-    sig = jnp.zeros((2, 128), F32)
-    for p in range(8):
-        for q in range(LT):
-            here = jnp.concatenate([step_ref[p:p + 1, lanes(q)], step_ref[p + 8:p + 9, lanes(q)]], axis=0)
-            sig = jnp.where(me == 8 * q + p, here, sig)
-    sig_ref[...] = sig
     for t in range(TD):
         for copy in copies[t]:
             copy.wait()
@@ -281,7 +269,10 @@
                 x_hbm, w_ref, w_edge_ref, w_halo_ref, rim_ref, x_ref, src_ref, jr_ref, jc_ref, pad_ref, late_ref, sem, sem_in):
     rad = rad_ref[0]
 
-    late_ref[...] = part_ref[...]
+
+    @pl.when(span_ref[0] != 0)
+    def _():
+        late_ref[...] = part_ref[(TD - 1) * NF:]
 
     @pl.when(span_ref[0] == 0)
     def _():
@@ -293,7 +284,7 @@
         clear_pad(pad_ref)
         for load in loads:
             load.wait()
-        interior_pass(TD - 1, psi_ref, src_ref, jr_ref, jc_ref, dis_ref, step_ref, pad_ref, late_ref)
+        interior_pass(TD - 1, psi_ref, src_ref, jr_ref, jc_ref, dis_ref, step_ref, pad_ref, late_ref, (TD - 1) * NF)
 
     fixes = [corrections(rad, edge_ref, halo_ref, jrb_ref, jce_ref, dis_ref, t) for t in range(TD)]
     rims = [rim_of(lambda q: halo_ref[20 * (q // 2) + 10 * t:20 * (q // 2) + 10 * t + 10, lanes(q % 2)], edge_ref[t])
@@ -308,7 +299,8 @@
         for t in range(TD):
             for f in range(NF):
                 mid = psi_ref[t * NF + f, :, lanes(q)]
-                w = late_ref[t * NF + f, :, lanes(q)] - step_ref[:, lanes(q)] * fixes[t](f, q)
+                before = part_ref[f, :, lanes(q)] if t < TD - 1 else late_ref[f, :, lanes(q)]
+                w = before - step_ref[:, lanes(q)] * fixes[t](f, q)
                 w_ref[t * NF + f, :, lanes(q)] = w
                 for h in range(HB):
                     x_ref[pl.ds(q * GRP + row_of(t, 0, f, h), 8, stride=ROWS), :] = mid[8 * h:8 * h + 8]
@@ -328,7 +320,25 @@
         copy.wait()
 
 
-def label_kernel(ids_ref, pick_ref, label_ref):
+def label_kernel(me_ref, cell_hbm, owner_hbm, local_hbm, step_ref, pick_ref, label_ref, ids_ref, sig_ref, cell_ref, owner_ref,
+                 local_ref, sem):
+    loads = [pltpu.make_async_copy(a, b, sem.at[i]) for i, (a, b) in enumerate(
+        [(cell_hbm, cell_ref), (owner_hbm, owner_ref), (local_hbm, local_ref)])]
+    for load in loads:
+        load.start()
+    for load in loads:
+        load.wait()
+    ids_ref[0:1] = cell_ref[...] % CT
+    ids_ref[1:2] = cell_ref[...] // CT
+    ids_ref[2:3] = owner_ref[...]
+    ids_ref[3:4] = local_ref[...]
+    me = me_ref[0]
+    sig = jnp.zeros((2, 128), F32)
+    for p in range(8):
+        for q in range(LT):
+            here = jnp.concatenate([step_ref[p:p + 1, lanes(q)], step_ref[p + 8:p + 9, lanes(q)]], axis=0)
+            sig = jnp.where(me == 8 * q + p, here, sig)
+    sig_ref[...] = sig
     pick_ref[...] = (lax.broadcasted_iota(jnp.int32, (CT, NODES), 0) == ids_ref[0:1]).astype(F32).astype(BF)
     label_ref[...] = (lax.broadcasted_iota(jnp.int32, (128, NODES), 0) % VAR_DEV == ids_ref[3:4]).astype(F32).astype(BF)
 
@@ -422,10 +432,12 @@
     mask = (lax.broadcasted_iota(jnp.int32, (CR, NODES), 0) == ids_ref[1:2]).astype(F32)
     acc = [jnp.zeros((CR, NODES), F32) for _ in range(3)]
     weights = [sd_ref[m].astype(F32) for m in range(3 * NF)]
-    for t in range(TD):
-        whole = psi_ref[t * NF:(t + 1) * NF].reshape(NF * CR, CT)
-        got = jnp.dot(jnp.concatenate(split(whole), axis=0), pick, preferred_element_type=F32)
-        value = got[:NF * CR] + got[NF * CR:2 * NF * CR] + got[2 * NF * CR:]
+    size = TD * NF * CR
+    whole = psi_ref[...].reshape(size, CT)
+    got = jnp.dot(jnp.concatenate(split(whole), axis=0), pick, preferred_element_type=F32)
+    got = got[:size] + got[size:2 * size] + got[2 * size:]
+    for t in range(TD):
+        value = got[t * NF * CR:(t + 1) * NF * CR]
         for f in range(NF):
             here = value[f * CR:(f + 1) * CR]
             for k in range(3):
@@ -439,7 +451,9 @@
     stack = jnp.concatenate(parts, axis=0)
     label = label_ref[...]
     dims = (((1,), (1,)), ((), ()))
-    total = sum(lax.dot_general(piece, label, dims, preferred_element_type=F32) for piece in split(stack))
+    total = lax.dot_general(jnp.concatenate(split(stack), axis=0), label, dims, preferred_element_type=F32)
+    count = stack.shape[0]
+    total = total[:count] + total[count:2 * count] + total[2 * count:]
     lane = lax.broadcasted_iota(jnp.int32, (1, 128), 1)
     line = []
     for s in range(2):
@@ -498,23 +512,25 @@
         edge_kernel, [SM, HM], [(f32(TD, CR, 128), VM), (f32(40, HALF), VM)],
         [VM((n, 8, CT), F32), VM((n, CR, 128), F32), VM((n, CR, 128), F32), dma((3,))])(rad, held[5])
     edge0, halo0 = swap_halos(edge0, halo0)
-    part, psi, jrb, jce, dis, step, sig, ids = call(
-        first_kernel, [SM, SM, SM] + [HM] * 9,
-        [(full, VM), (full, VM), (f32(n, NF, CT), VM), (jax.ShapeDtypeStruct((n, NF, CR, 128), BF), VM), (flat, VM), (flat, VM),
-         (f32(2, 128), VM), (jax.ShapeDtypeStruct((8, NODES), jnp.int32), VM)],
-        [VM((n, CR, CT), F32), VM(jac_rad.shape, BF), VM(jac_circ.shape, BF), pad] + [VM(line, jnp.int32)] * 3 + [dma((TD, 4)), dma((5,))],
-        micros=3)(rad, span, me, *held)
+    part, psi, jrb, jce, dis, step = call(
+        first_kernel, [SM, SM] + [HM] * 6,
+        [(full, VM), (full, VM), (f32(n, NF, CT), VM), (jax.ShapeDtypeStruct((n, NF, CR, 128), BF), VM), (flat, VM), (flat, VM)],
+        [VM((n, CR, CT), F32), VM(jac_rad.shape, BF), VM(jac_circ.shape, BF), pad, dma((TD, 4)), dma((2,))],
+        micros=3)(rad, span, held[0], held[1], *held[5:])
     rim = VM((96, 128), F32)
     swapped = [(f32(TD + 1, CR, 128), VM), (f32(48, HALF), VM)]
     x, w, w_edge, w_halo = call(
         send_kernel, [SM, SM] + [VM] * 8 + [HM] * 3, [(f32(32 * ROWS, 128), HM), (full, VM)] + swapped,
-        [rim, VM((32 * ROWS, 128), F32), VM((n, CR, CT), F32), VM(jac_rad.shape, BF), VM(jac_circ.shape, BF), pad, VM((n, CR, CT), F32),
+        [rim, VM((32 * ROWS, 128), F32), VM((n, CR, CT), F32), VM(jac_rad.shape, BF), VM(jac_circ.shape, BF), pad, VM((NF, CR, CT), F32),
          dma((LT,)), dma((3,))])(
         rad, span, psi, part, edge0, halo0, jrb, jce, dis, step, *held[6:])
     w_edge, w_halo = swap_halos(w_edge, w_halo)
     y = lax.all_to_all(x.reshape(32 * ROWS, 1, 128), "inst", 0, 0, tiled=True).reshape(32 * ROWS, 128)
     bf16 = lambda *shape: (jax.ShapeDtypeStruct(shape, BF), VM)
-    pick, label = call(label_kernel, [VM], [bf16(CT, NODES), bf16(128, NODES)])(ids)
+    pick, label, ids, sig = call(
+        label_kernel, [SM] + [HM] * 3 + [VM],
+        [bf16(CT, NODES), bf16(128, NODES), (jax.ShapeDtypeStruct((8, NODES), jnp.int32), VM), (f32(2, 128), VM)],
+        [VM(line, jnp.int32)] * 3 + [dma((3,))])(me, *held[2:5], step)
     v, w_edge, w_halo = call(
         time_kernel, [VM] * 5 + [pl.ANY] * 2, [(f32(32 * ROWS, 128), VM)] + swapped)(
         jnp.asarray(spectral_blocks()), sig, y, w_edge, w_halo, pick, label)

time: 69.5 us -> 69.1 us (level)
  waiting for transfers between devices: 14.4 us -> 13.3 us
  Pallas kernels: 9.89 us -> 10.7 us
    pallas_call x2, Pallas kernels: 2.36 us -> 3.39 us  [the longest x1 2.11 us: body(): call(first_kernel, [SM, SM] + [HM] * 6, [(full, VM), (full, VM), (f32(n,...]
    ppermute x2, waiting for transfers between devices: 0.96 us -> 0.01 us  [swap_halos(): edge = lax.ppermute(edge, 'span', SWAP)]
  transfers between devices with their start and end apart: 5 -> 5, of which waited for: 4 -> 3; matrix products, arithmetic and copies ran while one was open for 0% -> 0% of each run, Pallas kernels for 3% -> 5%
where the time goes in v6:
time: 69.1 us; the launch traced here: 68 us
  blocking collectives  30 us (43%)
  waiting for transfers between devices  13.3 us (19%)
  starting transfers between devices  13.2 us (19%)
  Pallas kernels  10.7 us (15%)
  between operations  0.75 us (1%)
    all_to_all x1, blocking collectives, body(): lax.all_to_all(v.reshape(32 * ROWS, 1, 128), 'inst', 0, 0, tiled=True)  16.7 us
    all_to_all x1, blocking collectives, body(): got = lax.all_to_all(parts, ALL, 0, 0, tiled=True)  13.3 us
    all_to_all x1, starting transfers between devices, body(): lax.all_to_all(x.reshape(32 * ROWS, 1, 128), 'inst', 0, 0, tiled=True)  10.9 us
    all_to_all x1, waiting for transfers between devices, body(): lax.all_to_all(x.reshape(32 * ROWS, 1, 128), 'inst', 0, 0, tiled=True)  6.99 us
    ppermute x2, waiting for transfers between devices, swap_halos(): halo = lax.ppermute(halo, 'rad', SWAP)  6.32 us
    pallas_call x1, Pallas kernels, body(): call(send_kernel, [SM, SM] + [VM] * 8 + [HM] * 3, [(f32(32 * ROWS, 128),...  2.93 us
    ppermute x2, starting transfers between devices, swap_halos(): halo = lax.ppermute(halo, 'rad', SWAP)  2.33 us
    pallas_call x1, Pallas kernels, body(): call(first_kernel, [SM, SM] + [HM] * 6, [(full, VM), (full, VM), (f32(n,...  2.11 us
  transfers between devices with their start and end apart: 5, of which 3 were waited for; matrix products, arithmetic and copies ran while one was open for 0% of the time, Pallas kernels for 5%

profile of v6, /device:TPU:0, one launch (start us, length us, event | category | flops | bytes accessed | tf_op | source)
XLA Modules:
  0.0 68.0 jit_solution(1780744739230106587)
XLA Ops:
  0.6 1.1 %shard_map.123 = (f32[2,16,128]{2,1,0:T(8,128)S(1)}, f32[40,256]{1,0:T(8,128)S(1)}) custom-call(s32[1]{0:T(128)} %bitcast.rad_ref, f32[10,16,512]{2,1,0:T(8,128)} %bitcast.33), custom_call_target="tpu_custom_call" | custom-call | bytes 3000000 | tf_op jit(solution)/shard_map/pallas_call | solution.py:511
  1.8 1.7 %collective-permute-start.1 = (f32[40,256]{1,0:T(8,128)S(1)}, f32[40,256]{1,0:T(8,128)S(1)}, u32[]{:S(2)}, u32[]{:S(2)}) collective-permute-start(f32[40,256]{1,0:T(8,128)S(1)} %get-tuple-element.26), channel_id=1, source_target_pairs={{0,1},{1,0},{2,3},{3,2},{4,5},{5,4},{6,7},{7,6},{8,9},{9,8},{10,11... | collective-permute-start | bytes 122888 | tf_op jit(solution)/shard_map/ppermute | solution.py:492
  3.4 0.0 collective-permute-start
  3.4 2.1 %shard_map.122 = (f32[10,16,512]{2,1,0:T(8,128)S(1)}, f32[10,16,512]{2,1,0:T(8,128)S(1)}, f32[10,5,512]{2,1,0:T(8,128)S(1)}, bf16[10,5,16,128]{3,2,1,0:T(8,128)(...) custom-call(s32[1]{0:T(128)} %bitcast.rad_ref, s32[1]{0:T(128)} %bitcast.1.span_ref, f32[16,512]{1,0:T(8,128)} %dis_hbm.1, ...), custom_call_target="tpu_custom_call" | custom-call | bytes 9000000 | tf_op jit(solution)/shard_map/pallas_call | solution.py:515
  5.5 0.0 collective-permute-done.edge_ref
  5.6 0.3 collective-permute-done.1.halo_ref
  5.8 2.9 %shard_map.124 = (f32[1376,128]{1,0:T(8,128)}, f32[10,16,512]{2,1,0:T(8,128)S(1)}, f32[3,16,128]{2,1,0:T(8,128)S(1)}, f32[48,256]{1,0:T(8,128)S(1)}) custom-call(s32[1]{0:T(128)} %bitcast.rad_ref, s32[1]{0:T(128)} %bitcast.1.span_ref, f32[10,16,512]{2,1,0:T(8,128)S(1)} %get-tuple-element.23.psi_ref, f32[10,16,512]{2,1,0:T(8,128)S(1)} %get-tuple-element.24.part_ref, ...), custom_call_target="tpu_custom_call" | custom-call | bytes 3000000 | tf_op jit(solution)/shard_map/pallas_call | solution.py:522
  8.8 10.9 %all-to-all-start = ((f32[1376,1,128]{2,1,0:T(1,128)}), f32[1376,1,128]{2,1,0:T(1,128)S(1)}, u32[]{:S(2)}, u32[]{:S(2)}) async-start(f32[1376,1,128]{2,1,0:T(1,128)} %bitcast.9), calls=%async_computation | async-start | bytes 1409024 | tf_op jit(solution)/shard_map/all_to_all | solution.py:528
  19.7 0.0 copy-start.4
  19.7 0.7 collective-permute-start.3
  20.4 0.0 collective-permute-start.2
  20.4 1.3 %shard_map.125 = (bf16[512,1024]{1,0:T(8,128)(2,1)S(1)}, bf16[128,1024]{1,0:T(8,128)(2,1)S(1)}, s32[8,1024]{1,0:T(8,128)S(1)}, f32[2,128]{1,0:T(2,128)S(1)}) custom-call(s32[1]{0:T(128)} %bitcast.4.me_ref, s32[1,1024]{1,0:T(1,128)} %bitcast.35, s32[1,1024]{1,0:T(1,128)} %bitcast.36, s32[1,1024]{1,0:T(1,128)} %bitcast.37, ...), custom_call_target="tpu_custom_call" | custom-call | bytes 3000000 | tf_op jit(solution)/shard_map/pallas_call | solution.py:530
  21.7 0.0 collective-permute-done.2.edge_ref
  21.7 6.0 %collective-permute-done.3.halo_ref = f32[48,256]{1,0:T(8,128)S(1)} collective-permute-done((f32[48,256]{1,0:T(8,128)S(1)}, f32[48,256]{1,0:T(8,128)S(1)}, u32[]{:S(2)}, u32[]{:S(2)}) %collective-permute-start.3) | collective-permute-done | bytes 49184 | tf_op jit(solution)/shard_map/ppermute | solution.py:492
  27.7 7.0 %all-to-all-done = f32[1376,1,128]{2,1,0:T(1,128)S(1)} async-done(((f32[1376,1,128]{2,1,0:T(1,128)}), f32[1376,1,128]{2,1,0:T(1,128)S(1)}, u32[]{:S(2)}, u32[]{:S(2)}) %all-to-all-start) | async-done | bytes 704544 | tf_op jit(solution)/shard_map/all_to_all | solution.py:528
  34.7 0.0 copy-done.4
  34.7 0.0 copy-start.1
  34.7 0.5 shard_map.126
  35.2 0.0 copy-start
  35.2 0.0 copy-start.2
  35.2 0.0 copy-start.3
  35.3 16.7 %all_to_all.21 = f32[1376,1,128]{2,1,0:T(1,128)S(1)} all-to-all(f32[1376,1,128]{2,1,0:T(1,128)S(1)} %bitcast.29), channel_id=1, replica_groups=mesh['inst'=32,'span'=2,'rad'=2] {'inst'}, dimensions={0} | all-to-all | bytes 1409024 | tf_op jit(solution)/shard_map/all_to_all | solution.py:537
  52.0 0.0 copy-done.1
  52.0 0.0 copy-done
  52.0 0.0 copy-done.2
  52.0 0.0 copy-done.3
  52.0 2.0 %shard_map.127 = (f32[10,16,512]{2,1,0:T(8,128)}, f32[128,128]{1,0:T(8,128)S(1)}) custom-call(s32[1]{0:T(128)} %bitcast.rad_ref, f32[10,16,512]{2,1,0:T(8,128)S(1)} %get-tuple-element.31.w_ref, f32[1376,128]{1,0:T(8,128)S(1)} %bitcast.28, f32[3,16,128]{2,1,0:T(8,128)S(1)} %get-tuple-element.39.w_edge_ref, f32[48,256]{1,0:T(8,128)S(1)} %get-tuple-element.40.w_halo_ref, ...), custom_call_target="tpu_custom_call" | custom-call | bytes 3000000 | tf_op jit(solution)/shard_map/pallas_call | solution.py:538
  54.0 13.3 %all_to_all.22 = f32[128,1,128]{2,1,0:T(1,128)S(1)} all-to-all(f32[128,1,128]{2,1,0:T(1,128)S(1)} %bitcast.31), channel_id=1, replica_groups=mesh['inst'=32,'span'=2,'rad'=2] {'inst','span','rad'}, dimensions={0} | all-to-all | bytes 131072 | tf_op jit(solution)/shard_map/all_to_all | solution.py:543
  67.3 0.7 shard_map.128
Async XLA Ops:
  1.8 4.1 %collective-permute-start.1 = (f32[40,256]{1,0:T(8,128)S(1)}, f32[40,256]{1,0:T(8,128)S(1)}, u32[]{:S(2)}, u32[]{:S(2)}) collective-permute-start(f32[40,256]{1,0:T(8,128)S(1)} %get-tuple-element.26), channel_id=1, source_target_pairs={{0,1},{1,0},{2,3},{3,2},{4,5},{5,4},{6,7},{7,6},{8,9},{9,8},{10,11... | collective-permute-start | bytes 122888 | tf_op jit(solution)/shard_map/ppermute | solution.py:492
  3.4 2.1 %collective-permute-start = (f32[2,16,128]{2,1,0:T(8,128)S(1)}, f32[2,16,128]{2,1,0:T(8,128)S(1)}, u32[]{:S(2)}, u32[]{:S(2)}) collective-permute-start(f32[2,16,128]{2,1,0:T(8,128)S(1)} %get-tuple-element.25), channel_id=1, source_target_pairs={{0,2},{2,0},{1,3},{3,1},{4,6},{6,4},{5,7},{7,5},{8,10},{10,8},{9,1... | collective-permute-start | bytes 49160 | tf_op jit(solution)/shard_map/ppermute | solution.py:493
  8.8 25.9 %all-to-all-start = ((f32[1376,1,128]{2,1,0:T(1,128)}), f32[1376,1,128]{2,1,0:T(1,128)S(1)}, u32[]{:S(2)}, u32[]{:S(2)}) async-start(f32[1376,1,128]{2,1,0:T(1,128)} %bitcast.9), calls=%async_computation | async-start | bytes 1409024 | tf_op jit(solution)/shard_map/all_to_all | solution.py:528
  19.7 15.0 %copy-start.4 = (bf16[64,384]{1,0:T(8,128)(2,1)S(1)}, bf16[64,384]{1,0:T(8,128)(2,1)}, u32[]{:S(2)}) copy-start(bf16[64,384]{1,0:T(8,128)(2,1)} %constant.14.clone.table_ref) | copy-start | bytes 147460
  19.7 8.0 %collective-permute-start.3 = (f32[48,256]{1,0:T(8,128)S(1)}, f32[48,256]{1,0:T(8,128)S(1)}, u32[]{:S(2)}, u32[]{:S(2)}) collective-permute-start(f32[48,256]{1,0:T(8,128)S(1)} %get-tuple-element.35), channel_id=1, source_target_pairs={{0,1},{1,0},{2,3},{3,2},{4,5},{5,4},{6,7},{7,6},{8,9},{9,8},{10,11... | collective-permute-start | bytes 147464 | tf_op jit(solution)/shard_map/ppermute | solution.py:492
  20.4 1.3 %collective-permute-start.2 = (f32[3,16,128]{2,1,0:T(8,128)S(1)}, f32[3,16,128]{2,1,0:T(8,128)S(1)}, u32[]{:S(2)}, u32[]{:S(2)}) collective-permute-start(f32[3,16,128]{2,1,0:T(8,128)S(1)} %get-tuple-element.34), channel_id=1, source_target_pairs={{0,2},{2,0},{1,3},{3,1},{4,6},{6,4},{5,7},{7,5},{8,10},{10,8},{9,1... | collective-permute-start | bytes 73736 | tf_op jit(solution)/shard_map/ppermute | solution.py:493
  34.7 17.3 %copy-start.1 = (bf16[2,5,5,16,512]{4,3,2,1,0:T(8,128)(2,1)S(1)}, bf16[2,5,5,16,512]{4,3,2,1,0:T(8,128)(2,1)}, u32[]{:S(2)}) copy-start(bf16[2,5,5,16,512]{4,3,2,1,0:T(8,128)(2,1)} %jc_ref.1) | copy-start | bytes 2457604
  35.2 16.8 %copy-start = (bf16[2,5,5,16,512]{4,3,2,1,0:T(8,128)(2,1)S(1)}, bf16[2,5,5,16,512]{4,3,2,1,0:T(8,128)(2,1)}, u32[]{:S(2)}) copy-start(bf16[2,5,5,16,512]{4,3,2,1,0:T(8,128)(2,1)} %jr_ref.1) | copy-start | bytes 2457604
  35.2 16.8 %copy-start.2 = (f32[2,5,16,512]{3,2,1,0:T(8,128)S(1)}, f32[2,5,16,512]{3,2,1,0:T(8,128)}, u32[]{:S(2)}) copy-start(f32[2,5,16,512]{3,2,1,0:T(8,128)} %param.16) | copy-start | bytes 983044
  35.2 16.8 %copy-start.3 = (bf16[2,5,3,1024]{3,0,2,1:T(2,128)(2,1)S(1)}, bf16[2,5,3,1024]{3,0,2,1:T(2,128)(2,1)}, u32[]{:S(2)}) copy-start(bf16[2,5,3,1024]{3,0,2,1:T(2,128)(2,1)} %param.20) | copy-start | bytes 184324

commit v7 on v6

--- a/solution.py
+++ b/solution.py
@@ -38,8 +38,8 @@
     for _ in range(3):
         pieces.append(apply.astype(BF))
         apply = apply - pieces[-1].astype(np.float32)
-    high, mid, low = pieces
-    return np.concatenate([high, high, mid, mid, high, low], axis=1)
+    high, mid, _ = pieces
+    return np.concatenate([high, high, mid, mid, high], axis=1)
 
 
 def split(x):
@@ -52,7 +52,7 @@
 
 def pair_up(x):
     high, mid, low = split(x)
-    return jnp.concatenate([high, mid, high, mid, low, high], axis=0)
+    return jnp.concatenate([high, mid, high, mid, low], axis=0)
 
 
 def row_of(t, what, f, h):
@@ -530,7 +530,7 @@
     pick, label, ids, sig = call(
         label_kernel, [SM] + [HM] * 3 + [VM],
         [bf16(CT, NODES), bf16(128, NODES), (jax.ShapeDtypeStruct((8, NODES), jnp.int32), VM), (f32(2, 128), VM)],
-        [VM(line, jnp.int32)] * 3 + [dma((3,))])(me, *held[2:5], step)
+        [VM(line, jnp.int32)] * 3 + [dma((3,))], micros=40)(me, *held[2:5], step)
     v, w_edge, w_halo = call(
         time_kernel, [VM] * 5 + [pl.ANY] * 2, [(f32(32 * ROWS, 128), VM)] + swapped)(
         jnp.asarray(spectral_blocks()), sig, y, w_edge, w_halo, pick, label)

time: 69.1 us -> 69 us (level)
  no operation moved by 1% of the time
where the time goes in v7:
time: 69 us; the launch traced here: 67.9 us
  blocking collectives  30 us (43%)
  waiting for transfers between devices  13.3 us (19%)
  starting transfers between devices  13.2 us (19%)
  Pallas kernels  10.6 us (15%)
  between operations  0.75 us (1%)
    all_to_all x1, blocking collectives, body(): lax.all_to_all(v.reshape(32 * ROWS, 1, 128), 'inst', 0, 0, tiled=True)  16.7 us
    all_to_all x1, blocking collectives, body(): got = lax.all_to_all(parts, ALL, 0, 0, tiled=True)  13.3 us
    all_to_all x1, starting transfers between devices, body(): lax.all_to_all(x.reshape(32 * ROWS, 1, 128), 'inst', 0, 0, tiled=True)  10.9 us
    all_to_all x1, waiting for transfers between devices, body(): lax.all_to_all(x.reshape(32 * ROWS, 1, 128), 'inst', 0, 0, tiled=True)  6.99 us
    ppermute x2, waiting for transfers between devices, swap_halos(): halo = lax.ppermute(halo, 'rad', SWAP)  6.32 us
    pallas_call x1, Pallas kernels, body(): call(send_kernel, [SM, SM] + [VM] * 8 + [HM] * 3, [(f32(32 * ROWS, 128),...  2.93 us
    ppermute x2, starting transfers between devices, swap_halos(): halo = lax.ppermute(halo, 'rad', SWAP)  2.33 us
    pallas_call x1, Pallas kernels, body(): call(first_kernel, [SM, SM] + [HM] * 6, [(full, VM), (full, VM), (f32(n,...  2.11 us
  transfers between devices with their start and end apart: 5, of which 3 were waited for; matrix products, arithmetic and copies ran while one was open for 0% of the time, Pallas kernels for 5%

profile of v7, /device:TPU:0, one launch (start us, length us, event | category | flops | bytes accessed | tf_op | source)
XLA Modules:
  0.0 67.9 jit_solution(2771709699993474706)
XLA Ops:
  0.6 1.1 %shard_map.123 = (f32[2,16,128]{2,1,0:T(8,128)S(1)}, f32[40,256]{1,0:T(8,128)S(1)}) custom-call(s32[1]{0:T(128)} %bitcast.rad_ref, f32[10,16,512]{2,1,0:T(8,128)} %bitcast.33), custom_call_target="tpu_custom_call" | custom-call | bytes 3000000 | tf_op jit(solution)/shard_map/pallas_call | solution.py:511
  1.8 1.7 %collective-permute-start.1 = (f32[40,256]{1,0:T(8,128)S(1)}, f32[40,256]{1,0:T(8,128)S(1)}, u32[]{:S(2)}, u32[]{:S(2)}) collective-permute-start(f32[40,256]{1,0:T(8,128)S(1)} %get-tuple-element.26), channel_id=1, source_target_pairs={{0,1},{1,0},{2,3},{3,2},{4,5},{5,4},{6,7},{7,6},{8,9},{9,8},{10,11... | collective-permute-start | bytes 122888 | tf_op jit(solution)/shard_map/ppermute | solution.py:492
  3.4 0.0 collective-permute-start
  3.4 2.1 %shard_map.122 = (f32[10,16,512]{2,1,0:T(8,128)S(1)}, f32[10,16,512]{2,1,0:T(8,128)S(1)}, f32[10,5,512]{2,1,0:T(8,128)S(1)}, bf16[10,5,16,128]{3,2,1,0:T(8,128)(...) custom-call(s32[1]{0:T(128)} %bitcast.rad_ref, s32[1]{0:T(128)} %bitcast.1.span_ref, f32[16,512]{1,0:T(8,128)} %dis_hbm.1, ...), custom_call_target="tpu_custom_call" | custom-call | bytes 9000000 | tf_op jit(solution)/shard_map/pallas_call | solution.py:515
  5.5 0.0 collective-permute-done.edge_ref
  5.6 0.3 collective-permute-done.1.halo_ref
  5.8 2.9 %shard_map.124 = (f32[1376,128]{1,0:T(8,128)}, f32[10,16,512]{2,1,0:T(8,128)S(1)}, f32[3,16,128]{2,1,0:T(8,128)S(1)}, f32[48,256]{1,0:T(8,128)S(1)}) custom-call(s32[1]{0:T(128)} %bitcast.rad_ref, s32[1]{0:T(128)} %bitcast.1.span_ref, f32[10,16,512]{2,1,0:T(8,128)S(1)} %get-tuple-element.23.psi_ref, f32[10,16,512]{2,1,0:T(8,128)S(1)} %get-tuple-element.24.part_ref, ...), custom_call_target="tpu_custom_call" | custom-call | bytes 3000000 | tf_op jit(solution)/shard_map/pallas_call | solution.py:522
  8.8 10.9 %all-to-all-start = ((f32[1376,1,128]{2,1,0:T(1,128)}), f32[1376,1,128]{2,1,0:T(1,128)S(1)}, u32[]{:S(2)}, u32[]{:S(2)}) async-start(f32[1376,1,128]{2,1,0:T(1,128)} %bitcast.9), calls=%async_computation | async-start | bytes 1409024 | tf_op jit(solution)/shard_map/all_to_all | solution.py:528
  19.7 0.0 copy-start.4
  19.7 0.7 collective-permute-start.3
  20.4 0.0 collective-permute-start.2
  20.4 1.3 %shard_map.125 = (bf16[512,1024]{1,0:T(8,128)(2,1)S(1)}, bf16[128,1024]{1,0:T(8,128)(2,1)S(1)}, s32[8,1024]{1,0:T(8,128)S(1)}, f32[2,128]{1,0:T(2,128)S(1)}) custom-call(s32[1]{0:T(128)} %bitcast.4.me_ref, s32[1,1024]{1,0:T(1,128)} %bitcast.35, s32[1,1024]{1,0:T(1,128)} %bitcast.36, s32[1,1024]{1,0:T(1,128)} %bitcast.37, ...), custom_call_target="tpu_custom_call" | custom-call | bytes 120000000 | tf_op jit(solution)/shard_map/pallas_call | solution.py:530
  21.7 0.0 collective-permute-done.2.edge_ref
  21.7 6.0 %collective-permute-done.3.halo_ref = f32[48,256]{1,0:T(8,128)S(1)} collective-permute-done((f32[48,256]{1,0:T(8,128)S(1)}, f32[48,256]{1,0:T(8,128)S(1)}, u32[]{:S(2)}, u32[]{:S(2)}) %collective-permute-start.3) | collective-permute-done | bytes 49184 | tf_op jit(solution)/shard_map/ppermute | solution.py:492
  27.7 7.0 %all-to-all-done = f32[1376,1,128]{2,1,0:T(1,128)S(1)} async-done(((f32[1376,1,128]{2,1,0:T(1,128)}), f32[1376,1,128]{2,1,0:T(1,128)S(1)}, u32[]{:S(2)}, u32[]{:S(2)}) %all-to-all-start) | async-done | bytes 704544 | tf_op jit(solution)/shard_map/all_to_all | solution.py:528
  34.7 0.0 copy-done.4
  34.7 0.0 copy-start.1
  34.7 0.5 shard_map.126
  35.2 0.0 copy-start
  35.2 0.0 copy-start.2
  35.2 0.0 copy-start.3
  35.2 16.7 %all_to_all.21 = f32[1376,1,128]{2,1,0:T(1,128)S(1)} all-to-all(f32[1376,1,128]{2,1,0:T(1,128)S(1)} %bitcast.29), channel_id=1, replica_groups=mesh['inst'=32,'span'=2,'rad'=2] {'inst'}, dimensions={0} | all-to-all | bytes 1409024 | tf_op jit(solution)/shard_map/all_to_all | solution.py:537
  51.9 0.0 copy-done.1
  51.9 0.0 copy-done
  51.9 0.0 copy-done.2
  51.9 0.0 copy-done.3
  51.9 2.0 %shard_map.127 = (f32[10,16,512]{2,1,0:T(8,128)}, f32[128,128]{1,0:T(8,128)S(1)}) custom-call(s32[1]{0:T(128)} %bitcast.rad_ref, f32[10,16,512]{2,1,0:T(8,128)S(1)} %get-tuple-element.31.w_ref, f32[1376,128]{1,0:T(8,128)S(1)} %bitcast.28, f32[3,16,128]{2,1,0:T(8,128)S(1)} %get-tuple-element.39.w_edge_ref, f32[48,256]{1,0:T(8,128)S(1)} %get-tuple-element.40.w_halo_ref, ...), custom_call_target="tpu_custom_call" | custom-call | bytes 3000000 | tf_op jit(solution)/shard_map/pallas_call | solution.py:538
  54.0 13.3 %all_to_all.22 = f32[128,1,128]{2,1,0:T(1,128)S(1)} all-to-all(f32[128,1,128]{2,1,0:T(1,128)S(1)} %bitcast.31), channel_id=1, replica_groups=mesh['inst'=32,'span'=2,'rad'=2] {'inst','span','rad'}, dimensions={0} | all-to-all | bytes 131072 | tf_op jit(solution)/shard_map/all_to_all | solution.py:543
  67.2 0.7 shard_map.128
Async XLA Ops:
  1.8 4.1 %collective-permute-start.1 = (f32[40,256]{1,0:T(8,128)S(1)}, f32[40,256]{1,0:T(8,128)S(1)}, u32[]{:S(2)}, u32[]{:S(2)}) collective-permute-start(f32[40,256]{1,0:T(8,128)S(1)} %get-tuple-element.26), channel_id=1, source_target_pairs={{0,1},{1,0},{2,3},{3,2},{4,5},{5,4},{6,7},{7,6},{8,9},{9,8},{10,11... | collective-permute-start | bytes 122888 | tf_op jit(solution)/shard_map/ppermute | solution.py:492
  3.4 2.1 %collective-permute-start = (f32[2,16,128]{2,1,0:T(8,128)S(1)}, f32[2,16,128]{2,1,0:T(8,128)S(1)}, u32[]{:S(2)}, u32[]{:S(2)}) collective-permute-start(f32[2,16,128]{2,1,0:T(8,128)S(1)} %get-tuple-element.25), channel_id=1, source_target_pairs={{0,2},{2,0},{1,3},{3,1},{4,6},{6,4},{5,7},{7,5},{8,10},{10,8},{9,1... | collective-permute-start | bytes 49160 | tf_op jit(solution)/shard_map/ppermute | solution.py:493
  8.8 25.9 %all-to-all-start = ((f32[1376,1,128]{2,1,0:T(1,128)}), f32[1376,1,128]{2,1,0:T(1,128)S(1)}, u32[]{:S(2)}, u32[]{:S(2)}) async-start(f32[1376,1,128]{2,1,0:T(1,128)} %bitcast.9), calls=%async_computation | async-start | bytes 1409024 | tf_op jit(solution)/shard_map/all_to_all | solution.py:528
  19.7 15.0 %copy-start.4 = (bf16[64,320]{1,0:T(8,128)(2,1)S(1)}, bf16[64,320]{1,0:T(8,128)(2,1)}, u32[]{:S(2)}) copy-start(bf16[64,320]{1,0:T(8,128)(2,1)} %constant.14.clone.table_ref) | copy-start | bytes 122884
  19.7 8.0 %collective-permute-start.3 = (f32[48,256]{1,0:T(8,128)S(1)}, f32[48,256]{1,0:T(8,128)S(1)}, u32[]{:S(2)}, u32[]{:S(2)}) collective-permute-start(f32[48,256]{1,0:T(8,128)S(1)} %get-tuple-element.35), channel_id=1, source_target_pairs={{0,1},{1,0},{2,3},{3,2},{4,5},{5,4},{6,7},{7,6},{8,9},{9,8},{10,11... | collective-permute-start | bytes 147464 | tf_op jit(solution)/shard_map/ppermute | solution.py:492
  20.4 1.3 %collective-permute-start.2 = (f32[3,16,128]{2,1,0:T(8,128)S(1)}, f32[3,16,128]{2,1,0:T(8,128)S(1)}, u32[]{:S(2)}, u32[]{:S(2)}) collective-permute-start(f32[3,16,128]{2,1,0:T(8,128)S(1)} %get-tuple-element.34), channel_id=1, source_target_pairs={{0,2},{2,0},{1,3},{3,1},{4,6},{6,4},{5,7},{7,5},{8,10},{10,8},{9,1... | collective-permute-start | bytes 73736 | tf_op jit(solution)/shard_map/ppermute | solution.py:493
  34.7 17.2 %copy-start.1 = (bf16[2,5,5,16,512]{4,3,2,1,0:T(8,128)(2,1)S(1)}, bf16[2,5,5,16,512]{4,3,2,1,0:T(8,128)(2,1)}, u32[]{:S(2)}) copy-start(bf16[2,5,5,16,512]{4,3,2,1,0:T(8,128)(2,1)} %jc_ref.1) | copy-start | bytes 2457604
  35.2 16.8 %copy-start = (bf16[2,5,5,16,512]{4,3,2,1,0:T(8,128)(2,1)S(1)}, bf16[2,5,5,16,512]{4,3,2,1,0:T(8,128)(2,1)}, u32[]{:S(2)}) copy-start(bf16[2,5,5,16,512]{4,3,2,1,0:T(8,128)(2,1)} %jr_ref.1) | copy-start | bytes 2457604
  35.2 16.8 %copy-start.2 = (f32[2,5,16,512]{3,2,1,0:T(8,128)S(1)}, f32[2,5,16,512]{3,2,1,0:T(8,128)}, u32[]{:S(2)}) copy-start(f32[2,5,16,512]{3,2,1,0:T(8,128)} %param.16) | copy-start | bytes 983044
  35.2 16.8 %copy-start.3 = (bf16[2,5,3,1024]{3,0,2,1:T(2,128)(2,1)S(1)}, bf16[2,5,3,1024]{3,0,2,1:T(2,128)(2,1)}, u32[]{:S(2)}) copy-start(bf16[2,5,3,1024]{3,0,2,1:T(2,128)(2,1)} %param.20) | copy-start | bytes 184324

commit v8 on v7

--- a/solution.py
+++ b/solution.py
@@ -343,10 +343,13 @@
     label_ref[...] = (lax.broadcasted_iota(jnp.int32, (128, NODES), 0) % VAR_DEV == ids_ref[3:4]).astype(F32).astype(BF)
 
 
-def total_kernel(got_ref, sens_ref):
+def total_kernel(got_ref, sens_hbm, sens_ref, sem):
     line = jnp.sum(got_ref[...], axis=0, keepdims=True)
     for k in range(3):
         sens_ref[k:k + 1, :] = pltpu.roll(line, (128 - VAR_DEV * k) % 128, 1)[:, :VAR_DEV]
+    copy = pltpu.make_async_copy(sens_ref, sens_hbm, sem)
+    copy.start()
+    copy.wait()
 
 
 def time_kernel(table_ref, sig_ref, y_ref, edge_ref, halo_ref, pick_ref, label_ref, v_ref, edge_out_ref, halo_out_ref):
@@ -541,7 +544,7 @@
         rad, w, u, w_edge, w_halo, jac_rad, jac_circ, jrb, jce, dis, step, src, ids, pick, label,
         shape_deriv.transpose(1, 2, 0, 3).reshape(3 * NF, TD, NODES))
     got = lax.all_to_all(parts, ALL, 0, 0, tiled=True)
-    sens, = call(total_kernel, [VM], [(f32(3, VAR_DEV), VM)])(got)
+    sens, = call(total_kernel, [VM], [(f32(3, VAR_DEV), HM)], [VM((3, VAR_DEV), F32), dma])(got)
     return psi2.reshape(TD, NF, CR, CT), sens
 
 

time: 69 us -> 69 us (level)
  no operation moved by 1% of the time
where the time goes in v8:
time: 69 us; the launch traced here: 67.9 us
  blocking collectives  30 us (43%)
  waiting for transfers between devices  13.3 us (19%)
  starting transfers between devices  13.2 us (19%)
  Pallas kernels  10.6 us (15%)
  between operations  0.75 us (1%)
    all_to_all x1, blocking collectives, body(): lax.all_to_all(v.reshape(32 * ROWS, 1, 128), 'inst', 0, 0, tiled=True)  16.7 us
    all_to_all x1, blocking collectives, body(): got = lax.all_to_all(parts, ALL, 0, 0, tiled=True)  13.3 us
    all_to_all x1, starting transfers between devices, body(): lax.all_to_all(x.reshape(32 * ROWS, 1, 128), 'inst', 0, 0, tiled=True)  10.9 us
    all_to_all x1, waiting for transfers between devices, body(): lax.all_to_all(x.reshape(32 * ROWS, 1, 128), 'inst', 0, 0, tiled=True)  6.99 us
    ppermute x2, waiting for transfers between devices, swap_halos(): halo = lax.ppermute(halo, 'rad', SWAP)  6.32 us
    pallas_call x1, Pallas kernels, body(): call(send_kernel, [SM, SM] + [VM] * 8 + [HM] * 3, [(f32(32 * ROWS, 128),...  2.93 us
    ppermute x2, starting transfers between devices, swap_halos(): halo = lax.ppermute(halo, 'rad', SWAP)  2.33 us
    pallas_call x1, Pallas kernels, body(): call(first_kernel, [SM, SM] + [HM] * 6, [(full, VM), (full, VM), (f32(n,...  2.11 us
  transfers between devices with their start and end apart: 5, of which 3 were waited for; matrix products, arithmetic and copies ran while one was open for 0% of the time, Pallas kernels for 5%

profile of v8, /device:TPU:0, one launch (start us, length us, event | category | flops | bytes accessed | tf_op | source)
XLA Modules:
  0.0 67.9 jit_solution(18236127190071369966)
XLA Ops:
  0.6 1.1 %shard_map.123 = (f32[2,16,128]{2,1,0:T(8,128)S(1)}, f32[40,256]{1,0:T(8,128)S(1)}) custom-call(s32[1]{0:T(128)} %bitcast.rad_ref, f32[10,16,512]{2,1,0:T(8,128)} %bitcast.33), custom_call_target="tpu_custom_call" | custom-call | bytes 3000000 | tf_op jit(solution)/shard_map/pallas_call | solution.py:514
  1.8 1.7 %collective-permute-start.1 = (f32[40,256]{1,0:T(8,128)S(1)}, f32[40,256]{1,0:T(8,128)S(1)}, u32[]{:S(2)}, u32[]{:S(2)}) collective-permute-start(f32[40,256]{1,0:T(8,128)S(1)} %get-tuple-element.26), channel_id=1, source_target_pairs={{0,1},{1,0},{2,3},{3,2},{4,5},{5,4},{6,7},{7,6},{8,9},{9,8},{10,11... | collective-permute-start | bytes 122888 | tf_op jit(solution)/shard_map/ppermute | solution.py:495
  3.4 0.0 collective-permute-start
  3.4 2.1 %shard_map.122 = (f32[10,16,512]{2,1,0:T(8,128)S(1)}, f32[10,16,512]{2,1,0:T(8,128)S(1)}, f32[10,5,512]{2,1,0:T(8,128)S(1)}, bf16[10,5,16,128]{3,2,1,0:T(8,128)(...) custom-call(s32[1]{0:T(128)} %bitcast.rad_ref, s32[1]{0:T(128)} %bitcast.1.span_ref, f32[16,512]{1,0:T(8,128)} %dis_hbm.1, ...), custom_call_target="tpu_custom_call" | custom-call | bytes 9000000 | tf_op jit(solution)/shard_map/pallas_call | solution.py:518
  5.5 0.0 collective-permute-done.edge_ref
  5.6 0.3 collective-permute-done.1.halo_ref
  5.8 2.9 %shard_map.124 = (f32[1376,128]{1,0:T(8,128)}, f32[10,16,512]{2,1,0:T(8,128)S(1)}, f32[3,16,128]{2,1,0:T(8,128)S(1)}, f32[48,256]{1,0:T(8,128)S(1)}) custom-call(s32[1]{0:T(128)} %bitcast.rad_ref, s32[1]{0:T(128)} %bitcast.1.span_ref, f32[10,16,512]{2,1,0:T(8,128)S(1)} %get-tuple-element.23.psi_ref, f32[10,16,512]{2,1,0:T(8,128)S(1)} %get-tuple-element.24.part_ref, ...), custom_call_target="tpu_custom_call" | custom-call | bytes 3000000 | tf_op jit(solution)/shard_map/pallas_call | solution.py:525
  8.8 10.9 %all-to-all-start = ((f32[1376,1,128]{2,1,0:T(1,128)}), f32[1376,1,128]{2,1,0:T(1,128)S(1)}, u32[]{:S(2)}, u32[]{:S(2)}) async-start(f32[1376,1,128]{2,1,0:T(1,128)} %bitcast.9), calls=%async_computation | async-start | bytes 1409024 | tf_op jit(solution)/shard_map/all_to_all | solution.py:531
  19.7 0.0 copy-start.4
  19.7 0.7 collective-permute-start.3
  20.4 0.0 collective-permute-start.2
  20.4 1.3 %shard_map.125 = (bf16[512,1024]{1,0:T(8,128)(2,1)S(1)}, bf16[128,1024]{1,0:T(8,128)(2,1)S(1)}, s32[8,1024]{1,0:T(8,128)S(1)}, f32[2,128]{1,0:T(2,128)S(1)}) custom-call(s32[1]{0:T(128)} %bitcast.4.me_ref, s32[1,1024]{1,0:T(1,128)} %bitcast.35, s32[1,1024]{1,0:T(1,128)} %bitcast.36, s32[1,1024]{1,0:T(1,128)} %bitcast.37, ...), custom_call_target="tpu_custom_call" | custom-call | bytes 120000000 | tf_op jit(solution)/shard_map/pallas_call | solution.py:533
  21.7 0.0 collective-permute-done.2.edge_ref
  21.7 6.0 %collective-permute-done.3.halo_ref = f32[48,256]{1,0:T(8,128)S(1)} collective-permute-done((f32[48,256]{1,0:T(8,128)S(1)}, f32[48,256]{1,0:T(8,128)S(1)}, u32[]{:S(2)}, u32[]{:S(2)}) %collective-permute-start.3) | collective-permute-done | bytes 49184 | tf_op jit(solution)/shard_map/ppermute | solution.py:495
  27.7 7.0 %all-to-all-done = f32[1376,1,128]{2,1,0:T(1,128)S(1)} async-done(((f32[1376,1,128]{2,1,0:T(1,128)}), f32[1376,1,128]{2,1,0:T(1,128)S(1)}, u32[]{:S(2)}, u32[]{:S(2)}) %all-to-all-start) | async-done | bytes 704544 | tf_op jit(solution)/shard_map/all_to_all | solution.py:531
  34.7 0.0 copy-done.4
  34.7 0.0 copy-start.1
  34.7 0.5 shard_map.126
  35.2 0.0 copy-start
  35.2 0.0 copy-start.2
  35.2 0.0 copy-start.3
  35.2 16.7 %all_to_all.21 = f32[1376,1,128]{2,1,0:T(1,128)S(1)} all-to-all(f32[1376,1,128]{2,1,0:T(1,128)S(1)} %bitcast.29), channel_id=1, replica_groups=mesh['inst'=32,'span'=2,'rad'=2] {'inst'}, dimensions={0} | all-to-all | bytes 1409024 | tf_op jit(solution)/shard_map/all_to_all | solution.py:540
  51.9 0.0 copy-done.1
  51.9 0.0 copy-done
  51.9 0.0 copy-done.2
  51.9 0.0 copy-done.3
  51.9 2.0 %shard_map.127 = (f32[10,16,512]{2,1,0:T(8,128)}, f32[128,128]{1,0:T(8,128)S(1)}) custom-call(s32[1]{0:T(128)} %bitcast.rad_ref, f32[10,16,512]{2,1,0:T(8,128)S(1)} %get-tuple-element.31.w_ref, f32[1376,128]{1,0:T(8,128)S(1)} %bitcast.28, f32[3,16,128]{2,1,0:T(8,128)S(1)} %get-tuple-element.39.w_edge_ref, f32[48,256]{1,0:T(8,128)S(1)} %get-tuple-element.40.w_halo_ref, ...), custom_call_target="tpu_custom_call" | custom-call | bytes 3000000 | tf_op jit(solution)/shard_map/pallas_call | solution.py:541
  54.0 13.3 %all_to_all.22 = f32[128,1,128]{2,1,0:T(1,128)S(1)} all-to-all(f32[128,1,128]{2,1,0:T(1,128)S(1)} %bitcast.31), channel_id=1, replica_groups=mesh['inst'=32,'span'=2,'rad'=2] {'inst','span','rad'}, dimensions={0} | all-to-all | bytes 131072 | tf_op jit(solution)/shard_map/all_to_all | solution.py:546
  67.2 0.7 shard_map.128
Async XLA Ops:
  1.8 4.1 %collective-permute-start.1 = (f32[40,256]{1,0:T(8,128)S(1)}, f32[40,256]{1,0:T(8,128)S(1)}, u32[]{:S(2)}, u32[]{:S(2)}) collective-permute-start(f32[40,256]{1,0:T(8,128)S(1)} %get-tuple-element.26), channel_id=1, source_target_pairs={{0,1},{1,0},{2,3},{3,2},{4,5},{5,4},{6,7},{7,6},{8,9},{9,8},{10,11... | collective-permute-start | bytes 122888 | tf_op jit(solution)/shard_map/ppermute | solution.py:495
  3.4 2.1 %collective-permute-start = (f32[2,16,128]{2,1,0:T(8,128)S(1)}, f32[2,16,128]{2,1,0:T(8,128)S(1)}, u32[]{:S(2)}, u32[]{:S(2)}) collective-permute-start(f32[2,16,128]{2,1,0:T(8,128)S(1)} %get-tuple-element.25), channel_id=1, source_target_pairs={{0,2},{2,0},{1,3},{3,1},{4,6},{6,4},{5,7},{7,5},{8,10},{10,8},{9,1... | collective-permute-start | bytes 49160 | tf_op jit(solution)/shard_map/ppermute | solution.py:496
  8.8 25.9 %all-to-all-start = ((f32[1376,1,128]{2,1,0:T(1,128)}), f32[1376,1,128]{2,1,0:T(1,128)S(1)}, u32[]{:S(2)}, u32[]{:S(2)}) async-start(f32[1376,1,128]{2,1,0:T(1,128)} %bitcast.9), calls=%async_computation | async-start | bytes 1409024 | tf_op jit(solution)/shard_map/all_to_all | solution.py:531
  19.7 15.0 %copy-start.4 = (bf16[64,320]{1,0:T(8,128)(2,1)S(1)}, bf16[64,320]{1,0:T(8,128)(2,1)}, u32[]{:S(2)}) copy-start(bf16[64,320]{1,0:T(8,128)(2,1)} %constant.14.clone.table_ref) | copy-start | bytes 122884
  19.7 8.0 %collective-permute-start.3 = (f32[48,256]{1,0:T(8,128)S(1)}, f32[48,256]{1,0:T(8,128)S(1)}, u32[]{:S(2)}, u32[]{:S(2)}) collective-permute-start(f32[48,256]{1,0:T(8,128)S(1)} %get-tuple-element.35), channel_id=1, source_target_pairs={{0,1},{1,0},{2,3},{3,2},{4,5},{5,4},{6,7},{7,6},{8,9},{9,8},{10,11... | collective-permute-start | bytes 147464 | tf_op jit(solution)/shard_map/ppermute | solution.py:495
  20.4 1.3 %collective-permute-start.2 = (f32[3,16,128]{2,1,0:T(8,128)S(1)}, f32[3,16,128]{2,1,0:T(8,128)S(1)}, u32[]{:S(2)}, u32[]{:S(2)}) collective-permute-start(f32[3,16,128]{2,1,0:T(8,128)S(1)} %get-tuple-element.34), channel_id=1, source_target_pairs={{0,2},{2,0},{1,3},{3,1},{4,6},{6,4},{5,7},{7,5},{8,10},{10,8},{9,1... | collective-permute-start | bytes 73736 | tf_op jit(solution)/shard_map/ppermute | solution.py:496
  34.7 17.2 %copy-start.1 = (bf16[2,5,5,16,512]{4,3,2,1,0:T(8,128)(2,1)S(1)}, bf16[2,5,5,16,512]{4,3,2,1,0:T(8,128)(2,1)}, u32[]{:S(2)}) copy-start(bf16[2,5,5,16,512]{4,3,2,1,0:T(8,128)(2,1)} %jc_ref.1) | copy-start | bytes 2457604
  35.2 16.8 %copy-start = (bf16[2,5,5,16,512]{4,3,2,1,0:T(8,128)(2,1)S(1)}, bf16[2,5,5,16,512]{4,3,2,1,0:T(8,128)(2,1)}, u32[]{:S(2)}) copy-start(bf16[2,5,5,16,512]{4,3,2,1,0:T(8,128)(2,1)} %jr_ref.1) | copy-start | bytes 2457604
  35.2 16.8 %copy-start.2 = (f32[2,5,16,512]{3,2,1,0:T(8,128)S(1)}, f32[2,5,16,512]{3,2,1,0:T(8,128)}, u32[]{:S(2)}) copy-start(f32[2,5,16,512]{3,2,1,0:T(8,128)} %param.16) | copy-start | bytes 983044
  35.2 16.8 %copy-start.3 = (bf16[2,5,3,1024]{3,0,2,1:T(2,128)(2,1)S(1)}, bf16[2,5,3,1024]{3,0,2,1:T(2,128)(2,1)}, u32[]{:S(2)}) copy-start(bf16[2,5,3,1024]{3,0,2,1:T(2,128)(2,1)} %param.20) | copy-start | bytes 184324

commit v9 on v7

--- a/solution.py
+++ b/solution.py
@@ -95,7 +95,9 @@
 
 
 def clear_pad(pad_ref):
-    pad_ref[...] = jnp.zeros(pad_ref.shape, F32)
+    for f in range(NF):
+        for at in (32 * f, 32 * f + 24):
+            pad_ref[at:at + 8, :] = jnp.zeros((8, 128), F32)
 
 
 def halo_rows(ref, at, count):

time: 69 us -> 69 us (level)
  no operation moved by 1% of the time
where the time goes in v9:
time: 69 us; the launch traced here: 67.9 us
  blocking collectives  30 us (43%)
  waiting for transfers between devices  13.3 us (19%)
  starting transfers between devices  13.2 us (19%)
  Pallas kernels  10.6 us (15%)
  between operations  0.75 us (1%)
    all_to_all x1, blocking collectives, body(): lax.all_to_all(v.reshape(32 * ROWS, 1, 128), 'inst', 0, 0, tiled=True)  16.7 us
    all_to_all x1, blocking collectives, body(): got = lax.all_to_all(parts, ALL, 0, 0, tiled=True)  13.3 us
    all_to_all x1, starting transfers between devices, body(): lax.all_to_all(x.reshape(32 * ROWS, 1, 128), 'inst', 0, 0, tiled=True)  10.9 us
    all_to_all x1, waiting for transfers between devices, body(): lax.all_to_all(x.reshape(32 * ROWS, 1, 128), 'inst', 0, 0, tiled=True)  6.99 us
    ppermute x2, waiting for transfers between devices, swap_halos(): halo = lax.ppermute(halo, 'rad', SWAP)  6.32 us
    pallas_call x1, Pallas kernels, body(): call(send_kernel, [SM, SM] + [VM] * 8 + [HM] * 3, [(f32(32 * ROWS, 128),...  2.93 us
    ppermute x2, starting transfers between devices, swap_halos(): halo = lax.ppermute(halo, 'rad', SWAP)  2.33 us
    pallas_call x1, Pallas kernels, body(): call(first_kernel, [SM, SM] + [HM] * 6, [(full, VM), (full, VM), (f32(n,...  2.11 us
  transfers between devices with their start and end apart: 5, of which 3 were waited for; matrix products, arithmetic and copies ran while one was open for 0% of the time, Pallas kernels for 5%

profile of v9, /device:TPU:0, one launch (start us, length us, event | category | flops | bytes accessed | tf_op | source)
XLA Modules:
  0.0 67.9 jit_solution(5198677750646142)
XLA Ops:
  0.6 1.1 %shard_map.123 = (f32[2,16,128]{2,1,0:T(8,128)S(1)}, f32[40,256]{1,0:T(8,128)S(1)}) custom-call(s32[1]{0:T(128)} %bitcast.rad_ref, f32[10,16,512]{2,1,0:T(8,128)} %bitcast.33), custom_call_target="tpu_custom_call" | custom-call | bytes 3000000 | tf_op jit(solution)/shard_map/pallas_call | solution.py:513
  1.8 1.7 %collective-permute-start.1 = (f32[40,256]{1,0:T(8,128)S(1)}, f32[40,256]{1,0:T(8,128)S(1)}, u32[]{:S(2)}, u32[]{:S(2)}) collective-permute-start(f32[40,256]{1,0:T(8,128)S(1)} %get-tuple-element.26), channel_id=1, source_target_pairs={{0,1},{1,0},{2,3},{3,2},{4,5},{5,4},{6,7},{7,6},{8,9},{9,8},{10,11... | collective-permute-start | bytes 122888 | tf_op jit(solution)/shard_map/ppermute | solution.py:494
  3.4 0.0 collective-permute-start
  3.4 2.1 %shard_map.122 = (f32[10,16,512]{2,1,0:T(8,128)S(1)}, f32[10,16,512]{2,1,0:T(8,128)S(1)}, f32[10,5,512]{2,1,0:T(8,128)S(1)}, bf16[10,5,16,128]{3,2,1,0:T(8,128)(...) custom-call(s32[1]{0:T(128)} %bitcast.rad_ref, s32[1]{0:T(128)} %bitcast.1.span_ref, f32[16,512]{1,0:T(8,128)} %dis_hbm.1, ...), custom_call_target="tpu_custom_call" | custom-call | bytes 9000000 | tf_op jit(solution)/shard_map/pallas_call | solution.py:517
  5.5 0.0 collective-permute-done.edge_ref
  5.6 0.3 collective-permute-done.1.halo_ref
  5.8 2.9 %shard_map.124 = (f32[1376,128]{1,0:T(8,128)}, f32[10,16,512]{2,1,0:T(8,128)S(1)}, f32[3,16,128]{2,1,0:T(8,128)S(1)}, f32[48,256]{1,0:T(8,128)S(1)}) custom-call(s32[1]{0:T(128)} %bitcast.rad_ref, s32[1]{0:T(128)} %bitcast.1.span_ref, f32[10,16,512]{2,1,0:T(8,128)S(1)} %get-tuple-element.23.psi_ref, f32[10,16,512]{2,1,0:T(8,128)S(1)} %get-tuple-element.24.part_ref, ...), custom_call_target="tpu_custom_call" | custom-call | bytes 3000000 | tf_op jit(solution)/shard_map/pallas_call | solution.py:524
  8.8 10.9 %all-to-all-start = ((f32[1376,1,128]{2,1,0:T(1,128)}), f32[1376,1,128]{2,1,0:T(1,128)S(1)}, u32[]{:S(2)}, u32[]{:S(2)}) async-start(f32[1376,1,128]{2,1,0:T(1,128)} %bitcast.9), calls=%async_computation | async-start | bytes 1409024 | tf_op jit(solution)/shard_map/all_to_all | solution.py:530
  19.7 0.0 copy-start.4
  19.7 0.7 collective-permute-start.3
  20.4 0.0 collective-permute-start.2
  20.4 1.3 %shard_map.125 = (bf16[512,1024]{1,0:T(8,128)(2,1)S(1)}, bf16[128,1024]{1,0:T(8,128)(2,1)S(1)}, s32[8,1024]{1,0:T(8,128)S(1)}, f32[2,128]{1,0:T(2,128)S(1)}) custom-call(s32[1]{0:T(128)} %bitcast.4.me_ref, s32[1,1024]{1,0:T(1,128)} %bitcast.35, s32[1,1024]{1,0:T(1,128)} %bitcast.36, s32[1,1024]{1,0:T(1,128)} %bitcast.37, ...), custom_call_target="tpu_custom_call" | custom-call | bytes 120000000 | tf_op jit(solution)/shard_map/pallas_call | solution.py:532
  21.7 0.0 collective-permute-done.2.edge_ref
  21.7 6.0 %collective-permute-done.3.halo_ref = f32[48,256]{1,0:T(8,128)S(1)} collective-permute-done((f32[48,256]{1,0:T(8,128)S(1)}, f32[48,256]{1,0:T(8,128)S(1)}, u32[]{:S(2)}, u32[]{:S(2)}) %collective-permute-start.3) | collective-permute-done | bytes 49184 | tf_op jit(solution)/shard_map/ppermute | solution.py:494
  27.7 7.0 %all-to-all-done = f32[1376,1,128]{2,1,0:T(1,128)S(1)} async-done(((f32[1376,1,128]{2,1,0:T(1,128)}), f32[1376,1,128]{2,1,0:T(1,128)S(1)}, u32[]{:S(2)}, u32[]{:S(2)}) %all-to-all-start) | async-done | bytes 704544 | tf_op jit(solution)/shard_map/all_to_all | solution.py:530
  34.7 0.0 copy-done.4
  34.7 0.0 copy-start.1
  34.7 0.5 shard_map.126
  35.2 0.0 copy-start
  35.2 0.0 copy-start.2
  35.2 0.0 copy-start.3
  35.2 16.7 %all_to_all.21 = f32[1376,1,128]{2,1,0:T(1,128)S(1)} all-to-all(f32[1376,1,128]{2,1,0:T(1,128)S(1)} %bitcast.29), channel_id=1, replica_groups=mesh['inst'=32,'span'=2,'rad'=2] {'inst'}, dimensions={0} | all-to-all | bytes 1409024 | tf_op jit(solution)/shard_map/all_to_all | solution.py:539
  51.9 0.0 copy-done.1
  51.9 0.0 copy-done
  51.9 0.0 copy-done.2
  51.9 0.0 copy-done.3
  51.9 2.0 %shard_map.127 = (f32[10,16,512]{2,1,0:T(8,128)}, f32[128,128]{1,0:T(8,128)S(1)}) custom-call(s32[1]{0:T(128)} %bitcast.rad_ref, f32[10,16,512]{2,1,0:T(8,128)S(1)} %get-tuple-element.31.w_ref, f32[1376,128]{1,0:T(8,128)S(1)} %bitcast.28, f32[3,16,128]{2,1,0:T(8,128)S(1)} %get-tuple-element.39.w_edge_ref, f32[48,256]{1,0:T(8,128)S(1)} %get-tuple-element.40.w_halo_ref, ...), custom_call_target="tpu_custom_call" | custom-call | bytes 3000000 | tf_op jit(solution)/shard_map/pallas_call | solution.py:540
  54.0 13.3 %all_to_all.22 = f32[128,1,128]{2,1,0:T(1,128)S(1)} all-to-all(f32[128,1,128]{2,1,0:T(1,128)S(1)} %bitcast.31), channel_id=1, replica_groups=mesh['inst'=32,'span'=2,'rad'=2] {'inst','span','rad'}, dimensions={0} | all-to-all | bytes 131072 | tf_op jit(solution)/shard_map/all_to_all | solution.py:545
  67.2 0.7 shard_map.128
Async XLA Ops:
  1.8 4.1 %collective-permute-start.1 = (f32[40,256]{1,0:T(8,128)S(1)}, f32[40,256]{1,0:T(8,128)S(1)}, u32[]{:S(2)}, u32[]{:S(2)}) collective-permute-start(f32[40,256]{1,0:T(8,128)S(1)} %get-tuple-element.26), channel_id=1, source_target_pairs={{0,1},{1,0},{2,3},{3,2},{4,5},{5,4},{6,7},{7,6},{8,9},{9,8},{10,11... | collective-permute-start | bytes 122888 | tf_op jit(solution)/shard_map/ppermute | solution.py:494
  3.4 2.1 %collective-permute-start = (f32[2,16,128]{2,1,0:T(8,128)S(1)}, f32[2,16,128]{2,1,0:T(8,128)S(1)}, u32[]{:S(2)}, u32[]{:S(2)}) collective-permute-start(f32[2,16,128]{2,1,0:T(8,128)S(1)} %get-tuple-element.25), channel_id=1, source_target_pairs={{0,2},{2,0},{1,3},{3,1},{4,6},{6,4},{5,7},{7,5},{8,10},{10,8},{9,1... | collective-permute-start | bytes 49160 | tf_op jit(solution)/shard_map/ppermute | solution.py:495
  8.8 25.9 %all-to-all-start = ((f32[1376,1,128]{2,1,0:T(1,128)}), f32[1376,1,128]{2,1,0:T(1,128)S(1)}, u32[]{:S(2)}, u32[]{:S(2)}) async-start(f32[1376,1,128]{2,1,0:T(1,128)} %bitcast.9), calls=%async_computation | async-start | bytes 1409024 | tf_op jit(solution)/shard_map/all_to_all | solution.py:530
  19.7 15.0 %copy-start.4 = (bf16[64,320]{1,0:T(8,128)(2,1)S(1)}, bf16[64,320]{1,0:T(8,128)(2,1)}, u32[]{:S(2)}) copy-start(bf16[64,320]{1,0:T(8,128)(2,1)} %constant.14.clone.table_ref) | copy-start | bytes 122884
  19.7 8.0 %collective-permute-start.3 = (f32[48,256]{1,0:T(8,128)S(1)}, f32[48,256]{1,0:T(8,128)S(1)}, u32[]{:S(2)}, u32[]{:S(2)}) collective-permute-start(f32[48,256]{1,0:T(8,128)S(1)} %get-tuple-element.35), channel_id=1, source_target_pairs={{0,1},{1,0},{2,3},{3,2},{4,5},{5,4},{6,7},{7,6},{8,9},{9,8},{10,11... | collective-permute-start | bytes 147464 | tf_op jit(solution)/shard_map/ppermute | solution.py:494
  20.4 1.3 %collective-permute-start.2 = (f32[3,16,128]{2,1,0:T(8,128)S(1)}, f32[3,16,128]{2,1,0:T(8,128)S(1)}, u32[]{:S(2)}, u32[]{:S(2)}) collective-permute-start(f32[3,16,128]{2,1,0:T(8,128)S(1)} %get-tuple-element.34), channel_id=1, source_target_pairs={{0,2},{2,0},{1,3},{3,1},{4,6},{6,4},{5,7},{7,5},{8,10},{10,8},{9,1... | collective-permute-start | bytes 73736 | tf_op jit(solution)/shard_map/ppermute | solution.py:495
  34.7 17.2 %copy-start.1 = (bf16[2,5,5,16,512]{4,3,2,1,0:T(8,128)(2,1)S(1)}, bf16[2,5,5,16,512]{4,3,2,1,0:T(8,128)(2,1)}, u32[]{:S(2)}) copy-start(bf16[2,5,5,16,512]{4,3,2,1,0:T(8,128)(2,1)} %jc_ref.1) | copy-start | bytes 2457604
  35.2 16.8 %copy-start = (bf16[2,5,5,16,512]{4,3,2,1,0:T(8,128)(2,1)S(1)}, bf16[2,5,5,16,512]{4,3,2,1,0:T(8,128)(2,1)}, u32[]{:S(2)}) copy-start(bf16[2,5,5,16,512]{4,3,2,1,0:T(8,128)(2,1)} %jr_ref.1) | copy-start | bytes 2457604
  35.2 16.8 %copy-start.2 = (f32[2,5,16,512]{3,2,1,0:T(8,128)S(1)}, f32[2,5,16,512]{3,2,1,0:T(8,128)}, u32[]{:S(2)}) copy-start(f32[2,5,16,512]{3,2,1,0:T(8,128)} %param.16) | copy-start | bytes 983044
  35.2 16.8 %copy-start.3 = (bf16[2,5,3,1024]{3,0,2,1:T(2,128)(2,1)S(1)}, bf16[2,5,3,1024]{3,0,2,1:T(2,128)(2,1)}, u32[]{:S(2)}) copy-start(bf16[2,5,3,1024]{3,0,2,1:T(2,128)(2,1)} %param.20) | copy-start | bytes 184324
